TPU v7x, 32 devices: a whole 2x2x4 slice. The times are simulated.
32 devices in a mesh: dp: 8 (over y, x, core), head: 4 (over z).
Axes of the slice: x: 2, y: 2, z: 4, core: 2. Of those that a mesh axis runs over, the one named last changes fastest.
Arguments:
- interface: float32 [8, 1024, 512], P('dp', 'head'), may hold values from -6 to 6
- latents: float32 [8, 128, 1024], P('dp'), may hold values from -6 to 6
- segment_ids: int32 [8, 1024], P('dp'), may hold values from 0 to 3, never falling along the last dimension, each value on 1 to 512 neighbouring positions
- read_gain_lat: float32 [1024], replicated, may hold values from 0.1 to 1.9
- read_gain_int: float32 [512], P('head'), may hold values from 0.1 to 1.9
- read_query: float32 [1024, 1024], P(None, 'head'), may hold values from -0.1875 to 0.1875
- read_keyval: float32 [512, 2, 1024], P(None, None, 'head'), may hold values from -0.25 to 0.25
- read_out: float32 [1024, 1024], P('head'), may hold values from -0.75 to 0.75
- read_gain_mlp: float32 [1024], replicated, may hold values from 0.1 to 1.9
- read_up: float32 [1024, 4096], P(None, 'head'), may hold values from -0.1875 to 0.1875
- read_down: float32 [4096, 1024], P('head'), may hold values from -0.09375 to 0.09375
- layer_gain_att: float32 [1, 1024], replicated, may hold values from 0.1 to 1.9
- layer_qkv: float32 [1, 1024, 3, 1024], P(None, None, None, 'head'), may hold values from -0.1875 to 0.1875
- layer_out: float32 [1, 1024, 1024], P(None, 'head'), may hold values from -0.375 to 0.375
- layer_gain_mlp: float32 [1, 1024], replicated, may hold values from 0.1 to 1.9
- layer_up: float32 [1, 1024, 4096], P(None, None, 'head'), may hold values from -0.1875 to 0.1875
- layer_down: float32 [1, 4096, 1024], P(None, 'head'), may hold values from -0.09375 to 0.09375
- write_gain_int: float32 [512], P('head'), may hold values from 0.1 to 1.9
- write_query: float32 [512, 512], P('head'), may hold values from -0.25 to 0.25
- write_gain_lat: float32 [1024], replicated, may hold values from 0.1 to 1.9
- write_keyval: float32 [1024, 2, 512], P(None, None, 'head'), may hold values from -0.1875 to 0.1875
- write_out: float32 [512, 512], P('head'), may hold values from -0.5 to 0.5
- write_gain_mlp: float32 [512], P('head'), may hold values from 0.1 to 1.9
- write_up: float32 [512, 2048], P('head'), may hold values from -0.25 to 0.25
- write_down: float32 [2048, 512], P('head'), may hold values from -0.125 to 0.125
- interface_cot: float32 [8, 1024, 512], P('dp', 'head'), may hold values from -6 to 6
- latents_cot: float32 [8, 128, 1024], P('dp'), may hold values from -6 to 6
Outputs:
- interface_new: float32 [8, 1024, 512], P('dp', 'head')
- latents_new: float32 [8, 128, 1024], P('dp')
- interface_grad: float32 [8, 1024, 512], P('dp', 'head')
- latents_grad: float32 [8, 128, 1024], P('dp')
- grad_read_gain_lat: float32 [1024], replicated
- grad_read_gain_int: float32 [512], P('head')
- grad_read_query: float32 [1024, 1024], P(None, 'head')
- grad_read_keyval: float32 [512, 2, 1024], P(None, None, 'head')
- grad_read_out: float32 [1024, 1024], P('head')
- grad_read_gain_mlp: float32 [1024], replicated
- grad_read_up: float32 [1024, 4096], P(None, 'head')
- grad_read_down: float32 [4096, 1024], P('head')
- grad_layer_gain_att: float32 [1, 1024], replicated
- grad_layer_qkv: float32 [1, 1024, 3, 1024], P(None, None, None, 'head')
- grad_layer_out: float32 [1, 1024, 1024], P(None, 'head')
- grad_layer_gain_mlp: float32 [1, 1024], replicated
- grad_layer_up: float32 [1, 1024, 4096], P(None, None, 'head')
- grad_layer_down: float32 [1, 4096, 1024], P(None, 'head')
- grad_write_gain_int: float32 [512], P('head')
- grad_write_query: float32 [512, 512], P('head')
- grad_write_gain_lat: float32 [1024], replicated
- grad_write_keyval: float32 [1024, 2, 512], P(None, None, 'head')
- grad_write_out: float32 [512, 512], P('head')
- grad_write_gain_mlp: float32 [512], P('head')
- grad_write_up: float32 [512, 2048], P('head')
- grad_write_down: float32 [2048, 512], P('head')
Inputs may be any that keep to these rules, and one draw needn't show every extreme that they name: `segment_ids`: along each sequence the crop numbers never fall; every crop holds 1 to 512 patches, and some crop of each sequence holds exactly 512.
All inputs are finite; a program needn't handle non-finite values.
Results may differ from a plain program's by a relative error of at most 0.0003.
Values sent between devices are 32-bit elements; how exact they have to be, the bound alone decides.
No kernel may reach another device: no remote copies, remote signals or barrier semaphores. Data moves between devices by JAX's collectives and lax.ppermute only.
A program may use at most 256 MiB of HBM per device.

v0:
```python
import jax
import jax.numpy as jnp
from jax import lax
from jax.sharding import PartitionSpec as P

HEADS = 16
NL = 128
CROPS = 4
LAYERS = 1


PRECISE = lax.Precision.HIGHEST
EPSILON = 1e-05


def layer_norm(values, scaling):
    average = jnp.mean(values, axis=-1, keepdims=True)
    centred = values - average
    spread = jnp.mean(centred * centred, axis=-1, keepdims=True)
    return centred * lax.rsqrt(spread + EPSILON) * scaling


def product(former, latter):
    return jnp.matmul(former, latter, precision=PRECISE)


def feed_forward(normed, upward, downward):
    return product(jax.nn.gelu(product(normed, upward), approximate=False), downward)


def project_keyval(normed, weight_keyval):
    return jnp.einsum("sni,icd->sncd", normed, weight_keyval, precision=PRECISE)


def split_heads(values, head_count):
    return values.reshape(values.shape[:-1] + (head_count, values.shape[-1] // head_count))


def attend(queries, key_rows, value_rows, allowed, head_count):
    query_heads = split_heads(queries, head_count)
    key_heads = split_heads(key_rows, head_count)
    value_heads = split_heads(value_rows, head_count)
    factor = query_heads.shape[-1] ** (-0.5)
    scores = jnp.einsum("sqhd,skhd->shqk", query_heads, key_heads, precision=PRECISE) * factor
    scores = jnp.where(allowed[:, None], scores, -1e30)
    weights = jax.nn.softmax(scores, axis=-1)
    blended = jnp.einsum("shqk,skhd->sqhd", weights, value_heads, precision=PRECISE)
    return blended.reshape(blended.shape[:-2] + (-1,))


def build_masks(segment_ids):
    latent_crop = jnp.arange(NL, dtype=jnp.int32) // (NL // CROPS)
    read_mask = latent_crop[None, :, None] == segment_ids[:, None, :]
    self_mask = jnp.broadcast_to(
        latent_crop[:, None] == latent_crop[None, :], (segment_ids.shape[0], NL, NL)
    )
    write_mask = segment_ids[:, :, None] == latent_crop[None, None, :]
    return (read_mask, self_mask, write_mask)


def local(
    interface,
    latents,
    segment_ids,
    read_gain_lat,
    read_gain_int,
    read_query,
    read_keyval,
    read_out,
    read_gain_mlp,
    read_up,
    read_down,
    layer_gain_att,
    layer_qkv,
    layer_out,
    layer_gain_mlp,
    layer_up,
    layer_down,
    write_gain_int,
    write_query,
    write_gain_lat,
    write_keyval,
    write_out,
    write_gain_mlp,
    write_up,
    write_down,
    interface_cot,
    latents_cot,
):
    heads_here = HEADS // lax.axis_size("head")
    read_mask, self_mask, write_mask = build_masks(segment_ids)

    def head_sum(partial_sum):
        return lax.psum(partial_sum, "head")

    def read_branch(lat_normed, keyval, weight_query, weight_out):
        attended = attend(
            product(lat_normed, weight_query),
            keyval[:, :, 0],
            keyval[:, :, 1],
            read_mask,
            heads_here,
        )
        return product(attended, weight_out)

    def self_branch(normed, weight_qkv, weight_out):
        packed = jnp.einsum("snd,dce->snce", normed, weight_qkv, precision=PRECISE)
        attended = attend(packed[:, :, 0], packed[:, :, 1], packed[:, :, 2], self_mask, heads_here)
        return product(attended, weight_out)

    def write_core(queries, keyval):
        return attend(queries, keyval[:, :, 0], keyval[:, :, 1], write_mask, heads_here)

    def row_mlp(values, scaling, upward, downward):
        return feed_forward(layer_norm(values, scaling), upward, downward)

    def query_path(values, scaling, weight_query):
        return product(layer_norm(values, scaling), weight_query)

    full_gain_read, full_gain_write, full_gain_mlp, full_query, full_wout, full_up, full_down = (
        lax.all_gather(read_gain_int, "head", axis=0, tiled=True),
        lax.all_gather(write_gain_int, "head", axis=0, tiled=True),
        lax.all_gather(write_gain_mlp, "head", axis=0, tiled=True),
        lax.all_gather(write_query, "head", axis=0, tiled=True),
        lax.all_gather(write_out, "head", axis=0, tiled=True),
        lax.all_gather(write_up, "head", axis=0, tiled=True),
        lax.all_gather(write_down, "head", axis=0, tiled=True),
    )
    read_normed = layer_norm(latents, read_gain_lat)
    int_normed = layer_norm(interface, full_gain_read)
    int_gathered = lax.all_gather(int_normed, "head", axis=1, tiled=True)
    keyval = project_keyval(int_gathered, read_keyval)
    after_read = latents + head_sum(read_branch(read_normed, keyval, read_query, read_out))
    mlp_normed = layer_norm(after_read, read_gain_mlp)
    carried = after_read + head_sum(feed_forward(mlp_normed, read_up, read_down))
    layer_no = 0
    att_normed = layer_norm(carried, layer_gain_att[layer_no])
    middle = carried + head_sum(self_branch(att_normed, layer_qkv[layer_no], layer_out[layer_no]))
    ffn_normed = layer_norm(middle, layer_gain_mlp[layer_no])
    layer_inputs = [(carried, middle)]
    carried = middle + head_sum(feed_forward(ffn_normed, layer_up[layer_no], layer_down[layer_no]))
    write_normed = layer_norm(carried, write_gain_lat)
    write_keys = project_keyval(write_normed, write_keyval)
    query_local = query_path(interface, full_gain_write, full_query)
    query_heads = lax.all_to_all(query_local, "head", split_axis=2, concat_axis=1, tiled=True)
    write_attended = write_core(query_heads, write_keys)
    attended_rows = lax.all_to_all(write_attended, "head", split_axis=1, concat_axis=2, tiled=True)
    after_write = interface + product(attended_rows, full_wout)
    interface_new = after_write + row_mlp(after_write, full_gain_mlp, full_up, full_down)
    _, pullback = jax.vjp(row_mlp, after_write, full_gain_mlp, full_up, full_down)
    grad_rows, grad_wgain_mlp, grad_wup, grad_wdown = pullback(interface_cot)
    grad_after_write = interface_cot + grad_rows
    grad_wout_full = jnp.einsum("snh,sni->hi", attended_rows, grad_after_write, precision=PRECISE)
    grad_attended_rows = product(grad_after_write, full_wout.T)
    grad_attended = lax.all_to_all(
        grad_attended_rows, "head", split_axis=2, concat_axis=1, tiled=True
    )
    _, pullback = jax.vjp(write_core, query_heads, write_keys)
    grad_query_heads, grad_write_keys = pullback(grad_attended)
    grad_query_local = lax.all_to_all(
        grad_query_heads, "head", split_axis=1, concat_axis=2, tiled=True
    )
    _, pullback = jax.vjp(query_path, interface, full_gain_write, full_query)
    grad_from_query, grad_wgain_int, grad_wquery = pullback(grad_query_local)
    _, pullback = jax.vjp(project_keyval, write_normed, write_keyval)
    grad_write_normed, grad_write_keyval = pullback(grad_write_keys)
    _, pullback = jax.vjp(layer_norm, carried, write_gain_lat)
    grad_carried, grad_write_gain_lat = pullback(head_sum(grad_write_normed))
    grad_carried = latents_cot + grad_carried
    layer_grads = []
    for layer_no in reversed(range(LAYERS)):
        before, middle = layer_inputs[layer_no]
        ffn_normed, norm_pull = jax.vjp(layer_norm, middle, layer_gain_mlp[layer_no])
        _, pullback = jax.vjp(feed_forward, ffn_normed, layer_up[layer_no], layer_down[layer_no])
        grad_normed, grad_lup, grad_ldown = pullback(grad_carried)
        grad_middle, grad_lgain_mlp = norm_pull(head_sum(grad_normed))
        grad_middle = grad_carried + grad_middle
        att_normed, norm_pull = jax.vjp(layer_norm, before, layer_gain_att[layer_no])
        _, pullback = jax.vjp(self_branch, att_normed, layer_qkv[layer_no], layer_out[layer_no])
        grad_normed, grad_lqkv, grad_lout = pullback(grad_middle)
        grad_before, grad_lgain_att = norm_pull(head_sum(grad_normed))
        grad_carried = grad_middle + grad_before
        layer_grads.insert(
            0, (grad_lgain_att, grad_lqkv, grad_lout, grad_lgain_mlp, grad_lup, grad_ldown)
        )
    _, norm_pull = jax.vjp(layer_norm, after_read, read_gain_mlp)
    _, pullback = jax.vjp(feed_forward, mlp_normed, read_up, read_down)
    grad_normed, grad_read_up, grad_read_down = pullback(grad_carried)
    grad_after_read, grad_read_gain_mlp = norm_pull(head_sum(grad_normed))
    grad_after_read = grad_carried + grad_after_read

    def read_whole(lat_normed, gathered, weight_query, weight_keyval, weight_out):
        return read_branch(
            lat_normed, project_keyval(gathered, weight_keyval), weight_query, weight_out
        )

    _, pullback = jax.vjp(read_whole, read_normed, int_gathered, read_query, read_keyval, read_out)
    grad_read_normed, grad_gathered, grad_read_query, grad_read_keyval, grad_read_out = pullback(
        grad_after_read
    )
    grad_int_normed = lax.psum_scatter(grad_gathered, "head", scatter_dimension=1, tiled=True)
    _, pullback = jax.vjp(layer_norm, latents, read_gain_lat)
    grad_latents_in, grad_read_gain_lat = pullback(head_sum(grad_read_normed))
    latents_grad = grad_after_read + grad_latents_in
    _, pullback = jax.vjp(layer_norm, interface, full_gain_read)
    grad_from_read, grad_rgain_int = pullback(grad_int_normed)
    interface_grad = grad_after_write + grad_from_query + grad_from_read
    (
        shard_rgain_int,
        shard_wgain_int,
        shard_wgain_mlp,
        shard_wquery,
        shard_wout,
        shard_wup,
        shard_wdown,
    ) = (
        lax.psum_scatter(grad_rgain_int, "head", scatter_dimension=0, tiled=True),
        lax.psum_scatter(grad_wgain_int, "head", scatter_dimension=0, tiled=True),
        lax.psum_scatter(grad_wgain_mlp, "head", scatter_dimension=0, tiled=True),
        lax.psum_scatter(grad_wquery, "head", scatter_dimension=0, tiled=True),
        lax.psum_scatter(grad_wout_full, "head", scatter_dimension=0, tiled=True),
        lax.psum_scatter(grad_wup, "head", scatter_dimension=0, tiled=True),
        lax.psum_scatter(grad_wdown, "head", scatter_dimension=0, tiled=True),
    )
    stacked_gain_att = jnp.stack([layer_entry[0] for layer_entry in layer_grads])
    stacked_qkv = jnp.stack([layer_entry[1] for layer_entry in layer_grads])
    stacked_out = jnp.stack([layer_entry[2] for layer_entry in layer_grads])
    stacked_gain_mlp = jnp.stack([layer_entry[3] for layer_entry in layer_grads])
    stacked_up = jnp.stack([layer_entry[4] for layer_entry in layer_grads])
    stacked_down = jnp.stack([layer_entry[5] for layer_entry in layer_grads])
    summed = lax.psum(
        (
            grad_read_gain_lat,
            shard_rgain_int,
            grad_read_query,
            grad_read_keyval,
            grad_read_out,
            grad_read_gain_mlp,
            grad_read_up,
            grad_read_down,
            stacked_gain_att,
            stacked_qkv,
            stacked_out,
            stacked_gain_mlp,
            stacked_up,
            stacked_down,
            shard_wgain_int,
            shard_wquery,
            grad_write_gain_lat,
            grad_write_keyval,
            shard_wout,
            shard_wgain_mlp,
            shard_wup,
            shard_wdown,
        ),
        "dp",
    )
    return (interface_new, carried, interface_grad, latents_grad) + tuple(summed)


def solution(mesh):
    in_specs = (
        P("dp", "head", None),
        P("dp", None, None),
        P("dp", None),
        P(),
        P("head"),
        P(None, "head"),
        P(None, None, "head"),
        P("head", None),
        P(),
        P(None, "head"),
        P("head", None),
        P(),
        P(None, None, None, "head"),
        P(None, "head", None),
        P(),
        P(None, None, "head"),
        P(None, "head", None),
        P("head"),
        P("head", None),
        P(),
        P(None, None, "head"),
        P("head", None),
        P("head"),
        P("head", None),
        P("head", None),
        P("dp", "head", None),
        P("dp", None, None),
    )
    out_specs = (
        P("dp", "head", None),
        P("dp", None, None),
        P("dp", "head", None),
        P("dp", None, None),
        P(),
        P("head"),
        P(None, "head"),
        P(None, None, "head"),
        P("head", None),
        P(),
        P(None, "head"),
        P("head", None),
        P(),
        P(None, None, None, "head"),
        P(None, "head", None),
        P(),
        P(None, None, "head"),
        P(None, "head", None),
        P("head"),
        P("head", None),
        P(),
        P(None, None, "head"),
        P("head", None),
        P("head"),
        P("head", None),
        P("head", None),
    )
    return jax.shard_map(local, mesh=mesh, in_specs=in_specs, out_specs=out_specs, check_vma=False)
```

profile of v0, /device:TPU:13, one launch (start us, length us, event | category | flops | bytes accessed | tf_op | source)
XLA Modules:
  0.0 1469.8 jit_solution(574410009377273047)
XLA Ops:
  10.4 6.3 all-gather
  20.4 2.5 copy.151
  26.9 39.6 %all-gather.9.cloned.1.call-done = f32[1,1024,512]{2,1,0:T(8,128)} async-done(((f32[1,256,512]{2,1,0:T(8,128)}), f32[1,1024,512]{2,1,0:T(8,128)}) %all-gather.9.cloned.1.call-update) | async-done | bytes 2097168 | tf_op jit(solution)/shard_map/all_gather | solution.py:131
  66.5 5.4 fusion.27
  75.0 2.8 fusion.52
  79.7 37.5 %all-reduce.24.cloned.1.call-done = f32[1,128,1024]{2,1,0:T(8,128)} async-done(((f32[1,128,1024]{2,1,0:T(8,128)}), f32[1,128,1024]{2,1,0:T(8,128)}) %all-reduce.24.cloned.1.call-update) | async-done | bytes 524304 | tf_op jit(solution)/shard_map/psum | solution.py:94
  119.3 4.8 fusion.101
  124.9 4.3 convolution_bitcast_fusion.13
  130.0 37.7 %all-reduce.26.cloned.1.call-done = f32[1,128,1024]{2,1,0:T(8,128)} async-done(((f32[1,128,1024]{2,1,0:T(8,128)}), f32[1,128,1024]{2,1,0:T(8,128)}) %all-reduce.26.cloned.1.call-update) | async-done | bytes 524304 | tf_op jit(solution)/shard_map/psum | solution.py:94
  182.9 37.4 %all-reduce.28.cloned.1.call-done = f32[1,128,1024]{2,1,0:T(8,128)} async-done(((f32[1,128,1024]{2,1,0:T(8,128)}), f32[1,128,1024]{2,1,0:T(8,128)}) %all-reduce.28.cloned.1.call-update) | async-done | bytes 524304 | tf_op jit(solution)/shard_map/psum | solution.py:94
  221.9 4.8 fusion.6
  227.5 4.3 fusion.39
  234.1 7.1 all-gather.1
  241.2 9.5 all-gather.11.cloned.1.call-done
  250.7 3.3 convolution_bitcast_fusion.9
  255.9 4.7 all-to-all-start
  263.0 15.3 %all-to-all-done = f32[1,256,512]{1,0,2:T(1,128)} async-done(((f32[1,256,512]{1,0,2:T(1,128)}), f32[1,256,512]{1,0,2:T(1,128)}, u32[]{:S(2)}, u32[]{:S(2)}) %all-to-all-start) | async-done | bytes 524320 | tf_op jit(solution)/shard_map/all_to_all | solution.py:145
  282.6 15.6 %all-reduce.30.cloned.1.call-done = f32[1,128,1024]{2,1,0:T(8,128)} async-done(((f32[1,128,1024]{2,1,0:T(8,128)}), f32[1,128,1024]{2,1,0:T(8,128)}) %all-reduce.30.cloned.1.call-update) | async-done | bytes 524304 | tf_op jit(solution)/shard_map/psum | solution.py:94
  308.7 5.0 all-to-all-start.1
  313.6 26.3 %all-gather.2 = f32[4,1,128]{2,1,0:T(1,128)} all-gather(f32[1,1,128]{2,1,0:T(1,128)} %bitcast.466), channel_id=1, replica_groups=mesh['dp'=8,'head'=4] {'head'}, dimensions={0}, use_global_device_ids=true | all-gather | bytes 2560 | tf_op jit(solution)/shard_map/all_gather | solution.py:123
  341.9 2.7 fusion.256
  346.8 72.7 %all-gather.15.cloned.1.call-done = f32[512,2048]{1,0:T(8,128)} async-done(((f32[128,2048]{1,0:T(8,128)}), f32[512,2048]{1,0:T(8,128)}) %all-gather.15.cloned.1.call-update) | async-done | bytes 4194320 | tf_op jit(solution)/shard_map/all_gather | solution.py:126
  419.5 11.1 fusion.12
  430.6 69.8 %all-gather.17.cloned.1.call-done = f32[2048,512]{1,0:T(8,128)} async-done(((f32[512,512]{1,0:T(8,128)}), f32[2048,512]{1,0:T(8,128)}) %all-gather.17.cloned.1.call-update) | async-done | bytes 4194320 | tf_op jit(solution)/shard_map/all_gather | solution.py:127
  500.4 7.9 multiply_add_fusion
  508.4 4.3 fusion.60
  517.8 6.8 all-to-all-start.2
  526.3 9.2 all-to-all-done.2
  539.8 4.9 fusion.53
  546.3 4.4 multiply_reduce_fusion.1
  552.9 2.8 fusion.258
  556.7 2.8 convolution_bitcast_fusion.5
  559.7 39.6 %all-reduce.32.cloned.1.call-done = f32[1,128,1024]{2,1,0:T(8,128)} async-done(((f32[1,128,1024]{2,1,0:T(8,128)}), f32[1,128,1024]{2,1,0:T(8,128)}) %all-reduce.32.cloned.1.call-update) | async-done | bytes 524304 | tf_op jit(solution)/shard_map/psum | solution.py:94
  603.2 7.6 multiply_add_fusion.2
  611.6 5.3 fusion.36
  617.8 37.6 %all-reduce.34.cloned.1.call-done = f32[1,128,1024]{2,1,0:T(8,128)} async-done(((f32[1,128,1024]{2,1,0:T(8,128)}), f32[1,128,1024]{2,1,0:T(8,128)}) %all-reduce.34.cloned.1.call-update) | async-done | bytes 524304 | tf_op jit(solution)/shard_map/psum | solution.py:94
  669.0 5.1 fusion.33
  674.4 38.1 %all-reduce.36.cloned.1.call-done = f32[1,128,1024]{2,1,0:T(8,128)} async-done(((f32[1,128,1024]{2,1,0:T(8,128)}), f32[1,128,1024]{2,1,0:T(8,128)}) %all-reduce.36.cloned.1.call-update) | async-done | bytes 524304 | tf_op jit(solution)/shard_map/psum | solution.py:94
  716.9 7.6 multiply_add_fusion.1
  725.3 5.3 convolution_bitcast_fusion.12
  735.2 22.9 %all_to_all.60 = f32[1,1024,128]{2,0,1:T(1,128)} all-to-all(f32[1,1024,128]{2,0,1:T(1,128)S(1)} %copy.165), channel_id=1, replica_groups=mesh['dp'=8,'head'=4] {'head'}, dimensions={1} | all-to-all | bytes 1048576 | tf_op jit(solution)/shard_map/all_to_all | solution.py:160
  759.5 3.6 fusion.90
  763.2 7.3 fusion.55
  772.2 6.0 fusion.86
  786.0 2.8 fusion.51
  791.3 3.7 multiply_reduce_fusion
  806.7 6.0 fusion.30
  813.7 2.7 fusion.58
  816.5 6.3 convolution_bitcast_fusion.1
  822.9 7.0 convolution_bitcast_fusion
  831.9 4.4 convolution_bitcast_fusion.2
  836.3 5.2 fusion.99
  841.6 7.2 fusion.65
  852.8 4.6 fusion.13
  857.4 56.3 %reduce-scatter.14.cloned.1.call-done = f32[512,512]{1,0:T(8,128)} async-done(((f32[2048,512]{1,0:T(8,128)}), f32[512,512]{1,0:T(8,128)}) %reduce-scatter.14.cloned.1.call-update) | async-done | bytes 1048592 | tf_op jit(solution)/shard_map/reduce_scatter | solution.py:223
  913.8 79.5 %reduce-scatter.12.cloned.1.call-done = f32[128,2048]{1,0:T(8,128)} async-done(((f32[512,2048]{1,0:T(8,128)}), f32[128,2048]{1,0:T(8,128)}) %reduce-scatter.12.cloned.1.call-update) | async-done | bytes 1048592 | tf_op jit(solution)/shard_map/reduce_scatter | solution.py:222
  995.2 8.0 fusion.43
  1003.2 29.8 %all-reduce.40.cloned.1.call-done = f32[1,128,1024]{2,1,0:T(8,128)} async-done(((f32[1,128,1024]{2,1,0:T(8,128)}), f32[1,128,1024]{2,1,0:T(8,128)}) %all-reduce.40.cloned.1.call-update) | async-done | bytes 524304 | tf_op jit(solution)/shard_map/psum | solution.py:94
  1036.6 41.5 %reduce-scatter.6.cloned.1.call-done = f32[1,256,512]{2,1,0:T(8,128)} async-done(((f32[1,1024,512]{2,1,0:T(8,128)}), f32[1,256,512]{2,1,0:T(8,128)}) %reduce-scatter.6.cloned.1.call-update) | async-done | bytes 524304 | tf_op jit(solution)/shard_map/reduce_scatter | solution.py:201
  1078.1 3.4 fusion.76
  1082.0 9.4 all-reduce.12
  1091.6 23.7 %all-reduce.10 = (f32[1024]{0:T(1024)}, f32[128]{0:T(128)}, f32[1024]{0:T(1024)}, f32[1,1024]{1,0:T(1,128)}, f32[1,1024]{1,0:T(1,128)}, /*index=5*/f32[128]{0:T(128)}, f32[1024]{0:T(1024)}, f32[128]{0:T(128)}) all-reduce(f32[1024]{0:T(1024)S(1)} %get-tuple-element.144, ...), channel_id=1, replica_groups=mesh['dp'=8,'head'=4] {'dp'}, use_global_device_ids=true, to_apply=%region_50.51 | all-reduce | flops 5504 | bytes 44032 | tf_op jit(solution)/shard_map/psum | solution.py:231
  1116.4 318.3 %all-reduce.42.cloned.1.call-done = (f32[1024,256]{1,0:T(8,128)}, f32[512,2,256]{2,0,1:T(8,128)}, f32[256,1024]{1,0:T(8,128)}, f32[1024,1024]{1,0:T(8,128)}, f32...) async-done(((f32[1024,256]{1,0:T(8,128)}, ...) | async-done | bytes 27787280 | tf_op jit(solution)/shard_map/psum | solution.py:231
  1434.7 3.2 copy.184
  (578 shorter events, 170.2 us)
Async XLA Ops:
  7.2 162.7 %copy-start = (f32[1,1024,3,256]{3,1,2,0:T(8,128)S(1)}, f32[1,1024,3,256]{3,1,2,0:T(8,128)}, u32[]{:S(2)}) copy-start(f32[1,1024,3,256]{3,1,2,0:T(8,128)} %param.39) | copy-start | bytes 9437188
  7.2 59.3 %all-gather.9.cloned.1.call-start = ((), (), s32[]{:S(2)}) async-start(), calls=%async_computation.9 | async-start | bytes 2621440 | tf_op jit(solution)/shard_map/all_gather | solution.py:131
  8.6 242.1 %copy-start.118 = (f32[256]{0:T(256)}, f32[256]{0:T(256)S(1)}, u32[]{:S(2)}) copy-start(f32[256]{0:T(256)S(1)} %broadcast_multiply_fusion.1) | copy-start | bytes 3076
  10.4 240.3 %copy-start.122 = (f32[256]{0:T(256)}, f32[256]{0:T(256)S(1)}, u32[]{:S(2)}) copy-start(f32[256]{0:T(256)S(1)} %fusion.213) | copy-start | bytes 3076
  19.2 98.0 %all-reduce.24.cloned.1.call-start = ((), (), s32[]{:S(2)}) async-start(), calls=%async_computation.10 | async-start | bytes 1048576 | tf_op jit(solution)/shard_map/psum | solution.py:94
  23.0 48.9 %copy-start.173 = (s32[128]{0:T(128)}, s32[128]{0:T(128)S(1)}, u32[]{:S(2)}) copy-start(s32[128]{0:T(128)S(1)} %and_select_fusion) | copy-start | bytes 1540
  23.0 48.9 %copy-start.148 = (f32[128]{0:T(128)}, f32[128]{0:T(128)S(1)}, u32[]{:S(2)}) copy-start(f32[128]{0:T(128)S(1)} %broadcast_multiply_fusion.6) | copy-start | bytes 1540
  24.2 47.7 %copy-start.183 = (f32[128]{0:T(128)}, f32[128]{0:T(128)S(1)}, u32[]{:S(2)}) copy-start(f32[128]{0:T(128)S(1)} %multiply_reduce_fusion.19) | copy-start | bytes 1540
  24.3 47.7 %copy-start.164 = (f32[128]{0:T(128)}, f32[128]{0:T(128)S(1)}, u32[]{:S(2)}) copy-start(f32[128]{0:T(128)S(1)} %fusion.215) | copy-start | bytes 1540
  77.9 40.9 %copy-start.99 = (f32[4,64,128]{2,1,0:T(8,128)}, f32[4,64,128]{2,1,0:T(8,128)S(1)}, u32[]{:S(2)}) copy-start(f32[4,64,128]{2,1,0:T(8,128)S(1)} %fusion.52) | copy-start | bytes 393220
  77.9 41.4 %copy-start.114 = (f32[1024]{0:T(1024)S(1)}, f32[1024]{0:T(1024)}, u32[]{:S(2)}) copy-start(f32[1024]{0:T(1024)} %param.35) | copy-start | bytes 12292
  79.4 88.3 %all-reduce.26.cloned.1.call-start = ((), (), s32[]{:S(2)}) async-start(), calls=%async_computation.11 | async-start | bytes 1048576 | tf_op jit(solution)/shard_map/psum | solution.py:94
  129.2 40.6 %copy-start.124 = (f32[1,1024]{1,0:T(1,128)S(1)}, f32[1,1024]{1,0:T(1,128)}, u32[]{:S(2)}) copy-start(f32[1,1024]{1,0:T(1,128)} %param.38) | copy-start | bytes 12292
  129.3 91.0 %all-reduce.28.cloned.1.call-start = ((), (), s32[]{:S(2)}) async-start(), calls=%async_computation.12 | async-start | bytes 1048576 | tf_op jit(solution)/shard_map/psum | solution.py:94
  180.3 41.6 %copy-start.112 = (f32[1,1024]{1,0:T(1,128)S(1)}, f32[1,1024]{1,0:T(1,128)}, u32[]{:S(2)}) copy-start(f32[1,1024]{1,0:T(1,128)} %param.41) | copy-start | bytes 12292
  181.9 68.8 %all-gather.11.cloned.1.call-start = ((), (), s32[]{:S(2)}) async-start(), calls=%async_computation.14 | async-start | bytes 1310720 | tf_op jit(solution)/shard_map/all_gather | solution.py:124
  182.4 115.8 %all-reduce.30.cloned.1.call-start = ((), (), s32[]{:S(2)}) async-start(), calls=%async_computation.13 | async-start | bytes 1048576 | tf_op jit(solution)/shard_map/psum | solution.py:94
  231.9 110.1 %all-gather.13.cloned.1.call-start = ((), (), s32[]{:S(2)}) async-start(), calls=%async_computation.15 | async-start | bytes 1310720 | tf_op jit(solution)/shard_map/all_gather | solution.py:125
  232.6 186.9 %all-gather.15.cloned.1.call-start = ((), (), s32[]{:S(2)}) async-start(), calls=%async_computation.16 | async-start | bytes 5242880 | tf_op jit(solution)/shard_map/all_gather | solution.py:126
  233.4 267.0 %all-gather.17.cloned.1.call-start = ((), (), s32[]{:S(2)}) async-start(), calls=%async_computation.17 | async-start | bytes 5242880 | tf_op jit(solution)/shard_map/all_gather | solution.py:127
  241.2 14.7 %copy-start.108 = (f32[4,1,128]{2,1,0:T(1,128)}, f32[4,1,128]{2,1,0:T(1,128)S(1)}, u32[]{:S(2)}) copy-start(f32[4,1,128]{2,1,0:T(1,128)S(1)} %all-gather.1) | copy-start | bytes 6148
  255.9 22.4 %all-to-all-start = ((f32[1,256,512]{1,0,2:T(1,128)}), f32[1,256,512]{1,0,2:T(1,128)}, u32[]{:S(2)}, u32[]{:S(2)}) async-start(f32[1,256,512]{1,0,2:T(1,128)} %copy.157), calls=%async_computation | async-start | bytes 1048576 | tf_op jit(solution)/shard_map/all_to_all | solution.py:145
  278.3 22.1 %copy-start.110 = (f32[1024]{0:T(1024)S(1)}, f32[1024]{0:T(1024)}, u32[]{:S(2)}) copy-start(f32[1024]{0:T(1024)} %param.46) | copy-start | bytes 12292
  308.7 31.2 %all-to-all-start.1 = ((f32[1,1024,128]{2,0,1:T(1,128)}), f32[1,1024,128]{2,0,1:T(1,128)}, u32[]{:S(2)}, u32[]{:S(2)}) async-start(f32[1,1024,128]{2,0,1:T(1,128)} %copy.160), calls=%async_computation.1 | async-start | bytes 1048576 | tf_op jit(solution)/shard_map/all_to_all | solution.py:147
  517.8 17.8 %all-to-all-start.2 = ((f32[1,256,512]{1,0,2:T(1,128)}), f32[1,256,512]{1,0,2:T(1,128)}, u32[]{:S(2)}, u32[]{:S(2)}) async-start(f32[1,256,512]{1,0,2:T(1,128)} %copy.162), calls=%async_computation.2 | async-start | bytes 1048576 | tf_op jit(solution)/shard_map/all_to_all | solution.py:155
  524.6 74.8 %all-reduce.32.cloned.1.call-start = ((), (), s32[]{:S(2)}) async-start(), calls=%async_computation.18 | async-start | bytes 1048576 | tf_op jit(solution)/shard_map/psum | solution.py:94
  552.9 46.5 %copy-start.111 = (f32[1024]{0:T(1024)S(1)}, f32[1024]{0:T(1024)}, u32[]{:S(2)}) copy-start(f32[1024]{0:T(1024)} %param.46) | copy-start | bytes 12292
  552.9 46.5 %copy-start.156 = (f32[128]{0:T(128)S(1)}, f32[128]{0:T(128)}, u32[]{:S(2)}) copy-start(f32[128]{0:T(128)} %copy-done.155) | copy-start | bytes 1540
  552.9 46.5 %copy-start.172 = (f32[128]{0:T(128)S(1)}, f32[128]{0:T(128)}, u32[]{:S(2)}) copy-start(f32[128]{0:T(128)} %copy-done.171) | copy-start | bytes 1540
  555.7 45.8 %copy-start.191 = (f32[128]{0:T(128)S(1)}, f32[128]{0:T(128)}, u32[]{:S(2)}) copy-start(f32[128]{0:T(128)} %copy-done.190) | copy-start | bytes 1540
  556.7 46.3 %copy-start.84 = (f32[1,128,1,128]{3,1,2,0:T(8,128)}, f32[1,128,1,128]{3,1,2,0:T(8,128)S(1)}, u32[]{:S(2)}) copy-start(f32[1,128,1,128]{3,1,2,0:T(8,128)S(1)} %copy.170) | copy-start | bytes 196612
  559.5 95.9 %all-reduce.34.cloned.1.call-start = ((), (), s32[]{:S(2)}) async-start(), calls=%async_computation.19 | async-start | bytes 1048576 | tf_op jit(solution)/shard_map/psum | solution.py:94
  611.6 43.8 %copy-start.113 = (f32[1,1024]{1,0:T(1,128)S(1)}, f32[1,1024]{1,0:T(1,128)}, u32[]{:S(2)}) copy-start(f32[1,1024]{1,0:T(1,128)} %param.41) | copy-start | bytes 12292
  611.6 43.8 %copy-start.154 = (f32[128]{0:T(128)S(1)}, f32[128]{0:T(128)}, u32[]{:S(2)}) copy-start(f32[128]{0:T(128)} %copy-done.153) | copy-start | bytes 1540
  611.6 43.8 %copy-start.170 = (f32[128]{0:T(128)S(1)}, f32[128]{0:T(128)}, u32[]{:S(2)}) copy-start(f32[128]{0:T(128)} %copy-done.169) | copy-start | bytes 1540
  611.6 45.9 %copy-start.189 = (f32[128]{0:T(128)S(1)}, f32[128]{0:T(128)}, u32[]{:S(2)}) copy-start(f32[128]{0:T(128)} %copy-done.188) | copy-start | bytes 1540
  616.9 95.6 %all-reduce.36.cloned.1.call-start = ((), (), s32[]{:S(2)}) async-start(), calls=%async_computation.20 | async-start | bytes 1048576 | tf_op jit(solution)/shard_map/psum | solution.py:94
  669.0 43.6 %copy-start.125 = (f32[1,1024]{1,0:T(1,128)S(1)}, f32[1,1024]{1,0:T(1,128)}, u32[]{:S(2)}) copy-start(f32[1,1024]{1,0:T(1,128)} %param.38) | copy-start | bytes 12292
  669.0 43.6 %copy-start.158 = (f32[128]{0:T(128)S(1)}, f32[128]{0:T(128)}, u32[]{:S(2)}) copy-start(f32[128]{0:T(128)} %copy-done.157) | copy-start | bytes 1540
  674.1 42.6 %copy-start.37 = (f32[1,128,1024]{2,1,0:T(8,128)S(1)}, f32[1,128,1024]{2,1,0:T(8,128)}, u32[]{:S(2)}) copy-start(f32[1,128,1024]{2,1,0:T(8,128)} %copy-done.36) | copy-start | bytes 1572868
  674.1 42.7 %copy-start.88 = (f32[128,1024]{1,0:T(8,128)S(1)}, f32[128,1024]{1,0:T(8,128)}, u32[]{:S(2)}) copy-start(f32[128,1024]{1,0:T(8,128)} %copy-done.87) | copy-start | bytes 1572868
  674.1 105.4 %all-reduce.38.cloned.1.call-start = ((), (), s32[]{:S(2)}) async-start(), calls=%async_computation.21 | async-start | bytes 1048576 | tf_op jit(solution)/shard_map/psum | solution.py:94
  730.6 126.8 %reduce-scatter.10.cloned.1.call-start = ((), (), s32[]{:S(2)}) async-start(), calls=%async_computation.25 | async-start | bytes 1310720 | tf_op jit(solution)/shard_map/reduce_scatter | solution.py:221
  732.7 124.7 %reduce-scatter.8.cloned.1.call-start = ((), (), s32[]{:S(2)}) async-start(), calls=%async_computation.24 | async-start | bytes 1310720 | tf_op jit(solution)/shard_map/reduce_scatter | solution.py:220
  734.8 24.7 %copy-start.2 = (f32[1,256,512]{2,1,0:T(8,128)S(1)}, f32[1,256,512]{2,1,0:T(8,128)}, u32[]{:S(2)}) copy-start(f32[1,256,512]{2,1,0:T(8,128)} %param.27) | copy-start | bytes 1572868
  734.8 24.7 %copy-start.109 = (f32[4,1,128]{2,1,0:T(1,128)S(1)}, f32[4,1,128]{2,1,0:T(1,128)}, u32[]{:S(2)}) copy-start(f32[4,1,128]{2,1,0:T(1,128)} %copy-done.108) | copy-start | bytes 6148
  734.8 24.7 %copy-start.119 = (f32[256]{0:T(256)S(1)}, f32[256]{0:T(256)}, u32[]{:S(2)}) copy-start(f32[256]{0:T(256)} %copy-done.118) | copy-start | bytes 3076
  763.1 150.6 %reduce-scatter.14.cloned.1.call-start = ((), (), s32[]{:S(2)}) async-start(), calls=%async_computation.27 | async-start | bytes 5242880 | tf_op jit(solution)/shard_map/reduce_scatter | solution.py:223
  770.5 222.8 %reduce-scatter.12.cloned.1.call-start = ((), (), s32[]{:S(2)}) async-start(), calls=%async_computation.26 | async-start | bytes 5242880 | tf_op jit(solution)/shard_map/reduce_scatter | solution.py:222
  778.3 254.7 %all-reduce.40.cloned.1.call-start = ((), (), s32[]{:S(2)}) async-start(), calls=%async_computation.23 | async-start | bytes 1048576 | tf_op jit(solution)/shard_map/psum | solution.py:94
  801.7 276.3 %reduce-scatter.6.cloned.1.call-start = ((), (), s32[]{:S(2)}) async-start(), calls=%async_computation.22 | async-start | bytes 2621440 | tf_op jit(solution)/shard_map/reduce_scatter | solution.py:201
  812.7 622.0 %all-reduce.42.cloned.1.call-start = ((), (), s32[]{:S(2)}) async-start(), calls=%async_computation.28 | async-start | bytes 55574528 | tf_op jit(solution)/shard_map/psum | solution.py:231
  995.2 39.1 %copy-start.184 = (f32[128]{0:T(128)S(1)}, f32[128]{0:T(128)}, u32[]{:S(2)}) copy-start(f32[128]{0:T(128)} %copy-done.183) | copy-start | bytes 1540
  1003.2 74.8 %copy-start.45 = (f32[1,256,4,128]{1,3,2,0:T(8,128)S(1)}, f32[1,256,4,128]{1,3,2,0:T(8,128)}, u32[]{:S(2)}) copy-start(f32[1,256,4,128]{1,3,2,0:T(8,128)} %copy-done.44) | copy-start | bytes 1572868
  1003.2 74.8 %copy-start.120 = (f32[256]{0:T(256)S(1)}, f32[256]{0:T(256)}, u32[]{:S(2)}) copy-start(f32[256]{0:T(256)} %copy-done.118) | copy-start | bytes 3076
  1003.2 74.8 %copy-start.128 = (f32[4,1,128]{2,1,0:T(1,128)S(1)}, f32[4,1,128]{2,1,0:T(1,128)}, u32[]{:S(2)}) copy-start(f32[4,1,128]{2,1,0:T(1,128)} %copy-done.127) | copy-start | bytes 6148
  1035.6 45.8 %copy-start.163 = (f32[256]{0:T(256)S(1)}, f32[256]{0:T(256)}, u32[]{:S(2)}) copy-start(f32[256]{0:T(256)} %copy-done.162) | copy-start | bytes 3076
  1035.6 45.8 %copy-start.123 = (f32[256]{0:T(256)S(1)}, f32[256]{0:T(256)}, u32[]{:S(2)}) copy-start(f32[256]{0:T(256)} %copy-done.122) | copy-start | bytes 3076
  1036.6 45.4 %copy-start.179 = (f32[512]{0:T(512)S(1)}, f32[512]{0:T(512)}, u32[]{:S(2)}) copy-start(f32[512]{0:T(512)} %get-tuple-element.134) | copy-start | bytes 6148
  1036.6 55.1 %copy-start.143 = (f32[1024]{0:T(1024)S(1)}, f32[1024]{0:T(1024)}, u32[]{:S(2)}) copy-start(f32[1024]{0:T(1024)} %get-tuple-element.136) | copy-start | bytes 12292
  1036.6 55.1 %copy-start.144 = (f32[1024]{0:T(1024)S(1)}, f32[1024]{0:T(1024)}, u32[]{:S(2)}) copy-start(f32[1024]{0:T(1024)} %get-tuple-element.138) | copy-start | bytes 12292
  1036.6 55.1 %copy-start.145 = (f32[1024]{0:T(1024)S(1)}, f32[1024]{0:T(1024)}, u32[]{:S(2)}) copy-start(f32[1024]{0:T(1024)} %get-tuple-element.140) | copy-start | bytes 12292
  1036.6 55.1 %copy-start.146 = (f32[1024]{0:T(1024)S(1)}, f32[1024]{0:T(1024)}, u32[]{:S(2)}) copy-start(f32[1024]{0:T(1024)} %get-tuple-element.142) | copy-start | bytes 12292
  1036.6 78.7 %copy-start.43 = (f32[1,256,512]{2,1,0:T(8,128)S(1)}, f32[1,256,512]{2,1,0:T(8,128)}, u32[]{:S(2)}) copy-start(f32[1,256,512]{2,1,0:T(8,128)} %copy-done.41) | copy-start | bytes 1572868
  (154 other events, 600.9 us)
Sparse Core Ops, SparseCore 0:
  19.4 47.1 all-gather.8
  79.6 37.5 all-reduce.23
  129.4 38.2 all-reduce.25
  182.0 38.2 all-reduce.27
  221.7 28.9 all-gather.10
  253.5 44.6 all-reduce.29
  299.8 37.8 all-gather.12
  339.2 80.2 all-gather.14
  421.0 79.2 all-gather.16
  559.6 39.6 all-reduce.31
  617.0 38.2 all-reduce.33
  674.2 38.2 all-reduce.35
  730.7 45.5 all-reduce.37
  779.0 26.4 reduce-scatter.9
  808.3 25.7 reduce-scatter.7
  836.3 77.4 reduce-scatter.13
  916.0 77.2 reduce-scatter.11
  995.5 37.4 all-reduce.39
  1035.3 42.7 reduce-scatter.5
  1087.7 346.8 all-reduce.41
where the time goes:
time: 1480 us; the launch traced here: 1470 us
  waiting for transfers between devices  988 us (67%)
  matrix products  223 us (15%)
  blocking collectives  95.6 us (6%)
  local copies, waits for them, and re-layouts  84.8 us (6%)
  other arithmetic  42.2 us (3%)
  starting transfers between devices  19.5 us (1%)
  between operations  17.4 us (1%)
    psum x1, waiting for transfers between devices, local(): lax.psum((grad_read_gain_lat, shard_rgain_int, grad_read_query, grad_read...  318 us
    psum x9, waiting for transfers between devices, head_sum(): return lax.psum(partial_sum, 'head')  273 us
    dot_general x32, matrix products, product(): return jnp.matmul(former, latter, precision=PRECISE)  145 us
    reduce_scatter x1, waiting for transfers between devices, local(): lax.psum_scatter(grad_wup, 'head', scatter_dimension=0, tiled=True)  79.5 us
    all_gather x1, waiting for transfers between devices, local(): lax.all_gather(write_up, 'head', axis=0, tiled=True)  72.7 us
    all_gather x1, waiting for transfers between devices, local(): lax.all_gather(write_down, 'head', axis=0, tiled=True)  69.8 us
    reduce_scatter x1, waiting for transfers between devices, local(): lax.psum_scatter(grad_wdown, 'head', scatter_dimension=0, tiled=True)  56.3 us
    unnamed x410, local copies, waits for them, and re-layouts  51.3 us
  transfers between devices with their start and end apart: 23, of which 18 were waited for; matrix products, arithmetic and copies ran while one was open for 12% of the time, Pallas kernels for 0%

commit v1 on v0

v1 whole, which is shorter than its diff:
```python
import jax
import jax.numpy as jnp
from jax import lax
from jax.sharding import PartitionSpec as P

HEADS = 16
CROPS = 4
EPSILON = 1e-05
PRECISE = lax.Precision.HIGH
ROOT_HALF = 0.7071067811865476
DENSITY = 0.3989422804014327


def mm(left, right):
    return lax.dot_general(left, right, (((1,), (0,)), ((), ())), precision=PRECISE)


def mmt(left, right):
    return lax.dot_general(left, right, (((1,), (1,)), ((), ())), precision=PRECISE)


def tmm(left, right):
    return lax.dot_general(left, right, (((0,), (0,)), ((), ())), precision=PRECISE)


def normalise(values):
    centred = values - jnp.mean(values, axis=-1, keepdims=True)
    root = lax.rsqrt(jnp.mean(centred * centred, axis=-1, keepdims=True) + EPSILON)
    return centred * root, root


def norm_back(grad, xhat, root, gain):
    scaled = grad * gain
    return root * (
        scaled
        - jnp.mean(scaled, axis=-1, keepdims=True)
        - xhat * jnp.mean(scaled * xhat, axis=-1, keepdims=True)
    )


def cdf(values):
    return 0.5 * (1.0 + lax.erf(values * ROOT_HALF))


def gelu_slope(values):
    return cdf(values) + values * DENSITY * jnp.exp(-0.5 * values * values)


def heads_of(values, count):
    return values.reshape(values.shape[0], count, values.shape[1] // count)


def attend(queries, keys, values, mask, count):
    q, k, v = heads_of(queries, count), heads_of(keys, count), heads_of(values, count)
    scores = jnp.einsum("qhd,khd->hqk", q, k, precision=PRECISE) * (q.shape[-1] ** -0.5)
    scores = jnp.where(mask[None], scores, -1e30)
    top = jnp.max(scores, axis=-1, keepdims=True)
    weights = jnp.exp(scores - top)
    weights = weights / jnp.sum(weights, axis=-1, keepdims=True)
    out = jnp.einsum("hqk,khd->qhd", weights, v, precision=PRECISE)
    return out.reshape(queries.shape), weights


def attend_back(grad, queries, keys, values, weights, count):
    q, k, v = heads_of(queries, count), heads_of(keys, count), heads_of(values, count)
    g = heads_of(grad, count)
    factor = q.shape[-1] ** -0.5
    dv = jnp.einsum("hqk,qhd->khd", weights, g, precision=PRECISE)
    dp = jnp.einsum("qhd,khd->hqk", g, v, precision=PRECISE)
    ds = weights * (dp - jnp.sum(dp * weights, axis=-1, keepdims=True)) * factor
    dq = jnp.einsum("hqk,khd->qhd", ds, k, precision=PRECISE)
    dk = jnp.einsum("hqk,qhd->khd", ds, q, precision=PRECISE)
    return dq.reshape(queries.shape), dk.reshape(keys.shape), dv.reshape(values.shape)


def local(
    interface,
    latents,
    segment_ids,
    read_gain_lat,
    read_gain_int,
    read_query,
    read_keyval,
    read_out,
    read_gain_mlp,
    read_up,
    read_down,
    layer_gain_att,
    layer_qkv,
    layer_out,
    layer_gain_mlp,
    layer_up,
    layer_down,
    write_gain_int,
    write_query,
    write_gain_lat,
    write_keyval,
    write_out,
    write_gain_mlp,
    write_up,
    write_down,
    interface_cot,
    latents_cot,
):
    zs, ds = lax.axis_size("head"), lax.axis_size("dp")
    me, dd = lax.axis_index("head"), lax.axis_index("dp")
    here = HEADS // zs

    def shift(values, step):
        return lax.ppermute(values, "head", [(i, (i + step) % zs) for i in range(zs)])

    def z_scatter(parts):
        total = lax.dynamic_index_in_dim(parts, me, 0, keepdims=False)
        for step in range(1, zs):
            sent = lax.dynamic_index_in_dim(parts, (me + step) % zs, 0, keepdims=False)
            total = total + shift(sent, step)
        return total

    def z_gather(own):
        out = jnp.zeros((zs,) + own.shape, own.dtype)
        out = lax.dynamic_update_index_in_dim(out, own, me, 0)
        for step in range(1, zs):
            out = lax.dynamic_update_index_in_dim(out, shift(own, step), (me - step) % zs, 0)
        return out

    def add_sum(base, partial):
        rows = base.shape[0] // zs
        own = z_scatter(partial.reshape(zs, rows, -1))
        own = own + lax.dynamic_slice_in_dim(base, me * rows, rows, 0)
        return z_gather(own).reshape(base.shape)

    def head_sum(partial):
        rows = partial.shape[0] // zs
        own = z_scatter(partial.reshape(zs, rows, -1))
        return z_gather(own).reshape(partial.shape)

    def d_gather(parts):
        joined = jnp.concatenate(parts, axis=1) if len(parts) > 1 else parts[0]
        full = lax.all_gather(joined, "dp", axis=0, tiled=True)
        out, at = [], 0
        for part in parts:
            out.append(full[:, at : at + part.shape[1]])
            at += part.shape[1]
        return out

    interface, latents, segments = interface[0], latents[0], segment_ids[0]
    interface_cot, latents_cot = interface_cot[0], latents_cot[0]
    layer_gain_att, layer_gain_mlp = layer_gain_att[0], layer_gain_mlp[0]
    layer_out, layer_up, layer_down = layer_out[0], layer_up[0], layer_down[0]
    patches, wide = interface.shape
    count, deep = latents.shape
    qkv = layer_qkv[0].reshape(deep, -1)
    keyval = read_keyval.reshape(wide, -1)
    part = deep // zs
    hidden = write_down.shape[0] * zs

    crop = jnp.arange(count, dtype=jnp.int32) // (count // CROPS)
    own_segments = lax.dynamic_slice_in_dim(segments, me * patches, patches, 0)
    read_mask = crop[:, None] == segments[None, :]
    self_mask = crop[:, None] == crop[None, :]
    write_mask = own_segments[:, None] == crop[None, :]

    int_hat, int_root = normalise(interface)
    int_all = z_gather(int_hat).reshape(zs * patches, wide)
    gains = jnp.stack([read_gain_int, write_gain_int, write_gain_mlp])
    gains = jnp.transpose(z_gather(gains), (1, 0, 2)).reshape(3, wide)
    gain_read, gain_write, gain_mlp = gains[0], gains[1], gains[2]

    wq_rows, up_cols, kv_rows = wide // zs // ds, hidden // ds, deep // ds
    up_share = write_up.reshape(wide // zs, zs, ds, hidden // zs // ds)
    up_share = lax.dynamic_index_in_dim(up_share, dd, 2, keepdims=False).reshape(wide // zs, up_cols)
    down_share = lax.dynamic_index_in_dim(write_down.reshape(ds, -1, wide), dd, 0, keepdims=False)
    kv_share = lax.dynamic_slice_in_dim(write_keyval, dd * kv_rows, kv_rows, 0).reshape(kv_rows, -1)
    q_share = lax.dynamic_slice_in_dim(write_query, dd * wq_rows, wq_rows, 0)
    o_share = lax.dynamic_slice_in_dim(write_out, dd * wq_rows, wq_rows, 0)

    def d_z_gather(share):
        return lax.all_gather(z_gather(share), "dp", axis=0, tiled=False)

    shares = [up_share, down_share, kv_share, q_share, o_share]
    flat = jnp.concatenate([s.reshape(-1, 128) for s in shares], axis=0)
    int_all, flat = lax.optimization_barrier((int_all, flat))
    everything = d_z_gather(flat)
    pieces, at = [], 0
    for s in shares:
        n = s.size // 128
        pieces.append(everything[:, :, at : at + n].reshape((ds, zs) + s.shape))
        at += n
    full_up = jnp.transpose(pieces[0], (1, 2, 0, 3)).reshape(wide, hidden)
    full_down = pieces[1].reshape(hidden, wide)
    full_kv = jnp.transpose(pieces[2].reshape(ds, zs, kv_rows, 2, -1), (0, 2, 3, 1, 4)).reshape(deep, 2 * wide)
    full_query = jnp.transpose(pieces[3], (1, 0, 2, 3)).reshape(wide, wide)
    full_out = jnp.transpose(pieces[4], (1, 0, 2, 3)).reshape(wide, wide)

    lat_hat, lat_root = normalise(latents)
    lat_normed = lat_hat * read_gain_lat
    query = mm(lat_normed, read_query)
    int_normed = int_all * gain_read
    read_kv = mm(int_normed, keyval)
    read_k, read_v = read_kv[:, :part], read_kv[:, part:]
    read_attended, read_weights = attend(query, read_k, read_v, read_mask, here)
    state1 = add_sum(latents, mm(read_attended, read_out))
    hat1, root1 = normalise(state1)
    normed1 = hat1 * read_gain_mlp
    pre1 = mm(normed1, read_up)
    act1 = pre1 * cdf(pre1)
    state2 = add_sum(state1, mm(act1, read_down))
    lat_all, read_att_all, normed1_all, act1_all = d_gather([lat_normed, read_attended, normed1, act1])

    hat2, root2 = normalise(state2)
    normed2 = hat2 * layer_gain_att
    packed = mm(normed2, qkv)
    q2, k2, v2 = packed[:, :part], packed[:, part : 2 * part], packed[:, 2 * part :]
    self_attended, self_weights = attend(q2, k2, v2, self_mask, here)
    state3 = add_sum(state2, mm(self_attended, layer_out))
    hat3, root3 = normalise(state3)
    normed3 = hat3 * layer_gain_mlp
    pre3 = mm(normed3, layer_up)
    act3 = pre3 * cdf(pre3)
    state4 = add_sum(state3, mm(act3, layer_down))
    hat4, root4 = normalise(state4)
    normed4 = hat4 * write_gain_lat
    normed2_all, self_att_all, normed3_all, act3_all, normed4_all = d_gather(
        [normed2, self_attended, normed3, act3, normed4]
    )

    kv4 = mm(normed4, full_kv)
    write_k, write_v = kv4[:, :wide], kv4[:, wide:]
    write_normed = int_hat * gain_write
    write_q = mm(write_normed, full_query)
    write_attended, write_weights = attend(write_q, write_k, write_v, write_mask, HEADS)
    after = interface + mm(write_attended, full_out)
    after_hat, after_root = normalise(after)
    after_normed = after_hat * gain_mlp
    pre5 = mm(after_normed, full_up)
    act5 = pre5 * cdf(pre5)
    interface_new = after + mm(act5, full_down)

    dpre5 = mmt(interface_cot, full_down) * gelu_slope(pre5)
    dafter_normed = mmt(dpre5, full_up)
    dafter = interface_cot + norm_back(dafter_normed, after_hat, after_root, gain_mlp)
    dattended = mmt(dafter, full_out)
    dwrite_q, dwrite_k, dwrite_v = attend_back(
        dattended, write_q, write_k, write_v, write_weights, HEADS
    )
    dkv4 = jnp.concatenate([dwrite_k, dwrite_v], axis=1)
    dnormed4 = mmt(dkv4, full_kv)
    dsum4 = head_sum(dnormed4)
    dstate4 = latents_cot + norm_back(dsum4, hat4, root4, write_gain_lat)

    dup = tmm(after_normed, dpre5).reshape(zs, wide // zs, ds, -1)
    dup = jnp.transpose(dup, (2, 0, 1, 3)).reshape(ds, zs, -1, 128)
    ddown = tmm(act5, interface_cot).reshape(ds, zs, -1, 128)
    dquery = jnp.transpose(tmm(write_normed, dwrite_q).reshape(zs, ds, wq_rows, wide), (1, 0, 2, 3))
    dquery = dquery.reshape(ds, zs, -1, 128)
    dout = jnp.transpose(tmm(write_attended, dafter).reshape(zs, ds, wq_rows, wide), (1, 0, 2, 3))
    dout = dout.reshape(ds, zs, -1, 128)
    packed_grads = jnp.concatenate([dup, ddown, dquery, dout], axis=2)
    grads_mine = lax.psum_scatter(packed_grads, "dp", scatter_dimension=0, tiled=False)
    grads_mine = z_scatter(grads_mine)
    grads_all = lax.all_gather(grads_mine, "dp", axis=0, tiled=False)
    sizes = [dup.shape[2], ddown.shape[2], dquery.shape[2], dout.shape[2]]
    cut, at = [], 0
    for n in sizes:
        cut.append(grads_all[:, at : at + n])
        at += n
    grad_write_up = jnp.transpose(cut[0].reshape(ds, wide // zs, zs, -1), (1, 2, 0, 3)).reshape(write_up.shape)
    down_mine = cut[1].reshape(write_down.shape)
    grad_write_query = cut[2].reshape(write_query.shape)
    grad_write_out = cut[3].reshape(write_out.shape)

    dwrite_normed = mmt(dwrite_q, full_query)
    dint = dafter + norm_back(dwrite_normed, int_hat, int_root, gain_write)

    dkv_parts = jnp.transpose(dkv4.reshape(count, 2, zs, -1), (2, 0, 1, 3)).reshape(zs, count, -1)
    dkv_mine = z_scatter(dkv_parts)
    dpre3 = mmt(dstate4, layer_down) * gelu_slope(pre3)
    dnormed3 = head_sum(mmt(dpre3, layer_up))
    dkv_all, dstate4_all, dpre3_all = d_gather([dkv_mine, dstate4, dpre3])
    dstate3 = dstate4 + norm_back(dnormed3, hat3, root3, layer_gain_mlp)
    dself = mmt(dstate3, layer_out)
    dq2, dk2, dv2 = attend_back(dself, q2, k2, v2, self_weights, here)
    dpacked = jnp.concatenate([dq2, dk2, dv2], axis=1)
    dnormed2 = head_sum(mmt(dpacked, qkv))
    dstate3_all, dpacked_all = d_gather([dstate3, dpacked])
    dstate2 = dstate3 + norm_back(dnormed2, hat2, root2, layer_gain_att)

    dpre1 = mmt(dstate2, read_down) * gelu_slope(pre1)
    dnormed1 = head_sum(mmt(dpre1, read_up))
    dstate2_all, dpre1_all = d_gather([dstate2, dpre1])
    dstate1 = dstate2 + norm_back(dnormed1, hat1, root1, read_gain_mlp)
    dread = mmt(dstate1, read_out)
    dquery0, dread_k, dread_v = attend_back(dread, query, read_k, read_v, read_weights, here)
    dread_kv = jnp.concatenate([dread_k, dread_v], axis=1)
    dstate1_all, dquery0_all = d_gather([dstate1, dquery0])
    dlat_part = mmt(dquery0, read_query)
    dlat = head_sum(dlat_part)
    latents_grad = dstate1 + norm_back(dlat, lat_hat, lat_root, read_gain_lat)
    dint_part = mmt(dread_kv, keyval)
    dint_normed = z_scatter(dint_part.reshape(zs, patches, wide))
    interface_grad = dint + norm_back(dint_normed, int_hat, int_root, gain_read)
    grad_read_keyval = lax.psum(tmm(int_normed, dread_kv), "dp")

    def own_rows(values):
        rows = values.shape[0] // zs
        return lax.dynamic_slice_in_dim(values, me * rows, rows, 0)

    def gain_part(grad, hat):
        return jnp.sum(own_rows(grad) * own_rows(hat), axis=0)

    small = jnp.concatenate(
        [
            jnp.sum(dlat_part * lat_hat, axis=0),
            gain_part(dnormed1, hat1),
            gain_part(dnormed2, hat2),
            gain_part(dnormed3, hat3),
            gain_part(dsum4, hat4),
            jnp.sum(dint_normed * int_hat, axis=0),
            jnp.sum(dwrite_normed * int_hat, axis=0),
            jnp.sum(dafter_normed * after_hat, axis=0),
        ]
    )
    small = lax.psum(small, ("dp", "head"))
    lat_gains = small[: 5 * deep].reshape(5, deep)
    int_gains = small[5 * deep :].reshape(3, zs, wide // zs)
    int_gains = lax.dynamic_index_in_dim(int_gains, me, 1, keepdims=False)

    return (
        interface_new[None],
        state4[None],
        interface_grad[None],
        latents_grad[None],
        lat_gains[0],
        int_gains[0],
        tmm(lat_all, dquery0_all),
        grad_read_keyval.reshape(read_keyval.shape),
        tmm(read_att_all, dstate1_all),
        lat_gains[1],
        tmm(normed1_all, dpre1_all),
        tmm(act1_all, dstate2_all),
        lat_gains[2][None],
        tmm(normed2_all, dpacked_all).reshape(layer_qkv.shape),
        tmm(self_att_all, dstate3_all)[None],
        lat_gains[3][None],
        tmm(normed3_all, dpre3_all)[None],
        tmm(act3_all, dstate4_all)[None],
        int_gains[1],
        grad_write_query,
        lat_gains[4],
        tmm(normed4_all, dkv_all).reshape(write_keyval.shape),
        grad_write_out,
        int_gains[2],
        grad_write_up,
        down_mine,
    )


def solution(mesh):
    rows, both = P("dp", "head", None), P("dp", None, None)
    weights = (
        P(),
        P("head"),
        P(None, "head"),
        P(None, None, "head"),
        P("head", None),
        P(),
        P(None, "head"),
        P("head", None),
        P(),
        P(None, None, None, "head"),
        P(None, "head", None),
        P(),
        P(None, None, "head"),
        P(None, "head", None),
        P("head"),
        P("head", None),
        P(),
        P(None, None, "head"),
        P("head", None),
        P("head"),
        P("head", None),
        P("head", None),
    )
    in_specs = (rows, both, P("dp", None)) + weights + (rows, both)
    out_specs = (rows, both, rows, both) + weights
    return jax.shard_map(local, mesh=mesh, in_specs=in_specs, out_specs=out_specs, check_vma=False)
```

time: 1480 us -> 1040 us (0.70)
  waiting for transfers between devices: 988 us -> 449 us
  local copies, waits for them, and re-layouts: 84.8 us -> 181 us
  blocking collectives: 95.6 us -> 41 us
  starting transfers between devices: 19.5 us -> 73 us
  matrix products: 223 us -> 192 us
  other arithmetic: 42.2 us -> 66.9 us
    psum x10 -> x1, waiting for transfers between devices: 592 us -> 17.2 us  [local(): grad_read_keyval = lax.psum(tmm(int_normed, dread_kv), 'dp')]
    ppermute x0 -> x72, waiting for transfers between devices: none -> 334 us  [shift(): lax.ppermute(values, 'head', [(i, (i + step) % zs) for i in range(zs)])]
    reduce_scatter x5 -> x1, waiting for transfers between devices: 177 us -> 0.01 us  [local(): lax.psum_scatter(packed_grads, 'dp', scatter_dimension=0, tiled=False)]
    all_gather x5 -> x8, waiting for transfers between devices: 192 us -> 97.5 us  [the longest x6 97.5 us: d_gather(): full = lax.all_gather(joined, 'dp', axis=0, tiled=True)]
    ppermute x0 -> x72, starting transfers between devices: none -> 72.1 us  [shift(): lax.ppermute(values, 'head', [(i, (i + step) % zs) for i in range(zs)])]
    all_gather x3 -> x0, blocking collectives: 39.6 us -> none  [the longest x1 26.3 us: local(): lax.all_gather(write_gain_mlp, 'head', axis=0, tiled=True)]
    reshape x10 -> x28, local copies, waits for them, and re-layouts: 15.3 us -> 54.1 us  [the longest x5 12.6 us: local(): pieces.append(everything[:, :, at:at + n].reshape((ds, zs) + s.shape))]
    dot_general x59 -> x60, matrix products: 222 us -> 192 us  [the longest x14 88.4 us: tmm(): lax.dot_general(left, right, (((0,), (0,)), ((), ())), precision=PRECISE)]
  transfers between devices with their start and end apart: 23 -> 82, of which waited for: 18 -> 62; matrix products, arithmetic and copies ran while one was open for 12% -> 29% of each run, Pallas kernels for 0% -> 0%
where the time goes in v1:
time: 1040 us; the launch traced here: 1020 us
  waiting for transfers between devices  449 us (43%)
  matrix products  192 us (18%)
  local copies, waits for them, and re-layouts  181 us (17%)
  starting transfers between devices  73 us (7%)
  other arithmetic  66.9 us (6%)
  blocking collectives  41 us (4%)
  between operations  18.1 us (2%)
    ppermute x72, waiting for transfers between devices, shift(): lax.ppermute(values, 'head', [(i, (i + step) % zs) for i in range(zs)])  334 us
    all_gather x6, waiting for transfers between devices, d_gather(): full = lax.all_gather(joined, 'dp', axis=0, tiled=True)  97.5 us
    dot_general x14, matrix products, tmm(): lax.dot_general(left, right, (((0,), (0,)), ((), ())), precision=PRECISE)  88.4 us
    ppermute x72, starting transfers between devices, shift(): lax.ppermute(values, 'head', [(i, (i + step) % zs) for i in range(zs)])  72.1 us
    psum x1, blocking collectives, local(): small = lax.psum(small, ('dp', 'head'))  41 us
    dot_general x14, matrix products, mm(): lax.dot_general(left, right, (((1,), (0,)), ((), ())), precision=PRECISE)  38.3 us
    dot_general x14, matrix products, mmt(): lax.dot_general(left, right, (((1,), (1,)), ((), ())), precision=PRECISE)  38.2 us
    unnamed x404, local copies, waits for them, and re-layouts  36.3 us
  transfers between devices with their start and end apart: 82, of which 62 were waited for; matrix products, arithmetic and copies ran while one was open for 29% of the time, Pallas kernels for 0%

profile of v1, /device:TPU:13, one launch (start us, length us, event | category | flops | bytes accessed | tf_op | source)
XLA Modules:
  0.0 1021.6 jit_solution(6261991920770751514)
XLA Ops:
  27.6 5.5 collective-permute-done
  34.1 30.6 %collective-permute-done.1 = f32[256,512]{1,0:T(8,128)} collective-permute-done((f32[256,512]{1,0:T(8,128)}, f32[256,512]{1,0:T(8,128)}, u32[]{:S(2)}, u32[]{:S(2)}) %collective-permute-start.1) | collective-permute-done | bytes 524320 | tf_op jit(solution)/shard_map/ppermute | solution.py:110
  65.8 4.5 collective-permute-done.2
  74.1 8.0 collective-permute-done.30
  82.8 26.8 %collective-permute-done.31 = f32[896,128]{1,0:T(8,128)S(1)} collective-permute-done((f32[896,128]{1,0:T(8,128)S(1)}, f32[896,128]{1,0:T(8,128)S(1)}, u32[]{:S(2)}, u32[]{:S(2)}) %collective-permute-start.31) | collective-permute-done | bytes 458784 | tf_op jit(solution)/shard_map/ppermute | solution.py:110
  130.8 6.2 collective-permute-done.7
  137.0 4.8 collective-permute-done.8
  146.7 6.5 collective-permute-done.10
  156.3 4.7 fusion.210
  169.3 4.8 collective-permute-done.13
  181.7 6.4 collective-permute-done.16
  190.4 3.6 fusion.255
  200.9 6.5 collective-permute-done.19
  218.3 6.5 collective-permute-done.23
  226.7 4.7 constant_dynamic-update-slice_fusion.10
  238.1 6.6 collective-permute-done.25
  256.3 6.4 collective-permute-done.29
  263.2 9.8 fusion.244
  273.0 6.9 copy.227
  279.9 5.5 reshape.1977
  285.4 3.5 fusion.256
  307.6 5.3 reshape.1985
  312.9 4.6 copy.168
  317.6 4.0 copy.218
  321.5 4.9 reshape_reshape.15
  326.4 4.6 fusion.146
  339.5 3.9 fusion.80
  348.7 5.1 reshape.2015
  372.3 4.7 reshape.2016
  377.0 8.1 pad_maximum_fusion
  385.2 5.5 reshape.2032
  390.7 4.8 fusion.85
  399.3 4.3 fusion.221
  408.3 4.5 fusion.93
  417.6 6.4 collective-permute-done.34
  436.9 5.8 collective-permute-done.38
  446.8 4.6 fusion.65
  458.8 6.4 collective-permute-done.40
  474.1 5.9 collective-permute-done.43
  493.0 19.2 %collective-permute-done.70 = f32[640,128]{1,0:T(8,128)S(1)} collective-permute-done((f32[640,128]{1,0:T(8,128)S(1)}, f32[640,128]{1,0:T(8,128)S(1)}, u32[]{:S(2)}, u32[]{:S(2)}) %collective-permute-start.70) | collective-permute-done | bytes 327712 | tf_op jit(solution)/shard_map/ppermute | solution.py:110
  537.6 6.5 collective-permute-done.46
  550.3 6.5 collective-permute-done.49
  568.0 4.4 fusion.257
  577.1 6.5 collective-permute-done.52
  593.7 5.0 collective-permute-done.55
  628.6 6.5 collective-permute-done.67
  650.0 5.2 fusion.68
  683.6 48.2 %collective-permute-done.60 = f32[32,1024]{1,0:T(8,128)S(1)} collective-permute-done((f32[32,1024]{1,0:T(8,128)S(1)}, f32[32,1024]{1,0:T(8,128)S(1)}, u32[]{:S(2)}, u32[]{:S(2)}) %collective-permute-start.60) | collective-permute-done | bytes 131104 | tf_op jit(solution)/shard_map/ppermute | solution.py:110
  739.0 10.9 %collective-permute-start.65 = (f32[32,1024]{1,0:T(8,128)S(1)}, f32[32,1024]{1,0:T(8,128)S(1)}, u32[]{:S(2)}, u32[]{:S(2)}) collective-permute-start(f32[32,1024]{1,0:T(8,128)S(1)} %get-tuple-element.135), channel_id=1, source_target_pairs={{0,3},{1,0},{2,1},{3,2},{4,7},{5,4},{6,5},{7,6},{8,11},{9,8},{10,9... | collective-permute-start | bytes 393224 | tf_op jit(solution)/shard_map/ppermute | solution.py:110
  751.7 5.0 collective-permute-done.65
  761.2 41.0 %psum.14 = f32[6656]{0:T(1024)S(1)} all-reduce(f32[6656]{0:T(1024)S(1)} %constant_dynamic-update-slice_fusion.13), channel_id=1, replica_groups=mesh['dp'=8,'head'=4] {'dp','head'}, use_global_device_ids=true, to_apply=%region_47.48 | all-reduce | flops 6656 | bytes 53248 | tf_op jit(solution)/shard_map/psum | solution.py:323
  815.8 12.0 %fusion.12 = f32[1024,1024]{1,0:T(8,128)} fusion(f32[1024,2048]{1,0:T(8,128)} %all-gather.16.cloned.1.call-done, f32[1024,3328]{1,0:T(8,128)} %all-gather.12.cloned.1.call-done), kind=kOutput, calls=%fused_computation.13 | convolution fusion | flops 6442450944 | bytes 12582912 | tf_op jit(solution)/shard_map/dot_general | solution.py:23
  827.8 10.2 %fusion.15 = f32[1024,1024]{1,0:T(8,128)} fusion(f32[1024,2048]{1,0:T(8,128)S(1)} %copy-done.183, f32[1024,3328]{1,0:T(8,128)} %all-gather.12.cloned.1.call-done), kind=kOutput, calls=%fused_computation.16 | convolution fusion | flops 6442450944 | bytes 12582912 | tf_op jit(solution)/shard_map/dot_general | solution.py:23
  838.1 5.4 fusion.18
  843.5 6.9 fusion.20
  850.4 50.8 %all-gather.18.cloned.1.call-done = f32[1024,4352]{1,0:T(8,128)} async-done(((f32[128,4352]{1,0:T(8,128)}), f32[1024,4352]{1,0:T(8,128)}) %all-gather.18.cloned.1.call-update) | async-done | bytes 17825808 | tf_op jit(solution)/shard_map/all_gather | solution.py:139
  901.2 4.4 fusion
  906.9 46.7 %all-gather.20.cloned.1.call-done = f32[1024,1792]{1,0:T(8,128)} async-done(((f32[128,1792]{1,0:T(8,128)}), f32[1024,1792]{1,0:T(8,128)}) %all-gather.20.cloned.1.call-update) | async-done | bytes 7340048 | tf_op jit(solution)/shard_map/all_gather | solution.py:139
  953.6 9.2 fusion.10
  962.8 3.6 copy.198
  966.4 11.4 %fusion.37 = f32[1,1024,1024]{2,1,0:T(8,128)} fusion(f32[1024,2304]{1,0:T(8,128)} %all-gather.22.cloned.1.call-done, f32[1024,4352]{1,0:T(8,128)} %all-gather.18.cloned.1.call-done), kind=kOutput, calls=%fused_computation.38 | convolution fusion | flops 6442450944 | bytes 12582912 | tf_op jit(solution)/shard_map/dot_general | solution.py:23
  977.8 5.5 fusion.62
  983.4 11.2 %fusion.32 = f32[1,1024,1024]{2,1,0:T(8,128)} fusion(f32[1024,2304]{1,0:T(8,128)} %all-gather.22.cloned.1.call-done, f32[1024,4352]{1,0:T(8,128)} %all-gather.18.cloned.1.call-done), kind=kOutput, calls=%fused_computation.37 | convolution fusion | flops 6442450944 | bytes 12582912 | tf_op jit(solution)/shard_map/dot_general | solution.py:23
  994.5 17.2 %all-reduce.2.cloned.1.call-done = f32[512,2,256]{2,1,0:T(2,128)} async-done(((f32[512,2,256]{2,1,0:T(2,128)}), f32[512,2,256]{2,1,0:T(2,128)}) %all-reduce.2.cloned.1.call-update) | async-done | bytes 1048592 | tf_op jit(solution)/shard_map/psum | solution.py:302
  (830 shorter events, 381.5 us)
Async XLA Ops:
  7.2 256.0 %all-gather.10.cloned.1.call-start = ((), (), s32[]{:S(2)}) async-start(), calls=%async_computation.1 | async-start | bytes 16515072 | tf_op jit(solution)/shard_map/all_gather | solution.py:178
  8.0 11.0 %collective-permute-start.3 = (f32[3,128]{1,0:T(4,128)S(1)}, f32[3,128]{1,0:T(4,128)S(1)}, u32[]{:S(2)}, u32[]{:S(2)}) collective-permute-start(f32[3,128]{1,0:T(4,128)S(1)} %pad_maximum_fusion.6), channel_id=1, source_target_pairs={{0,1},{1,2},{2,3},{3,0},{4,5},{5,6},{6,7},{7,4},{8,9},{9,10},{10,1... | collective-permute-start | bytes 4616 | tf_op jit(solution)/shard_map/ppermute | solution.py:110
  9.3 9.7 collective-permute-start.4
  10.4 8.7 collective-permute-start.5
  20.8 12.2 %collective-permute-start = (f32[256,512]{1,0:T(8,128)}, f32[256,512]{1,0:T(8,128)}, u32[]{:S(2)}, u32[]{:S(2)}) collective-permute-start(f32[256,512]{1,0:T(8,128)} %get-tuple-element.131), channel_id=1, source_target_pairs={{0,1},{1,2},{2,3},{3,0},{4,5},{5,6},{6,7},{7,4},{8,9},{9,10},{10,1... | collective-permute-start | bytes 1572872 | tf_op jit(solution)/shard_map/ppermute | solution.py:110
  22.4 42.4 %collective-permute-start.1 = (f32[256,512]{1,0:T(8,128)}, f32[256,512]{1,0:T(8,128)}, u32[]{:S(2)}, u32[]{:S(2)}) collective-permute-start(f32[256,512]{1,0:T(8,128)} %get-tuple-element.131), channel_id=1, source_target_pairs={{0,2},{1,3},{2,0},{3,1},{4,6},{5,7},{6,4},{7,5},{8,10},{9,11},{10,... | collective-permute-start | bytes 1572872 | tf_op jit(solution)/shard_map/ppermute | solution.py:110
  26.9 43.4 %collective-permute-start.2 = (f32[256,512]{1,0:T(8,128)}, f32[256,512]{1,0:T(8,128)S(1)}, u32[]{:S(2)}, u32[]{:S(2)}) collective-permute-start(f32[256,512]{1,0:T(8,128)} %get-tuple-element.131), channel_id=1, source_target_pairs={{0,3},{1,0},{2,1},{3,2},{4,7},{5,4},{6,5},{7,6},{8,11},{9,8},{10,9... | collective-permute-start | bytes 1572872 | tf_op jit(solution)/shard_map/ppermute | solution.py:110
  70.4 11.6 %collective-permute-start.30 = (f32[896,128]{1,0:T(8,128)S(1)}, f32[896,128]{1,0:T(8,128)S(1)}, u32[]{:S(2)}, u32[]{:S(2)}) collective-permute-start(f32[896,128]{1,0:T(8,128)S(1)} %copy-done.78), channel_id=1, source_target_pairs={{0,1},{1,2},{2,3},{3,0},{4,5},{5,6},{6,7},{7,4},{8,9},{9,10},{10,1... | collective-permute-start | bytes 1376264 | tf_op jit(solution)/shard_map/ppermute | solution.py:110
  70.5 39.2 %collective-permute-start.31 = (f32[896,128]{1,0:T(8,128)S(1)}, f32[896,128]{1,0:T(8,128)S(1)}, u32[]{:S(2)}, u32[]{:S(2)}) collective-permute-start(f32[896,128]{1,0:T(8,128)S(1)} %copy-done.78), channel_id=1, source_target_pairs={{0,2},{1,3},{2,0},{3,1},{4,6},{5,7},{6,4},{7,5},{8,10},{9,11},{10,... | collective-permute-start | bytes 1376264 | tf_op jit(solution)/shard_map/ppermute | solution.py:110
  70.5 39.9 %collective-permute-start.32 = (f32[896,128]{1,0:T(8,128)S(1)}, f32[896,128]{1,0:T(8,128)S(1)}, u32[]{:S(2)}, u32[]{:S(2)}) collective-permute-start(f32[896,128]{1,0:T(8,128)S(1)} %copy-done.78), channel_id=1, source_target_pairs={{0,3},{1,0},{2,1},{3,2},{4,7},{5,4},{6,5},{7,6},{8,11},{9,8},{10,9... | collective-permute-start | bytes 1376264 | tf_op jit(solution)/shard_map/ppermute | solution.py:110
  111.3 371.6 %reduce-scatter.2.cloned.1.call-start = ((), (), s32[]{:S(2)}) async-start(), calls=%async_computation.9 | async-start | bytes 11796480 | tf_op jit(solution)/shard_map/reduce_scatter | solution.py:259
  126.3 10.7 %collective-permute-start.7 = (f32[32,1024]{1,0:T(8,128)S(1)}, f32[32,1024]{1,0:T(8,128)S(1)}, u32[]{:S(2)}, u32[]{:S(2)}) collective-permute-start(f32[32,1024]{1,0:T(8,128)S(1)} %get-tuple-element.209), channel_id=1, source_target_pairs={{0,2},{1,3},{2,0},{3,1},{4,6},{5,7},{6,4},{7,5},{8,10},{9,11},{10,... | collective-permute-start | bytes 393224 | tf_op jit(solution)/shard_map/ppermute | solution.py:110
  129.4 12.4 %collective-permute-start.8 = (f32[32,1024]{1,0:T(8,128)S(1)}, f32[32,1024]{1,0:T(8,128)S(1)}, u32[]{:S(2)}, u32[]{:S(2)}) collective-permute-start(f32[32,1024]{1,0:T(8,128)S(1)} %get-tuple-element.208), channel_id=1, source_target_pairs={{0,3},{1,0},{2,1},{3,2},{4,7},{5,4},{6,5},{7,6},{8,11},{9,8},{10,9... | collective-permute-start | bytes 393224 | tf_op jit(solution)/shard_map/ppermute | solution.py:110
  142.0 11.2 %collective-permute-start.10 = (f32[32,1024]{1,0:T(8,128)S(1)}, f32[32,1024]{1,0:T(8,128)S(1)}, u32[]{:S(2)}, u32[]{:S(2)}) collective-permute-start(f32[32,1024]{1,0:T(8,128)S(1)} %get-tuple-element.158), channel_id=1, source_target_pairs={{0,2},{1,3},{2,0},{3,1},{4,6},{5,7},{6,4},{7,5},{8,10},{9,11},{10,... | collective-permute-start | bytes 393224 | tf_op jit(solution)/shard_map/ppermute | solution.py:110
  142.3 12.5 %collective-permute-start.11 = (f32[32,1024]{1,0:T(8,128)S(1)}, f32[32,1024]{1,0:T(8,128)S(1)}, u32[]{:S(2)}, u32[]{:S(2)}) collective-permute-start(f32[32,1024]{1,0:T(8,128)S(1)} %get-tuple-element.158), channel_id=1, source_target_pairs={{0,3},{1,0},{2,1},{3,2},{4,7},{5,4},{6,5},{7,6},{8,11},{9,8},{10,9... | collective-permute-start | bytes 393224 | tf_op jit(solution)/shard_map/ppermute | solution.py:110
  162.7 6.5 collective-permute-start.12
  162.8 11.3 %collective-permute-start.13 = (f32[32,1024]{1,0:T(8,128)S(1)}, f32[32,1024]{1,0:T(8,128)S(1)}, u32[]{:S(2)}, u32[]{:S(2)}) collective-permute-start(f32[32,1024]{1,0:T(8,128)S(1)} %get-tuple-element.206), channel_id=1, source_target_pairs={{0,2},{1,3},{2,0},{3,1},{4,6},{5,7},{6,4},{7,5},{8,10},{9,11},{10,... | collective-permute-start | bytes 393224 | tf_op jit(solution)/shard_map/ppermute | solution.py:110
  164.3 12.4 %collective-permute-start.14 = (f32[32,1024]{1,0:T(8,128)S(1)}, f32[32,1024]{1,0:T(8,128)S(1)}, u32[]{:S(2)}, u32[]{:S(2)}) collective-permute-start(f32[32,1024]{1,0:T(8,128)S(1)} %get-tuple-element.205), channel_id=1, source_target_pairs={{0,3},{1,0},{2,1},{3,2},{4,7},{5,4},{6,5},{7,6},{8,11},{9,8},{10,9... | collective-permute-start | bytes 393224 | tf_op jit(solution)/shard_map/ppermute | solution.py:110
  177.0 11.1 %collective-permute-start.16 = (f32[32,1024]{1,0:T(8,128)S(1)}, f32[32,1024]{1,0:T(8,128)S(1)}, u32[]{:S(2)}, u32[]{:S(2)}) collective-permute-start(f32[32,1024]{1,0:T(8,128)S(1)} %get-tuple-element.154), channel_id=1, source_target_pairs={{0,2},{1,3},{2,0},{3,1},{4,6},{5,7},{6,4},{7,5},{8,10},{9,11},{10,... | collective-permute-start | bytes 393224 | tf_op jit(solution)/shard_map/ppermute | solution.py:110
  177.6 12.3 %collective-permute-start.17 = (f32[32,1024]{1,0:T(8,128)S(1)}, f32[32,1024]{1,0:T(8,128)S(1)}, u32[]{:S(2)}, u32[]{:S(2)}) collective-permute-start(f32[32,1024]{1,0:T(8,128)S(1)} %get-tuple-element.154), channel_id=1, source_target_pairs={{0,3},{1,0},{2,1},{3,2},{4,7},{5,4},{6,5},{7,6},{8,11},{9,8},{10,9... | collective-permute-start | bytes 393224 | tf_op jit(solution)/shard_map/ppermute | solution.py:110
  196.2 11.2 %collective-permute-start.19 = (f32[32,1024]{1,0:T(8,128)S(1)}, f32[32,1024]{1,0:T(8,128)S(1)}, u32[]{:S(2)}, u32[]{:S(2)}) collective-permute-start(f32[32,1024]{1,0:T(8,128)S(1)} %get-tuple-element.203), channel_id=1, source_target_pairs={{0,2},{1,3},{2,0},{3,1},{4,6},{5,7},{6,4},{7,5},{8,10},{9,11},{10,... | collective-permute-start | bytes 393224 | tf_op jit(solution)/shard_map/ppermute | solution.py:110
  197.7 12.3 %collective-permute-start.20 = (f32[32,1024]{1,0:T(8,128)S(1)}, f32[32,1024]{1,0:T(8,128)S(1)}, u32[]{:S(2)}, u32[]{:S(2)}) collective-permute-start(f32[32,1024]{1,0:T(8,128)S(1)} %get-tuple-element.202), channel_id=1, source_target_pairs={{0,3},{1,0},{2,1},{3,2},{4,7},{5,4},{6,5},{7,6},{8,11},{9,8},{10,9... | collective-permute-start | bytes 393224 | tf_op jit(solution)/shard_map/ppermute | solution.py:110
  213.4 11.4 %collective-permute-start.23 = (f32[32,1024]{1,0:T(8,128)S(1)}, f32[32,1024]{1,0:T(8,128)S(1)}, u32[]{:S(2)}, u32[]{:S(2)}) collective-permute-start(f32[32,1024]{1,0:T(8,128)S(1)} %get-tuple-element.152), channel_id=1, source_target_pairs={{0,3},{1,0},{2,1},{3,2},{4,7},{5,4},{6,5},{7,6},{8,11},{9,8},{10,9... | collective-permute-start | bytes 393224 | tf_op jit(solution)/shard_map/ppermute | solution.py:110
  233.6 11.1 %collective-permute-start.25 = (f32[32,1024]{1,0:T(8,128)S(1)}, f32[32,1024]{1,0:T(8,128)S(1)}, u32[]{:S(2)}, u32[]{:S(2)}) collective-permute-start(f32[32,1024]{1,0:T(8,128)S(1)} %get-tuple-element.200), channel_id=1, source_target_pairs={{0,2},{1,3},{2,0},{3,1},{4,6},{5,7},{6,4},{7,5},{8,10},{9,11},{10,... | collective-permute-start | bytes 393224 | tf_op jit(solution)/shard_map/ppermute | solution.py:110
  234.0 12.4 %collective-permute-start.26 = (f32[32,1024]{1,0:T(8,128)S(1)}, f32[32,1024]{1,0:T(8,128)S(1)}, u32[]{:S(2)}, u32[]{:S(2)}) collective-permute-start(f32[32,1024]{1,0:T(8,128)S(1)} %get-tuple-element.199), channel_id=1, source_target_pairs={{0,3},{1,0},{2,1},{3,2},{4,7},{5,4},{6,5},{7,6},{8,11},{9,8},{10,9... | collective-permute-start | bytes 393224 | tf_op jit(solution)/shard_map/ppermute | solution.py:110
  248.2 5.9 collective-permute-start.27
  250.6 5.6 collective-permute-start.28
  252.6 10.0 collective-permute-start.29
  385.1 420.4 %all-gather.24.cloned.1.call-start = ((), (), s32[]{:S(2)}) async-start(), calls=%async_computation.10 | async-start | bytes 2949120 | tf_op jit(solution)/shard_map/all_gather | solution.py:261
  412.9 11.2 %collective-permute-start.34 = (f32[32,1024]{1,0:T(8,128)S(1)}, f32[32,1024]{1,0:T(8,128)S(1)}, u32[]{:S(2)}, u32[]{:S(2)}) collective-permute-start(f32[32,1024]{1,0:T(8,128)S(1)} %get-tuple-element.195), channel_id=1, source_target_pairs={{0,2},{1,3},{2,0},{3,1},{4,6},{5,7},{6,4},{7,5},{8,10},{9,11},{10,... | collective-permute-start | bytes 393224 | tf_op jit(solution)/shard_map/ppermute | solution.py:110
  413.0 13.4 %collective-permute-start.35 = (f32[32,1024]{1,0:T(8,128)S(1)}, f32[32,1024]{1,0:T(8,128)S(1)}, u32[]{:S(2)}, u32[]{:S(2)}) collective-permute-start(f32[32,1024]{1,0:T(8,128)S(1)} %get-tuple-element.194), channel_id=1, source_target_pairs={{0,3},{1,0},{2,1},{3,2},{4,7},{5,4},{6,5},{7,6},{8,11},{9,8},{10,9... | collective-permute-start | bytes 393224 | tf_op jit(solution)/shard_map/ppermute | solution.py:110
  431.4 11.3 %collective-permute-start.38 = (f32[32,1024]{1,0:T(8,128)S(1)}, f32[32,1024]{1,0:T(8,128)S(1)}, u32[]{:S(2)}, u32[]{:S(2)}) collective-permute-start(f32[32,1024]{1,0:T(8,128)S(1)} %get-tuple-element.148), channel_id=1, source_target_pairs={{0,3},{1,0},{2,1},{3,2},{4,7},{5,4},{6,5},{7,6},{8,11},{9,8},{10,9... | collective-permute-start | bytes 393224 | tf_op jit(solution)/shard_map/ppermute | solution.py:110
  454.0 11.2 %collective-permute-start.40 = (f32[32,1024]{1,0:T(8,128)S(1)}, f32[32,1024]{1,0:T(8,128)S(1)}, u32[]{:S(2)}, u32[]{:S(2)}) collective-permute-start(f32[32,1024]{1,0:T(8,128)S(1)} %get-tuple-element.192), channel_id=1, source_target_pairs={{0,2},{1,3},{2,0},{3,1},{4,6},{5,7},{6,4},{7,5},{8,10},{9,11},{10,... | collective-permute-start | bytes 393224 | tf_op jit(solution)/shard_map/ppermute | solution.py:110
  455.0 12.4 %collective-permute-start.41 = (f32[32,1024]{1,0:T(8,128)S(1)}, f32[32,1024]{1,0:T(8,128)S(1)}, u32[]{:S(2)}, u32[]{:S(2)}) collective-permute-start(f32[32,1024]{1,0:T(8,128)S(1)} %get-tuple-element.191), channel_id=1, source_target_pairs={{0,3},{1,0},{2,1},{3,2},{4,7},{5,4},{6,5},{7,6},{8,11},{9,8},{10,9... | collective-permute-start | bytes 393224 | tf_op jit(solution)/shard_map/ppermute | solution.py:110
  468.9 11.1 %collective-permute-start.43 = (f32[32,1024]{1,0:T(8,128)S(1)}, f32[32,1024]{1,0:T(8,128)S(1)}, u32[]{:S(2)}, u32[]{:S(2)}) collective-permute-start(f32[32,1024]{1,0:T(8,128)S(1)} %get-tuple-element.146), channel_id=1, source_target_pairs={{0,2},{1,3},{2,0},{3,1},{4,6},{5,7},{6,4},{7,5},{8,10},{9,11},{10,... | collective-permute-start | bytes 393224 | tf_op jit(solution)/shard_map/ppermute | solution.py:110
  469.9 12.4 %collective-permute-start.44 = (f32[32,1024]{1,0:T(8,128)S(1)}, f32[32,1024]{1,0:T(8,128)S(1)}, u32[]{:S(2)}, u32[]{:S(2)}) collective-permute-start(f32[32,1024]{1,0:T(8,128)S(1)} %get-tuple-element.146), channel_id=1, source_target_pairs={{0,3},{1,0},{2,1},{3,2},{4,7},{5,4},{6,5},{7,6},{8,11},{9,8},{10,9... | collective-permute-start | bytes 393224 | tf_op jit(solution)/shard_map/ppermute | solution.py:110
  484.2 8.8 collective-permute-start.69
  484.3 28.0 %collective-permute-start.70 = (f32[640,128]{1,0:T(8,128)S(1)}, f32[640,128]{1,0:T(8,128)S(1)}, u32[]{:S(2)}, u32[]{:S(2)}) collective-permute-start(f32[640,128]{1,0:T(8,128)S(1)} %get-tuple-element.175), channel_id=1, source_target_pairs={{0,2},{1,3},{2,0},{3,1},{4,6},{5,7},{6,4},{7,5},{8,10},{9,11},{10,... | collective-permute-start | bytes 983048 | tf_op jit(solution)/shard_map/ppermute | solution.py:110
  485.9 29.2 %collective-permute-start.71 = (f32[640,128]{1,0:T(8,128)S(1)}, f32[640,128]{1,0:T(8,128)S(1)}, u32[]{:S(2)}, u32[]{:S(2)}) collective-permute-start(f32[640,128]{1,0:T(8,128)S(1)} %get-tuple-element.174), channel_id=1, source_target_pairs={{0,3},{1,0},{2,1},{3,2},{4,7},{5,4},{6,5},{7,6},{8,11},{9,8},{10,9... | collective-permute-start | bytes 983048 | tf_op jit(solution)/shard_map/ppermute | solution.py:110
  516.9 298.9 %all-gather.16.cloned.1.call-start = ((), (), s32[]{:S(2)}) async-start(), calls=%async_computation.5 | async-start | bytes 9437184 | tf_op jit(solution)/shard_map/all_gather | solution.py:139
  532.9 11.1 %collective-permute-start.46 = (f32[32,1024]{1,0:T(8,128)S(1)}, f32[32,1024]{1,0:T(8,128)S(1)}, u32[]{:S(2)}, u32[]{:S(2)}) collective-permute-start(f32[32,1024]{1,0:T(8,128)S(1)} %get-tuple-element.189), channel_id=1, source_target_pairs={{0,2},{1,3},{2,0},{3,1},{4,6},{5,7},{6,4},{7,5},{8,10},{9,11},{10,... | collective-permute-start | bytes 393224 | tf_op jit(solution)/shard_map/ppermute | solution.py:110
  533.2 12.3 %collective-permute-start.47 = (f32[32,1024]{1,0:T(8,128)S(1)}, f32[32,1024]{1,0:T(8,128)S(1)}, u32[]{:S(2)}, u32[]{:S(2)}) collective-permute-start(f32[32,1024]{1,0:T(8,128)S(1)} %get-tuple-element.188), channel_id=1, source_target_pairs={{0,3},{1,0},{2,1},{3,2},{4,7},{5,4},{6,5},{7,6},{8,11},{9,8},{10,9... | collective-permute-start | bytes 393224 | tf_op jit(solution)/shard_map/ppermute | solution.py:110
  545.7 11.1 %collective-permute-start.49 = (f32[32,1024]{1,0:T(8,128)S(1)}, f32[32,1024]{1,0:T(8,128)S(1)}, u32[]{:S(2)}, u32[]{:S(2)}) collective-permute-start(f32[32,1024]{1,0:T(8,128)S(1)} %get-tuple-element.144), channel_id=1, source_target_pairs={{0,2},{1,3},{2,0},{3,1},{4,6},{5,7},{6,4},{7,5},{8,10},{9,11},{10,... | collective-permute-start | bytes 393224 | tf_op jit(solution)/shard_map/ppermute | solution.py:110
  547.3 12.3 %collective-permute-start.50 = (f32[32,1024]{1,0:T(8,128)S(1)}, f32[32,1024]{1,0:T(8,128)S(1)}, u32[]{:S(2)}, u32[]{:S(2)}) collective-permute-start(f32[32,1024]{1,0:T(8,128)S(1)} %get-tuple-element.144), channel_id=1, source_target_pairs={{0,3},{1,0},{2,1},{3,2},{4,7},{5,4},{6,5},{7,6},{8,11},{9,8},{10,9... | collective-permute-start | bytes 393224 | tf_op jit(solution)/shard_map/ppermute | solution.py:110
  568.0 247.8 %all-gather.12.cloned.1.call-start = ((), (), s32[]{:S(2)}) async-start(), calls=%async_computation.2 | async-start | bytes 15335424 | tf_op jit(solution)/shard_map/all_gather | solution.py:139
  572.6 11.1 %collective-permute-start.52 = (f32[32,1024]{1,0:T(8,128)S(1)}, f32[32,1024]{1,0:T(8,128)S(1)}, u32[]{:S(2)}, u32[]{:S(2)}) collective-permute-start(f32[32,1024]{1,0:T(8,128)S(1)} %get-tuple-element.186), channel_id=1, source_target_pairs={{0,2},{1,3},{2,0},{3,1},{4,6},{5,7},{6,4},{7,5},{8,10},{9,11},{10,... | collective-permute-start | bytes 393224 | tf_op jit(solution)/shard_map/ppermute | solution.py:110
  573.0 12.5 %collective-permute-start.53 = (f32[32,1024]{1,0:T(8,128)S(1)}, f32[32,1024]{1,0:T(8,128)S(1)}, u32[]{:S(2)}, u32[]{:S(2)}) collective-permute-start(f32[32,1024]{1,0:T(8,128)S(1)} %get-tuple-element.185), channel_id=1, source_target_pairs={{0,3},{1,0},{2,1},{3,2},{4,7},{5,4},{6,5},{7,6},{8,11},{9,8},{10,9... | collective-permute-start | bytes 393224 | tf_op jit(solution)/shard_map/ppermute | solution.py:110
  587.2 11.4 %collective-permute-start.55 = (f32[32,1024]{1,0:T(8,128)}, f32[32,1024]{1,0:T(8,128)S(1)}, u32[]{:S(2)}, u32[]{:S(2)}) collective-permute-start(f32[32,1024]{1,0:T(8,128)} %get-tuple-element.138), channel_id=1, source_target_pairs={{0,2},{1,3},{2,0},{3,1},{4,6},{5,7},{6,4},{7,5},{8,10},{9,11},{10,... | collective-permute-start | bytes 393224 | tf_op jit(solution)/shard_map/ppermute | solution.py:110
  588.5 12.5 %collective-permute-start.56 = (f32[32,1024]{1,0:T(8,128)}, f32[32,1024]{1,0:T(8,128)S(1)}, u32[]{:S(2)}, u32[]{:S(2)}) collective-permute-start(f32[32,1024]{1,0:T(8,128)} %get-tuple-element.138), channel_id=1, source_target_pairs={{0,3},{1,0},{2,1},{3,2},{4,7},{5,4},{6,5},{7,6},{8,11},{9,8},{10,9... | collective-permute-start | bytes 393224 | tf_op jit(solution)/shard_map/ppermute | solution.py:110
  613.4 224.7 %all-gather.14.cloned.1.call-start = ((), (), s32[]{:S(2)}) async-start(), calls=%async_computation.3 | async-start | bytes 5898240 | tf_op jit(solution)/shard_map/all_gather | solution.py:139
  616.7 233.8 %all-gather.22.cloned.1.call-start = ((), (), s32[]{:S(2)}) async-start(), calls=%async_computation.8 | async-start | bytes 10616832 | tf_op jit(solution)/shard_map/all_gather | solution.py:139
  624.0 11.2 %collective-permute-start.67 = (f32[128,256]{1,0:T(8,128)S(1)}, f32[128,256]{1,0:T(8,128)S(1)}, u32[]{:S(2)}, u32[]{:S(2)}) collective-permute-start(f32[128,256]{1,0:T(8,128)S(1)} %get-tuple-element.180), channel_id=1, source_target_pairs={{0,2},{1,3},{2,0},{3,1},{4,6},{5,7},{6,4},{7,5},{8,10},{9,11},{10,... | collective-permute-start | bytes 393224 | tf_op jit(solution)/shard_map/ppermute | solution.py:110
  625.4 12.4 %collective-permute-start.68 = (f32[128,256]{1,0:T(8,128)S(1)}, f32[128,256]{1,0:T(8,128)S(1)}, u32[]{:S(2)}, u32[]{:S(2)}) collective-permute-start(f32[128,256]{1,0:T(8,128)S(1)} %get-tuple-element.179), channel_id=1, source_target_pairs={{0,3},{1,0},{2,1},{3,2},{4,7},{5,4},{6,5},{7,6},{8,11},{9,8},{10,9... | collective-permute-start | bytes 393224 | tf_op jit(solution)/shard_map/ppermute | solution.py:110
  640.9 260.3 %all-gather.18.cloned.1.call-start = ((), (), s32[]{:S(2)}) async-start(), calls=%async_computation.6 | async-start | bytes 20054016 | tf_op jit(solution)/shard_map/all_gather | solution.py:139
  643.0 310.6 %all-gather.20.cloned.1.call-start = ((), (), s32[]{:S(2)}) async-start(), calls=%async_computation.7 | async-start | bytes 8257536 | tf_op jit(solution)/shard_map/all_gather | solution.py:139
  646.3 365.5 %all-reduce.2.cloned.1.call-start = ((), (), s32[]{:S(2)}) async-start(), calls=%async_computation.4 | async-start | bytes 2097152 | tf_op jit(solution)/shard_map/psum | solution.py:302
  678.2 79.9 %collective-permute-start.57 = (f32[256,512]{1,0:T(8,128)}, f32[256,512]{1,0:T(8,128)}, u32[]{:S(2)}, u32[]{:S(2)}) collective-permute-start(f32[256,512]{1,0:T(8,128)} %get-tuple-element.168), channel_id=1, source_target_pairs={{0,1},{1,2},{2,3},{3,0},{4,5},{5,6},{6,7},{7,4},{8,9},{9,10},{10,1... | collective-permute-start | bytes 1572872 | tf_op jit(solution)/shard_map/ppermute | solution.py:110
  678.3 79.9 %collective-permute-start.58 = (f32[256,512]{1,0:T(8,128)}, f32[256,512]{1,0:T(8,128)}, u32[]{:S(2)}, u32[]{:S(2)}) collective-permute-start(f32[256,512]{1,0:T(8,128)} %get-tuple-element.170), channel_id=1, source_target_pairs={{0,2},{1,3},{2,0},{3,1},{4,6},{5,7},{6,4},{7,5},{8,10},{9,11},{10,... | collective-permute-start | bytes 1572872 | tf_op jit(solution)/shard_map/ppermute | solution.py:110
  678.9 52.9 %collective-permute-start.60 = (f32[32,1024]{1,0:T(8,128)S(1)}, f32[32,1024]{1,0:T(8,128)S(1)}, u32[]{:S(2)}, u32[]{:S(2)}) collective-permute-start(f32[32,1024]{1,0:T(8,128)S(1)} %get-tuple-element.181), channel_id=1, source_target_pairs={{0,1},{1,2},{2,3},{3,0},{4,5},{5,6},{6,7},{7,4},{8,9},{9,10},{10,1... | collective-permute-start | bytes 393224 | tf_op jit(solution)/shard_map/ppermute | solution.py:110
  681.0 53.6 %collective-permute-start.61 = (f32[32,1024]{1,0:T(8,128)S(1)}, f32[32,1024]{1,0:T(8,128)S(1)}, u32[]{:S(2)}, u32[]{:S(2)}) collective-permute-start(f32[32,1024]{1,0:T(8,128)S(1)} %get-tuple-element.183), channel_id=1, source_target_pairs={{0,2},{1,3},{2,0},{3,1},{4,6},{5,7},{6,4},{7,5},{8,10},{9,11},{10,... | collective-permute-start | bytes 393224 | tf_op jit(solution)/shard_map/ppermute | solution.py:110
  682.5 52.1 %collective-permute-start.62 = (f32[32,1024]{1,0:T(8,128)S(1)}, f32[32,1024]{1,0:T(8,128)S(1)}, u32[]{:S(2)}, u32[]{:S(2)}) collective-permute-start(f32[32,1024]{1,0:T(8,128)S(1)} %get-tuple-element.182), channel_id=1, source_target_pairs={{0,3},{1,0},{2,1},{3,2},{4,7},{5,4},{6,5},{7,6},{8,11},{9,8},{10,9... | collective-permute-start | bytes 393224 | tf_op jit(solution)/shard_map/ppermute | solution.py:110
  731.8 26.3 %collective-permute-start.59 = (f32[256,512]{1,0:T(8,128)}, f32[256,512]{1,0:T(8,128)}, u32[]{:S(2)}, u32[]{:S(2)}) collective-permute-start(f32[256,512]{1,0:T(8,128)} %get-tuple-element.169), channel_id=1, source_target_pairs={{0,3},{1,0},{2,1},{3,2},{4,7},{5,4},{6,5},{7,6},{8,11},{9,8},{10,9... | collective-permute-start | bytes 1572872 | tf_op jit(solution)/shard_map/ppermute | solution.py:110
  734.8 16.8 %collective-permute-start.64 = (f32[32,1024]{1,0:T(8,128)S(1)}, f32[32,1024]{1,0:T(8,128)S(1)}, u32[]{:S(2)}, u32[]{:S(2)}) collective-permute-start(f32[32,1024]{1,0:T(8,128)S(1)} %get-tuple-element.135), channel_id=1, source_target_pairs={{0,2},{1,3},{2,0},{3,1},{4,6},{5,7},{6,4},{7,5},{8,10},{9,11},{10,... | collective-permute-start | bytes 393224 | tf_op jit(solution)/shard_map/ppermute | solution.py:110
  739.0 17.7 %collective-permute-start.65 = (f32[32,1024]{1,0:T(8,128)S(1)}, f32[32,1024]{1,0:T(8,128)S(1)}, u32[]{:S(2)}, u32[]{:S(2)}) collective-permute-start(f32[32,1024]{1,0:T(8,128)S(1)} %get-tuple-element.135), channel_id=1, source_target_pairs={{0,3},{1,0},{2,1},{3,2},{4,7},{5,4},{6,5},{7,6},{8,11},{9,8},{10,9... | collective-permute-start | bytes 393224 | tf_op jit(solution)/shard_map/ppermute | solution.py:110
  (209 other events, 1962.7 us)
Sparse Core Ops, SparseCore 0:
  111.4 83.0 all-gather.9
  385.3 81.9 reduce-scatter.1
  517.0 29.5 all-gather.23
  568.1 53.5 all-gather.15
  624.0 76.3 all-gather.11
  702.1 41.4 all-gather.13
  745.5 59.8 all-gather.21
  807.3 93.8 all-gather.17
  903.1 50.4 all-gather.19
  957.2 54.5 all-reduce.1

commit v2 on v1

v2 whole, which is shorter than its diff:
```python
import functools

import jax
import jax.numpy as jnp
from jax import lax
from jax.experimental import pallas as pl
from jax.experimental.pallas import tpu as pltpu
from jax.sharding import PartitionSpec as P

HEADS = 16
CROPS = 4
EPSILON = 1e-05
PRECISE = lax.Precision.HIGH
ROOT_HALF = 0.7071067811865476
DENSITY = 0.3989422804014327
VMEM_LIMIT = 56 * 1024 * 1024


def mm(left, right):
    return lax.dot_general(left, right, (((1,), (0,)), ((), ())), precision=PRECISE)


def mmt(left, right):
    return lax.dot_general(left, right, (((1,), (1,)), ((), ())), precision=PRECISE)


def tmm(left, right):
    return lax.dot_general(left, right, (((0,), (0,)), ((), ())), precision=PRECISE)


def normalise(values):
    centred = values - jnp.mean(values, axis=-1, keepdims=True)
    root = lax.rsqrt(jnp.mean(centred * centred, axis=-1, keepdims=True) + EPSILON)
    return centred * root, root


def norm_back(grad, xhat, root, gain):
    scaled = grad * gain
    return root * (
        scaled
        - jnp.mean(scaled, axis=-1, keepdims=True)
        - xhat * jnp.mean(scaled * xhat, axis=-1, keepdims=True)
    )


def cdf(values):
    return 0.5 * (1.0 + lax.erf(values * ROOT_HALF))


def gelu_slope(values):
    return cdf(values) + values * DENSITY * jnp.exp(-0.5 * values * values)


def shape_of(*dims):
    return jax.ShapeDtypeStruct(dims, jnp.float32)


def run_whole(kernel, outs, args, flops=1e9, scratch=(), anywhere=0):
    moved = sum(a.size * 4 for a in args) + sum(int(functools.reduce(lambda x, y: x * y, o.shape)) * 4 for o in outs)
    fast = len(args) - anywhere
    return pl.pallas_call(
        kernel,
        out_shape=outs,
        in_specs=[pl.BlockSpec(memory_space=pltpu.VMEM)] * fast + [pl.BlockSpec(memory_space=pl.ANY)] * anywhere,
        out_specs=[pl.BlockSpec(memory_space=pltpu.VMEM)] * len(outs),
        scratch_shapes=list(scratch),
        compiler_params=pltpu.CompilerParams(vmem_limit_bytes=VMEM_LIMIT),
        cost_estimate=pl.CostEstimate(flops=int(flops * 3), bytes_accessed=int(moved), transcendentals=0),
    )(*args)


def lane_mask(lanes, width, head):
    return lax.broadcasted_iota(jnp.int32, (1, lanes), 1) // width == head


def spread(values, width):
    lanes = values.shape[1]
    return jnp.concatenate(
        [jnp.where(lane_mask(lanes, width, h), values, 0.0) for h in range(lanes // width)], axis=0
    )


def fold(values, width):
    lanes = values.shape[1]
    rows = values.shape[0] // (lanes // width)
    total = jnp.zeros((rows, lanes), jnp.float32)
    for h in range(lanes // width):
        total = total + jnp.where(lane_mask(lanes, width, h), values[h * rows : (h + 1) * rows], 0.0)
    return total


def attend_group(q, k, v, mask, width):
    count = q.shape[1] // width
    scores = mmt(spread(q, width), k) * (width ** -0.5)
    scores = scores.reshape(count, q.shape[0], k.shape[0])
    scores = jnp.where(mask[None], scores, -1e30)
    weights = jnp.exp(scores - jnp.max(scores, axis=-1, keepdims=True))
    weights = weights / jnp.sum(weights, axis=-1, keepdims=True)
    weights = weights.reshape(count * q.shape[0], k.shape[0])
    return fold(mm(weights, v), width), weights


def attend_group_back(grad, q, k, v, weights, width):
    grads = spread(grad, width)
    dp = mmt(grads, v)
    ds = weights * (dp - jnp.sum(dp * weights, axis=-1, keepdims=True)) * (width ** -0.5)
    return fold(mm(ds, k), width), tmm(ds, spread(q, width)), tmm(weights, grads)


def crop_rows(count, total):
    return lax.broadcasted_iota(jnp.int32, (count, 1), 0) // (total // CROPS)


def crop_lanes(count, total):
    return lax.broadcasted_iota(jnp.int32, (1, count), 1) // (total // CROPS)


def groups_of(ref, start, size, lanes):
    return [slice(start + at, start + at + lanes) for at in range(0, size, lanes)]


def ffn_kernel(state_ref, gain_ref, up_ref, down_ref, normed_ref, pre_ref, act_ref, out_ref):
    @pl.when(pl.program_id(0) == 0)
    def _():
        hat, _ = normalise(state_ref[...])
        normed_ref[...] = hat * gain_ref[...]
        out_ref[...] = jnp.zeros_like(out_ref)

    pre = mm(normed_ref[...], up_ref[...])
    act = pre * cdf(pre)
    pre_ref[...] = pre
    act_ref[...] = act
    out_ref[...] += mm(act, down_ref[...])


def ffn_forward(state, gain, up, down):
    rows, deep = state.shape
    inner = up.shape[1]
    tile = min(256, inner)
    whole = pl.BlockSpec((rows, deep), lambda t: (0, 0))
    part = pl.BlockSpec((rows, tile), lambda t: (0, t))
    return pl.pallas_call(
        ffn_kernel,
        grid=(inner // tile,),
        out_shape=[shape_of(rows, deep), shape_of(rows, inner), shape_of(rows, inner), shape_of(rows, deep)],
        in_specs=[
            whole,
            pl.BlockSpec((1, deep), lambda t: (0, 0)),
            pl.BlockSpec((deep, tile), lambda t: (0, t)),
            pl.BlockSpec((tile, deep), lambda t: (t, 0)),
        ],
        out_specs=[whole, part, part, whole],
        compiler_params=pltpu.CompilerParams(vmem_limit_bytes=VMEM_LIMIT),
        cost_estimate=pl.CostEstimate(flops=12 * rows * deep * inner, bytes_accessed=8 * deep * inner, transcendentals=0),
    )(state, gain[None], up, down)


def residual_back(base_ref, dsum_ref, state_ref, gain_ref, grad_ref, dgain_ref):
    hat, root = normalise(state_ref[...])
    dsum = dsum_ref[...]
    grad_ref[...] = base_ref[...] + norm_back(dsum, hat, root, gain_ref[...])
    dgain_ref[...] = jnp.sum(dsum * hat, axis=0, keepdims=True)


def ffn_back_kernel(
    base_ref, dsum_ref, state_ref, gain_ref, pre_ref, up_ref, down_ref, grad_ref, dgain_ref, dpre_ref, out_ref
):
    @pl.when(pl.program_id(0) == 0)
    def _():
        residual_back(base_ref, dsum_ref, state_ref, gain_ref, grad_ref, dgain_ref)
        out_ref[...] = jnp.zeros_like(out_ref)

    dpre = mmt(grad_ref[...], down_ref[...]) * gelu_slope(pre_ref[...])
    dpre_ref[...] = dpre
    out_ref[...] += mmt(dpre, up_ref[...])


def ffn_backward(base, dsum, state, gain, pre, up, down):
    rows, deep = state.shape
    inner = up.shape[1]
    tile = min(256, inner)
    whole = pl.BlockSpec((rows, deep), lambda t: (0, 0))
    row = pl.BlockSpec((1, deep), lambda t: (0, 0))
    part = pl.BlockSpec((rows, tile), lambda t: (0, t))
    return pl.pallas_call(
        ffn_back_kernel,
        grid=(inner // tile,),
        out_shape=[shape_of(rows, deep), shape_of(1, deep), shape_of(rows, inner), shape_of(rows, deep)],
        in_specs=[
            whole,
            whole,
            whole,
            row,
            part,
            pl.BlockSpec((deep, tile), lambda t: (0, t)),
            pl.BlockSpec((tile, deep), lambda t: (t, 0)),
        ],
        out_specs=[whole, row, part, whole],
        compiler_params=pltpu.CompilerParams(vmem_limit_bytes=VMEM_LIMIT),
        cost_estimate=pl.CostEstimate(flops=12 * rows * deep * inner, bytes_accessed=8 * deep * inner, transcendentals=0),
    )(base, dsum, state, gain[None], pre, up, down)


def self_kernel(width, state_ref, gain_ref, qkv_ref, wout_ref, normed_ref, packed_ref, att_ref, weights_ref, out_ref):
    hat, _ = normalise(state_ref[...])
    normed = hat * gain_ref[...]
    normed_ref[...] = normed
    part = att_ref.shape[1]
    for at in range(3):
        packed_ref[:, at * part : (at + 1) * part] = mm(normed, qkv_ref[:, at * part : (at + 1) * part])
    rows = normed.shape[0]
    mask = crop_rows(rows, rows) == crop_lanes(rows, rows)
    for g in range(part // 128):
        q, k, v = [packed_ref[:, at * part + g * 128 : at * part + (g + 1) * 128] for at in range(3)]
        att, weights = attend_group(q, k, v, mask, width)
        att_ref[:, g * 128 : (g + 1) * 128] = att
        n = weights.shape[0]
        weights_ref[g * n : (g + 1) * n] = weights
    out_ref[...] = mm(att_ref[...], wout_ref[...])


def self_back_kernel(
    width,
    base_ref,
    dsum_ref,
    state_ref,
    gain_ref,
    packed_ref,
    weights_ref,
    qkv_ref,
    wout_ref,
    grad_ref,
    dgain_ref,
    dpacked_ref,
    out_ref,
):
    residual_back(base_ref, dsum_ref, state_ref, gain_ref, grad_ref, dgain_ref)
    part = dpacked_ref.shape[1] // 3
    datt = mmt(grad_ref[...], wout_ref[...])
    count = 128 // width * datt.shape[0]
    for g in range(part // 128):
        q, k, v = [packed_ref[:, at * part + g * 128 : at * part + (g + 1) * 128] for at in range(3)]
        found = attend_group_back(
            datt[:, g * 128 : (g + 1) * 128], q, k, v, weights_ref[g * count : (g + 1) * count], width
        )
        for at in range(3):
            dpacked_ref[:, at * part + g * 128 : at * part + (g + 1) * 128] = found[at]
    out_ref[...] = mmt(dpacked_ref[...], qkv_ref[...])


def read_kernel(width, q_ref, hat_ref, gain_ref, seg_ref, keyval_ref, wout_ref, kv_ref, att_ref, weights_ref, out_ref):
    part = att_ref.shape[1]
    patches = kv_ref.shape[0] // hat_ref.shape[0]
    for z in range(hat_ref.shape[0]):
        kv_ref[z * patches : (z + 1) * patches] = mm(hat_ref[z, :patches] * gain_ref[...], keyval_ref[...])
    rows = q_ref.shape[0]
    mask = crop_rows(rows, rows) == seg_ref[...]
    for g in range(part // 128):
        at = slice(g * 128, (g + 1) * 128)
        att, weights = attend_group(
            q_ref[:, at], kv_ref[:, at], kv_ref[:, part + g * 128 : part + (g + 1) * 128], mask, width
        )
        att_ref[:, at] = att
        n = weights.shape[0]
        weights_ref[g * n : (g + 1) * n] = weights
    out_ref[...] = mm(att_ref[...], wout_ref[...])


def read_back_kernel(
    width,
    base_ref,
    dsum_ref,
    state_ref,
    gain_ref,
    q_ref,
    kv_ref,
    weights_ref,
    wquery_ref,
    keyval_ref,
    wout_ref,
    latents_ref,
    hat_ref,
    grad_ref,
    dgain_ref,
    dq_ref,
    dkv_ref,
    dlat_ref,
    dint_ref,
    dgain_lat_ref,
    dgain_int_ref,
):
    residual_back(base_ref, dsum_ref, state_ref, gain_ref, grad_ref, dgain_ref)
    part = dq_ref.shape[1]
    datt = mmt(grad_ref[...], wout_ref[...])
    count = 128 // width * datt.shape[0]
    for g in range(part // 128):
        at, behind = slice(g * 128, (g + 1) * 128), slice(part + g * 128, part + (g + 1) * 128)
        found = attend_group_back(
            datt[:, at], q_ref[:, at], kv_ref[:, at], kv_ref[:, behind], weights_ref[g * count : (g + 1) * count], width
        )
        dq_ref[:, at], dkv_ref[:, at], dkv_ref[:, behind] = found
    dlat = mmt(dq_ref[...], wquery_ref[...])
    dlat_ref[...] = dlat
    hat, _ = normalise(latents_ref[...])
    dgain_lat_ref[...] = jnp.sum(dlat * hat, axis=0, keepdims=True)
    dint = mmt(dkv_ref[...], keyval_ref[...])
    dint_ref[...] = dint
    patches = dint.shape[0] // hat_ref.shape[0]
    dgain_int = jnp.zeros_like(dgain_int_ref)
    for z in range(hat_ref.shape[0]):
        dgain_int += jnp.sum(dint[z * patches : (z + 1) * patches] * hat_ref[z, :patches], axis=0, keepdims=True)
    dgain_int_ref[...] = dgain_int


def write_kernel(
    width,
    state_ref,
    gain_ref,
    hat_ref,
    int_ref,
    cot_ref,
    gains_ref,
    seg_ref,
    place_ref,
    sources,
    normed_ref,
    new_ref,
    dafter_ref,
    dq_ref,
    att_ref,
    y_ref,
    act_ref,
    dpre_ref,
    dkv_ref,
    dgain_ref,
    out_ref,
    dhat_ref,
    wkv,
    wquery,
    wout,
    up,
    down,
    kv,
    q,
    weights,
    dy,
    sems,
):
    targets = [wkv, wquery, wout, up, down]
    if len(sources) == 5:
        for n in range(5):
            pltpu.make_async_copy(sources[n], targets[n], sems.at[n]).start()
    else:
        bring_pieces(sources, targets, sems, place_ref[0])

    def arrived(n):
        pltpu.make_async_copy(targets[n], targets[n], sems.at[n]).wait()

    hat4, _ = normalise(state_ref[...])
    normed = hat4 * gain_ref[...]
    normed_ref[...] = normed
    wide = hat_ref.shape[1]
    patches = hat_ref.shape[0]
    lats = normed.shape[0]
    arrived(1)
    q[...] = mm(hat_ref[...] * gains_ref[0:1], wquery[...].reshape(wide, wide))
    arrived(0)

    def project(t, carry):
        at = pl.ds(pl.multiple_of(t * 256, 256), 256)
        kv[:, at] = mm(normed_ref[...], wkv[:, at])
        return carry

    lax.fori_loop(0, kv.shape[1] // 256, project, 0)
    mask = seg_ref[...] == crop_lanes(lats, lats)
    count = 128 // width * patches

    def forward(g, carry):
        at = pl.ds(pl.multiple_of(g * 128, 128), 128)
        behind = pl.ds(pl.multiple_of(wide + g * 128, 128), 128)
        found, shares = attend_group(q[:, at], kv[:, at], kv[:, behind], mask, width)
        att_ref[:, at] = found
        weights[pl.ds(pl.multiple_of(g * count, count), count)] = shares
        return carry

    lax.fori_loop(0, wide // 128, forward, 0)
    arrived(2)
    after = int_ref[...] + mm(att_ref[...], wout[...].reshape(wide, wide))
    after_hat, after_root = normalise(after)
    y_ref[...] = after_hat * gains_ref[1:2]
    new_ref[...] = after
    dy[...] = jnp.zeros_like(dy)
    arrived(3)
    arrived(4)
    tile = down.shape[1] * down.shape[2]

    def mlp(t, carry):
        at = pl.ds(pl.multiple_of(t * tile, tile), tile)
        up_part = up[:, :, at].reshape(wide, tile)
        down_part = down[t].reshape(tile, wide)
        pre = mm(y_ref[...], up_part)
        share = cdf(pre)
        act = pre * share
        act_ref[:, at] = act
        new_ref[...] += mm(act, down_part)
        slope = share + pre * DENSITY * jnp.exp(-0.5 * pre * pre)
        dpre = mmt(cot_ref[...], down_part) * slope
        dpre_ref[:, at] = dpre
        dy[...] += mmt(dpre, up_part)
        return carry

    lax.fori_loop(0, down.shape[0], mlp, 0)
    dgain_ref[...] = jnp.sum(dy[...] * after_hat, axis=0, keepdims=True)
    dafter_ref[...] = cot_ref[...] + norm_back(dy[...], after_hat, after_root, gains_ref[1:2])
    dy[...] = mmt(dafter_ref[...], wout[...].reshape(wide, wide))

    def backward(g, carry):
        at = pl.ds(pl.multiple_of(g * 128, 128), 128)
        behind = pl.ds(pl.multiple_of(wide + g * 128, 128), 128)
        shares = weights[pl.ds(pl.multiple_of(g * count, count), count)]
        found = attend_group_back(dy[:, at], q[:, at], kv[:, at], kv[:, behind], shares, width)
        dq_ref[:, at], dkv_ref[:, at], dkv_ref[:, behind] = found
        return carry

    lax.fori_loop(0, wide // 128, backward, 0)

    def close(t, carry):
        at = pl.ds(pl.multiple_of(t * 256, 256), 256)
        out_ref[:, at] = mmt(dkv_ref[...], wkv[at, :])
        return carry

    lax.fori_loop(0, out_ref.shape[1] // 256, close, 0)
    dhat_ref[...] = mmt(dq_ref[...], wquery[...].reshape(wide, wide))


def bring_pieces(sources, targets, sems, place):
    wkv, wquery, wout, up, down = targets
    zs, rows, wide = wquery.shape
    ds, _, inner, _ = down.shape
    pack = up.shape[2] // ds
    deep_rows, q_rows = wkv.shape[0] // ds, rows // ds
    lanes = wide // zs
    first = rows + inner * (wide // pack)
    for step in range(ds):
        d = jnp.bitwise_xor(place, step)
        base = (step % 2) * 5
        near = sources[base + min(step // 2, 3)]
        far, shift = (sources[base + 4], first) if step // 2 == 3 else (near, 0)

        def bring(source, target, sem):
            pltpu.make_async_copy(source, target, sems.at[sem]).start()

        at = first - shift
        for z in range(zs):
            for b in range(2):
                bring(
                    far.at[z, at : at + deep_rows, b * lanes : (b + 1) * lanes],
                    wkv.at[pl.ds(pl.multiple_of(d * deep_rows, deep_rows), deep_rows), pl.ds(b * wide + z * lanes, lanes)],
                    0,
                )
        at += deep_rows
        for n, target in ((1, wquery), (2, wout)):
            for b in range(wide // pack):
                bring(
                    far.at[:, at : at + q_rows],
                    target.at[:, pl.ds(pl.multiple_of(d * q_rows, q_rows), q_rows), pl.ds(b * pack, pack)],
                    n,
                )
                at += q_rows
        bring(near.at[:, :rows], up.at[:, :, pl.ds(pl.multiple_of(d * pack, pack), pack)], 3)
        for b in range(wide // pack):
            start = rows + b * inner
            bring(near.at[:, start : start + inner], down.at[d, :, :, pl.ds(b * pack, pack)], 4)


def write_stage(state, gain, hat, interface, cot, gains, seg, place, sources, shapes):
    rows, deep = state.shape
    patches, wide = hat.shape
    hidden = shapes[3][2]
    n = HEADS * patches
    small = shape_of(patches, wide)
    big = shape_of(patches, hidden)
    outs = [
        shape_of(rows, deep), small, small, small, small, small, big, big,
        shape_of(rows, 2 * wide), shape_of(1, wide), shape_of(rows, deep), small,
    ]
    vmem = pl.BlockSpec(memory_space=pltpu.VMEM)
    kernel = functools.partial(write_kernel, wide // HEADS)
    count = len(sources)

    def call(*refs):
        kernel(*refs[:8], refs[8 : 8 + count], *refs[8 + count :])

    return pl.pallas_call(
        call,
        out_shape=outs,
        in_specs=[vmem] * 7 + [pl.BlockSpec(memory_space=pltpu.SMEM)] + [pl.BlockSpec(memory_space=pl.ANY)] * count,
        out_specs=[vmem] * len(outs),
        scratch_shapes=[pltpu.VMEM(shape, jnp.float32) for shape in shapes]
        + [
            pltpu.VMEM((rows, 2 * wide), jnp.float32),
            pltpu.VMEM((patches, wide), jnp.float32),
            pltpu.VMEM((n, rows), jnp.float32),
            pltpu.VMEM((patches, wide), jnp.float32),
            pltpu.SemaphoreType.DMA((5,)),
        ],
        compiler_params=pltpu.CompilerParams(vmem_limit_bytes=VMEM_LIMIT),
        cost_estimate=pl.CostEstimate(flops=20_000_000_000, bytes_accessed=40_000_000, transcendentals=0),
    )(state, gain[None], hat, interface, cot, gains, seg, place, *sources)


def grads_kernel(y_ref, dpre_ref, act_ref, cot_ref, hat_ref, gain_ref, dq_ref, att_ref, dafter_ref, place_ref, mine_ref, other_ref, square):
    core = jnp.bitwise_and(place_ref[0], 1)
    wide = y_ref.shape[1]
    pack = mine_ref.shape[3]
    chips, zs = mine_ref.shape[0], mine_ref.shape[1]
    rows = wide // zs
    inner = pack // zs
    q_rows = rows // (2 * chips)
    square[0] = tmm(hat_ref[...] * gain_ref[...], dq_ref[...])
    square[1] = tmm(att_ref[...], dafter_ref[...])

    def step(j, carry):
        for out_ref, bit in ((mine_ref, core), (other_ref, 1 - core)):
            d = 2 * j + bit
            at = pl.ds(pl.multiple_of(d * pack, pack), pack)
            out_ref[j, :, :rows] = tmm(y_ref[...], dpre_ref[:, at]).reshape(zs, rows, pack)
            start = rows
            ddown = tmm(act_ref[:, at], cot_ref[...])
            for b in range(wide // pack):
                out_ref[j, :, start : start + inner] = ddown[:, b * pack : (b + 1) * pack].reshape(zs, inner, pack)
                start += inner
            for n in range(2):
                for b in range(wide // pack):
                    for z in range(zs):
                        source = pl.ds(pl.multiple_of(z * rows + d * q_rows, q_rows), q_rows)
                        out_ref[j, z, start : start + q_rows] = square[n, source, b * pack : (b + 1) * pack]
                    start += q_rows
        return carry

    lax.fori_loop(0, chips, step, 0)


def interface_grads(y, dpre, act, cot, hat, gain, dq, att, dafter, place, zs, rows):
    patches, wide = y.shape
    pack = dpre.shape[1] // 8
    out = shape_of(4, zs, rows, pack)
    vmem = pl.BlockSpec(memory_space=pltpu.VMEM)
    return pl.pallas_call(
        grads_kernel,
        out_shape=[out, out],
        in_specs=[vmem] * 9 + [pl.BlockSpec(memory_space=pltpu.SMEM)],
        out_specs=[vmem, vmem],
        scratch_shapes=[pltpu.VMEM((2, wide, wide), jnp.float32)],
        compiler_params=pltpu.CompilerParams(vmem_limit_bytes=VMEM_LIMIT),
        cost_estimate=pl.CostEstimate(flops=10_000_000_000, bytes_accessed=20_000_000, transcendentals=0),
    )(y, dpre, act, cot, hat, gain, dq, att, dafter, place)


def outer_kernel(specs, lefts, sums, place_ref, *refs):
    pieces, refs = refs[:10], refs[10:]
    arrays, refs = refs[:lefts], refs[lefts:]
    outs, refs = refs[: len(specs)], refs[len(specs) :]
    if sums:
        sum_ref, refs = refs[0], refs[1:]
    right, held, sems = refs[0], refs[1 : 1 + len(specs)], refs[1 + len(specs)]
    ds, rows, _ = right.shape
    for step in range(ds):
        d = jnp.bitwise_xor(place_ref[0], step)
        base, far = (step % 2) * 5, step // 2
        if far < 3:
            pltpu.make_async_copy(pieces[base + far], right.at[d], sems.at[0]).start()
        else:
            for n in range(2):
                target = right.at[d, n * rows // 2 : (n + 1) * rows // 2]
                pltpu.make_async_copy(pieces[base + 3 + n], target, sems.at[0]).start()
    copies = []
    for n, (which, at, width, _, _) in enumerate(specs):
        copies.append(pltpu.make_async_copy(arrays[which].at[:, at : at + width], held[n], sems.at[n + 1]))
        copies[-1].start()
    pltpu.make_async_copy(right, right, sems.at[0]).wait()
    if sums:
        sum_ref[...] = jnp.sum(right[:, :, sums[0] : sums[0] + sums[1]], axis=0)
    for n, (_, _, width, at, columns) in enumerate(specs):
        copies[n].wait()
        tile = min(256, width)

        def step(t, carry, n=n, at=at, columns=columns, tile=tile):
            here = pl.ds(pl.multiple_of(t * tile, tile), tile)
            values = right[:, :, at : at + columns].reshape(ds * rows, columns)
            outs[n][here, :] = tmm(held[n][:, here], values)
            return carry

        lax.fori_loop(0, width // tile, step, 0)


def outer_products(pieces, place, arrays, specs, sums=()):
    rows, columns = pieces[0].shape
    outs = [shape_of(spec[2], spec[4]) for spec in specs]
    if sums:
        outs.append(shape_of(rows, sums[1]))
    anywhere = pl.BlockSpec(memory_space=pl.ANY)
    total = arrays[0].shape[0]
    return pl.pallas_call(
        functools.partial(outer_kernel, specs, len(arrays), sums),
        out_shape=outs,
        in_specs=[pl.BlockSpec(memory_space=pltpu.SMEM)] + [anywhere] * (len(pieces) + len(arrays)),
        out_specs=[pl.BlockSpec(memory_space=pltpu.VMEM)] * len(outs),
        scratch_shapes=[pltpu.VMEM((total // rows, rows, columns), jnp.float32)]
        + [pltpu.VMEM((total, spec[2]), jnp.float32) for spec in specs]
        + [pltpu.SemaphoreType.DMA((len(specs) + 1,))],
        compiler_params=pltpu.CompilerParams(vmem_limit_bytes=VMEM_LIMIT),
        cost_estimate=pl.CostEstimate(
            flops=sum(6 * total * spec[2] * spec[4] for spec in specs), bytes_accessed=20_000_000, transcendentals=0
        ),
    )(place, *pieces, *arrays)


def local(
    interface,
    latents,
    segment_ids,
    read_gain_lat,
    read_gain_int,
    read_query,
    read_keyval,
    read_out,
    read_gain_mlp,
    read_up,
    read_down,
    layer_gain_att,
    layer_qkv,
    layer_out,
    layer_gain_mlp,
    layer_up,
    layer_down,
    write_gain_int,
    write_query,
    write_gain_lat,
    write_keyval,
    write_out,
    write_gain_mlp,
    write_up,
    write_down,
    interface_cot,
    latents_cot,
):
    zs, ds = lax.axis_size("head"), lax.axis_size("dp")
    me, dd = lax.axis_index("head"), lax.axis_index("dp")
    here = HEADS // zs

    def shift(values, step):
        return lax.ppermute(values, "head", [(i, (i + step) % zs) for i in range(zs)])

    def z_scatter(parts):
        total = lax.dynamic_index_in_dim(parts, me, 0, keepdims=False)
        for step in range(1, zs):
            sent = lax.dynamic_index_in_dim(parts, (me + step) % zs, 0, keepdims=False)
            total = total + shift(sent, step)
        return total

    def z_gather(own):
        out = jnp.zeros((zs,) + own.shape, own.dtype)
        out = lax.dynamic_update_index_in_dim(out, own, me, 0)
        for step in range(1, zs):
            out = lax.dynamic_update_index_in_dim(out, shift(own, step), (me - step) % zs, 0)
        return out

    def tie(*values):
        return lax.optimization_barrier(values)

    def sum_over_head(partial, base=None, release=()):
        rows = partial.shape[0] // zs
        own = z_scatter(partial.reshape(zs, rows, -1))
        if base is not None:
            own = own + lax.dynamic_slice_in_dim(base, me * rows, rows, 0)
        own, *release = tie(own, *release)
        full = z_gather(own).reshape(partial.shape)
        return (full, *release) if release else full

    def cut_up(full, parts):
        out, at = [], 0
        for part in parts:
            out.append(full[:, at : at + part.shape[1]])
            at += part.shape[1]
        return out

    def join(parts):
        return jnp.concatenate(parts, axis=1) if len(parts) > 1 else parts[0]

    def d_gather(parts):
        return lax.all_gather(join(parts), "dp", axis=0, tiled=True)

    direct = ds == 8
    chip, core = dd // 2, dd % 2

    def swap(values, bits):
        return lax.ppermute(values, "dp", [(i, i ^ bits) for i in range(ds)])

    def to_sides(joined):
        return [joined, swap(joined, 2), swap(joined, 4)]

    def to_across(joined, by_x, by_y):
        half = joined.shape[0] // 2
        return [joined, by_x, by_y, swap(by_x[:half], 4), swap(by_y[half:], 2)]

    def to_core(*blocks):
        return [*blocks, *(swap(block, 1) for block in blocks)]

    def pick(values, index, axis):
        return lax.dynamic_index_in_dim(values, index, axis, keepdims=False)

    def scatter_one(mine, got):
        x, rows = chip % 2, mine.shape[1]
        mine = mine.reshape((2, 2) + mine.shape[1:])
        got = got.reshape(mine.shape)
        y = chip // 2
        mh, gh, ml, gl = mine[:, :, : rows // 2], got[:, :, : rows // 2], mine[:, :, rows // 2 :], got[:, :, rows // 2 :]
        high, low = pick(mh, x, 1) + pick(gh, x, 1), pick(ml, y, 0) + pick(gl, y, 0)
        sent_high, sent_low = pick(mh, 1 - x, 1) + pick(gh, 1 - x, 1), pick(ml, 1 - y, 0) + pick(gl, 1 - y, 0)
        return high, low, swap(sent_high, 2), swap(sent_low, 4)

    def scatter_two(high, low, got_high, got_low):
        y, x = chip // 2, chip % 2
        sent_high, sent_low = pick(high, 1 - y, 0) + pick(got_high, 1 - y, 0), pick(low, 1 - x, 0) + pick(got_low, 1 - x, 0)
        high, low = pick(high, y, 0) + pick(got_high, y, 0), pick(low, x, 0) + pick(got_low, x, 0)
        return jnp.concatenate([high + swap(sent_high, 4), low + swap(sent_low, 2)], axis=0)

    def d_scatter(parts):
        parts = parts.reshape((4, 2) + parts.shape[1:])
        return scatter_two(*scatter_one(pick(parts, core, 1), swap(pick(parts, 1 - core, 1), 1)))

    interface, latents, segments = interface[0], latents[0], segment_ids[0]
    interface_cot, latents_cot = interface_cot[0], latents_cot[0]
    layer_gain_att, layer_gain_mlp = layer_gain_att[0], layer_gain_mlp[0]
    layer_out, layer_up, layer_down = layer_out[0], layer_up[0], layer_down[0]
    patches, wide = interface.shape
    count, deep = latents.shape
    qkv = layer_qkv[0].reshape(deep, -1)
    keyval = read_keyval.reshape(wide, -1)
    part = deep // zs
    hidden = write_down.shape[0] * zs

    own_segments = lax.dynamic_slice_in_dim(segments, me * patches, patches, 0)

    lat_hat, lat_root = normalise(latents)
    lat_normed = lat_hat * read_gain_lat
    early_all = d_gather([lat_normed])
    int_hat, int_root = normalise(interface)
    gains = jnp.stack([read_gain_int, write_gain_int, write_gain_mlp])
    gains = jnp.pad(gains, ((0, 5), (0, wide - gains.shape[1])))
    int_pack = z_gather(jnp.concatenate([int_hat, gains], axis=0))
    query = mm(lat_normed, read_query)

    wq_rows, up_cols, kv_rows = wide // zs // ds, hidden // ds, deep // ds
    pack = up_cols
    up_share = write_up.reshape(wide // zs, zs, ds, up_cols // zs)
    up_share = lax.dynamic_index_in_dim(up_share, dd, 2, keepdims=False).reshape(wide // zs, up_cols)
    down_share = lax.dynamic_index_in_dim(write_down.reshape(ds, -1, wide), dd, 0, keepdims=False)
    kv_share = lax.dynamic_slice_in_dim(write_keyval, dd * kv_rows, kv_rows, 0).reshape(kv_rows, -1)
    q_share = lax.dynamic_slice_in_dim(write_query, dd * wq_rows, wq_rows, 0)
    o_share = lax.dynamic_slice_in_dim(write_out, dd * wq_rows, wq_rows, 0)

    def narrow(share):
        return [share[:, at : at + pack] for at in range(0, share.shape[1], pack)]

    def widen(full, at, rows, columns):
        n = columns // pack
        return jnp.concatenate([full[:, :, at + i * rows : at + (i + 1) * rows] for i in range(n)], axis=-1)

    flat = jnp.concatenate(
        [up_share] + narrow(down_share) + narrow(kv_share) + narrow(q_share) + narrow(o_share), axis=0
    )
    query, int_pack, flat, early_all = lax.optimization_barrier((query, int_pack, flat, early_all))
    gains = jnp.transpose(int_pack[:, patches : patches + 3, : wide // zs], (1, 0, 2)).reshape(3, wide)
    gain_read, gain_write, gain_mlp = gains[0], gains[1], gains[2]
    shares = lax.all_gather(flat, "head", axis=0, tiled=False)

    kv0, read_attended, read_weights, part0 = run_whole(
        functools.partial(read_kernel, deep // HEADS),
        [
            shape_of(zs * patches, 2 * part),
            shape_of(count, part),
            shape_of(here * count, zs * patches),
            shape_of(count, deep),
        ],
        (query, int_pack, gain_read[None], segment_ids, keyval, read_out),
        flops=8 * zs * patches * wide * part,
    )

    state1 = sum_over_head(part0, latents)
    normed1, pre1, act1, part1 = ffn_forward(state1, read_gain_mlp, read_up, read_down)
    down_rows = hidden // zs // ds
    middle = wide // zs + down_rows * (wide // pack)
    part1, shares = tie(part1, shares)
    if direct:
        by_x, by_y = swap(shares, 2), swap(shares, 4)
    state2, read_attended, normed1, act1 = sum_over_head(part1, state1, (read_attended, normed1, act1))
    read_joined = join([read_attended, normed1, act1])

    normed2, packed, self_attended, self_weights, part2 = run_whole(
        functools.partial(self_kernel, deep // HEADS),
        [
            shape_of(count, deep),
            shape_of(count, 3 * part),
            shape_of(count, part),
            shape_of(here * count, count),
            shape_of(count, deep),
        ],
        (state2, layer_gain_att[None], qkv, layer_out),
        flops=8 * count * deep * part,
    )
    if direct:
        part2, by_x, by_y = tie(part2, by_x, by_y)
        pieces = [shares, by_x, by_y, swap(by_x[:, :middle], 4), swap(by_y[:, middle:], 2)]
    state3 = sum_over_head(part2, state2)
    normed3, pre3, act3, part3 = ffn_forward(state3, layer_gain_mlp, layer_up, layer_down)

    if direct:
        part3, read_joined, *pieces = tie(part3, read_joined, *pieces)
        pieces = pieces + [swap(piece, 1) for piece in pieces]
    else:
        everything = lax.all_gather(shares, "dp", axis=0, tiled=False)
        full_up = jnp.transpose(everything[:, :, : wide // zs], (1, 2, 0, 3)).reshape(zs, wide // zs, hidden)
        at = wide // zs
        full_down = widen(everything, at, down_rows, wide)
        at += down_rows * (wide // pack)
        full_kv = widen(everything, at, kv_rows, 2 * wide // zs)
        full_kv = jnp.transpose(full_kv.reshape(ds, zs, kv_rows, 2, -1), (0, 2, 3, 1, 4)).reshape(deep, 2 * wide)
        at += kv_rows * (2 * wide // zs // pack)
        full_query = jnp.transpose(widen(everything, at, wq_rows, wide), (1, 0, 2, 3)).reshape(zs, -1, wide)
        at += wq_rows * (wide // pack)
        full_out = jnp.transpose(widen(everything, at, wq_rows, wide), (1, 0, 2, 3)).reshape(zs, -1, wide)
        pieces = [full_kv, full_query, full_out, full_up, full_down]
    read_all = d_gather([read_joined])
    state4, normed2, self_attended, normed3, act3 = sum_over_head(
        part3, state3, (normed2, self_attended, normed3, act3)
    )
    layer_all = d_gather([normed2, self_attended, normed3, act3])

    (
        normed4, interface_new, dafter, dwrite_q, write_attended, after_normed, act5, dpre5, dkv4, dgain_mlp, part4,
        dwrite_normed,
    ) = write_stage(
        state4,
        write_gain_lat,
        int_hat,
        interface,
        interface_cot,
        jnp.stack([gain_write, gain_mlp]),
        own_segments[:, None],
        dd.astype(jnp.int32)[None],
        pieces,
        [
            (deep, 2 * wide),
            (zs, wide // zs, wide),
            (zs, wide // zs, wide),
            (zs, wide // zs, hidden),
            (ds, zs, down_rows, wide),
        ],
    )
    dsum4, after_normed, dpre5, act5, dwrite_q, write_attended, dafter, dkv4 = sum_over_head(
        part4, None, (after_normed, dpre5, act5, dwrite_q, write_attended, dafter, dkv4)
    )

    place = dd.astype(jnp.int32)[None]
    piece_rows = middle + 2 * wq_rows * (wide // pack)
    if direct:
        grads_mine, grads_other = interface_grads(
            after_normed, dpre5, act5, interface_cot, int_hat, gain_write[None], dwrite_q, write_attended, dafter,
            place, zs, piece_rows,
        )
        dsum4, grads_mine, grads_other = tie(dsum4, grads_mine, grads_other)
        grads_mine = grads_mine.reshape(4, -1, pack)
        grads_got = swap(grads_other.reshape(4, -1, pack), 1)
    else:
        write_normed = int_hat * gain_write
        dup = jnp.transpose(tmm(after_normed, dpre5).reshape(zs, wide // zs, ds, -1), (2, 0, 1, 3))

        def pack_grad(grad, rows):
            grad = grad.reshape(ds, zs, rows, wide)
            return [grad[..., at : at + pack] for at in range(0, wide, pack)]

        ddown = tmm(act5, interface_cot)
        dquery = jnp.transpose(tmm(write_normed, dwrite_q).reshape(zs, ds, wq_rows, wide), (1, 0, 2, 3))
        dout = jnp.transpose(tmm(write_attended, dafter).reshape(zs, ds, wq_rows, wide), (1, 0, 2, 3))
        packed_grads = jnp.concatenate(
            [dup] + pack_grad(ddown, down_rows) + pack_grad(dquery, wq_rows) + pack_grad(dout, wq_rows), axis=2
        )
        grads_mine = lax.psum_scatter(packed_grads, "dp", scatter_dimension=0, tiled=False)

    dint = dafter + norm_back(dwrite_normed, int_hat, int_root, gain_write)

    dkv_parts = jnp.transpose(dkv4.reshape(count, 2, zs, -1), (2, 0, 1, 3)).reshape(zs, count, -1)
    dsum4, dkv_parts = tie(dsum4, dkv_parts)
    dkv_mine = z_scatter(dkv_parts)
    dstate4, dgain4, dpre3, part5 = ffn_backward(
        latents_cot, dsum4, state4, write_gain_lat, pre3, layer_up, layer_down
    )
    if direct:
        part5, grads_mine, grads_got, dkv_mine = tie(part5, grads_mine, grads_got, dkv_mine)
        grads_mine = lax.psum_scatter(
            grads_mine + grads_got,
            "dp",
            scatter_dimension=0,
            axis_index_groups=[[2 * k + c for k in range(ds // 2)] for c in range(2)],
        )
    dsum3, normed4, dkv_mine, released4, dpre3 = sum_over_head(part5, None, (normed4, dkv_mine, dstate4, dpre3))
    write_all = d_gather([normed4, dkv_mine, released4, dpre3])
    dsum3, read_all = tie(dsum3, read_all)
    dstate3, dgain3, dpacked, part6 = run_whole(
        functools.partial(self_back_kernel, deep // HEADS),
        [shape_of(count, deep), shape_of(1, deep), shape_of(count, 3 * part), shape_of(count, deep)],
        (dstate4, dsum3, state3, layer_gain_mlp[None], packed, self_weights, qkv, layer_out),
        flops=8 * count * deep * part,
    )
    dsum2, released3, dpacked = sum_over_head(part6, None, (dstate3, dpacked))
    dsum2, layer_all = tie(dsum2, layer_all)

    dstate2, dgain2, dpre1, part7 = ffn_backward(
        dstate3, dsum2, state2, layer_gain_att, pre1, read_up, read_down
    )
    dsum1, released2, dpre1 = sum_over_head(part7, None, (dstate2, dpre1))
    both_all = d_gather([released3, dpacked, released2, dpre1])
    dsum1, grads_mine = tie(dsum1, grads_mine)
    grads_mine = z_scatter(grads_mine.reshape(zs, -1, pack))
    dstate1, dgain1, dquery0, dread_kv, dlat_part, dint_part, dgain_lat, dgain_int = run_whole(
        functools.partial(read_back_kernel, deep // HEADS),
        [
            shape_of(count, deep),
            shape_of(1, deep),
            shape_of(count, part),
            shape_of(zs * patches, 2 * part),
            shape_of(count, deep),
            shape_of(zs * patches, wide),
            shape_of(1, deep),
            shape_of(1, wide),
        ],
        (dstate2, dsum1, state1, read_gain_mlp[None], query, kv0, read_weights, read_query, keyval, read_out, latents, int_pack),
        flops=16 * zs * patches * wide * part,
    )
    dlat_part, dstate1, grads_mine = tie(dlat_part, dstate1, grads_mine)

    first = (me == 0).astype(jnp.float32)
    small = jnp.concatenate(
        [dgain_lat[0]]
        + [g[0] * first for g in (dgain1, dgain2, dgain3, dgain4)]
        + [dgain_int[0], jnp.sum(dwrite_normed * int_hat, axis=0), dgain_mlp[0]]
    )
    lanes = small.size // count
    fill = jnp.pad(small.reshape(count, lanes), ((0, 0), (0, -lanes % 128)))
    late = [join([dstate1, dquery0, fill])]

    dkeyval = tmm(int_pack[:, :patches].reshape(zs * patches, wide) * gain_read, dread_kv)
    half = z_scatter(dlat_part.reshape(zs, count // zs, deep))
    wide_lat = read_attended.shape[1]
    write_all = tie(write_all, dgain_int)[0]
    normed4_all, dkv_all, dstate4_all, dpre3_all = cut_up(write_all, [normed4, dkv_mine, dstate4, dpre3])
    normed2_all, self_att_all, normed3_all, act3_all = cut_up(layer_all, [normed2, self_attended, normed3, act3])
    grad_layer_up, grad_layer_down = tmm(normed3_all, dpre3_all), tmm(act3_all, dstate4_all)
    grad_write_keyval = tmm(normed4_all, dkv_all)
    if direct:
        late = to_sides(*late)
        dkeyval = dkeyval.reshape(4, 2, -1, 2 * part)
        pair = [pick(dkeyval, core, 1), swap(pick(dkeyval, 1 - core, 1), 1)]
        half, dint_part, grad_layer_up, grad_layer_down, grad_write_keyval, *held = tie(
            half, dint_part, grad_layer_up, grad_layer_down, grad_write_keyval, *late, *pair
        )
        late, pair = to_across(*held[:3]), scatter_one(*held[3:])
    dint_normed = z_scatter(dint_part.reshape(zs, patches, wide))
    dlat = z_gather(half).reshape(count, deep)
    if direct:
        dlat, dint_normed, both_all, *held = tie(dlat, dint_normed, both_all, *late, *pair)
        late, pair = held[:5], held[5:]
        late, dkeyval = to_core(*late), scatter_two(*pair)
        flat = jnp.concatenate([grads_mine] + [dkeyval[:, at : at + pack] for at in range(0, 2 * part, pack)], axis=0)
        grads_all = lax.all_gather(flat, "dp", axis=0, tiled=False)
        grad_read_keyval = widen(grads_all[:, None], piece_rows, dkeyval.shape[0], 2 * part)
    else:
        grads_all = lax.all_gather(grads_mine, "dp", axis=0, tiled=False)
        grad_read_keyval = lax.psum(dkeyval, "dp")
    dstate3_all, dpacked_all, dstate2_all, dpre1_all = cut_up(both_all, [dstate3, dpacked, dstate2, dpre1])
    grad_layer_qkv, grad_layer_out = tmm(normed2_all, dpacked_all), tmm(self_att_all, dstate3_all)
    read_att_all, normed1_all, act1_all = cut_up(read_all, [read_attended, normed1, act1])
    if direct:
        grad_read_query, grad_read_out, small = outer_products(
            late,
            place,
            [early_all, read_all],
            [(0, 0, deep, deep, part), (1, 0, part, 0, deep)],
            (deep + part, fill.shape[1]),
        )
        small = small[:, :lanes]
    else:
        late_all = d_gather(late)
        dstate1_all, dquery0_all, small = cut_up(late_all, [dstate1, dquery0, fill])
        grad_read_query, grad_read_out = tmm(early_all, dquery0_all), tmm(read_att_all, dstate1_all)
        small = jnp.sum(small.reshape(ds, count, -1)[:, :, :lanes], axis=0)
    grad_read_up, grad_read_down = tmm(normed1_all, dpre1_all), tmm(act1_all, dstate2_all)
    latents_grad = dstate1 + norm_back(dlat, lat_hat, lat_root, read_gain_lat)
    interface_grad = dint + norm_back(dint_normed, int_hat, int_root, gain_read)
    small = jnp.sum(z_gather(small), axis=0).reshape(-1)
    lat_gains = small[: 5 * deep].reshape(5, deep)
    int_gains = small[5 * deep :].reshape(3, zs, wide // zs)
    int_gains = lax.dynamic_index_in_dim(int_gains, me, 1, keepdims=False)

    full = grads_all[:, None]
    grad_write_up = grads_all[:, : wide // zs].reshape(ds, wide // zs, zs, up_cols // zs)
    grad_write_up = jnp.transpose(grad_write_up, (1, 2, 0, 3)).reshape(write_up.shape)
    at = wide // zs
    grad_write_down = widen(full, at, down_rows, wide).reshape(write_down.shape)
    at += down_rows * (wide // pack)
    grad_write_query = widen(full, at, wq_rows, wide).reshape(write_query.shape)
    at += wq_rows * (wide // pack)
    grad_write_out = widen(full, at, wq_rows, wide).reshape(write_out.shape)

    return (
        interface_new[None],
        state4[None],
        interface_grad[None],
        latents_grad[None],
        lat_gains[0],
        int_gains[0],
        grad_read_query,
        grad_read_keyval.reshape(read_keyval.shape),
        grad_read_out,
        lat_gains[1],
        grad_read_up,
        grad_read_down,
        lat_gains[2][None],
        grad_layer_qkv.reshape(layer_qkv.shape),
        grad_layer_out[None],
        lat_gains[3][None],
        grad_layer_up[None],
        grad_layer_down[None],
        int_gains[1],
        grad_write_query,
        lat_gains[4],
        grad_write_keyval.reshape(write_keyval.shape),
        grad_write_out,
        int_gains[2],
        grad_write_up,
        grad_write_down,
    )


def solution(mesh):
    rows, both = P("dp", "head", None), P("dp", None, None)
    weights = (
        P(),
        P("head"),
        P(None, "head"),
        P(None, None, "head"),
        P("head", None),
        P(),
        P(None, "head"),
        P("head", None),
        P(),
        P(None, None, None, "head"),
        P(None, "head", None),
        P(),
        P(None, None, "head"),
        P(None, "head", None),
        P("head"),
        P("head", None),
        P(),
        P(None, None, "head"),
        P("head", None),
        P("head"),
        P("head", None),
        P("head", None),
    )
    in_specs = (rows, both, P("dp", None)) + weights + (rows, both)
    out_specs = (rows, both, rows, both) + weights
    return jax.shard_map(local, mesh=mesh, in_specs=in_specs, out_specs=out_specs, check_vma=False)
```

time: 1040 us -> 723 us (0.70)
  waiting for transfers between devices: 449 us -> 227 us
  Pallas kernels: 0 us -> 134 us
  matrix products: 192 us -> 65.4 us
  local copies, waits for them, and re-layouts: 181 us -> 69.8 us
  starting transfers between devices: 73 us -> 151 us
  blocking collectives: 41 us -> 0 us
  other arithmetic: 66.9 us -> 49.1 us
    pallas_call x0 -> x11, Pallas kernels: none -> 134 us  [the longest x1 38.7 us: write_stage(): pl.pallas_call(call, out_shape=outs, in_specs=[vmem] * 7 + [pl.BlockSpec(...]
    ppermute x72 -> x69, waiting for transfers between devices: 334 us -> 214 us  [shift(): lax.ppermute(values, 'head', [(i, (i + step) % zs) for i in range(zs)])]
    all_gather x8 -> x7, waiting for transfers between devices: 97.5 us -> 9.35 us  [the longest x5 9.33 us: d_gather(): return lax.all_gather(join(parts), 'dp', axis=0, tiled=True)]
    dot_general x32 -> x0, matrix products: 65.8 us -> none  [the longest x14 38.2 us: mmt(): lax.dot_general(left, right, (((1,), (1,)), ((), ())), precision=PRECISE)]
    reshape x26 -> x4, local copies, waits for them, and re-layouts: 49.6 us -> 1.95 us  [the longest x1 1.49 us: local(): grad_write_keyval.reshape(write_keyval.shape)]
    ppermute x0 -> x24, starting transfers between devices: none -> 43.4 us  [swap(): return lax.ppermute(values, 'dp', [(i, i ^ bits) for i in range(ds)])]
    psum x1 -> x0, blocking collectives: 41 us -> none  [local(): small = lax.psum(small, ('dp', 'head'))]
    dot_general x14 -> x1, matrix products: 38.3 us -> 2.36 us  [mm(): lax.dot_general(left, right, (((1,), (0,)), ((), ())), precision=PRECISE)]
  transfers between devices with their start and end apart: 82 -> 101, of which waited for: 62 -> 51; matrix products, arithmetic and copies ran while one was open for 29% -> 21% of each run, Pallas kernels for 0% -> 19%
where the time goes in v2:
time: 723 us; the launch traced here: 712 us
  waiting for transfers between devices  227 us (31%)
  starting transfers between devices  151 us (21%)
  Pallas kernels  134 us (19%)
  local copies, waits for them, and re-layouts  69.8 us (10%)
  matrix products  65.4 us (9%)
  other arithmetic  49.1 us (7%)
  between operations  16.3 us (2%)
    ppermute x69, waiting for transfers between devices, shift(): lax.ppermute(values, 'head', [(i, (i + step) % zs) for i in range(zs)])  214 us
    ppermute x69, starting transfers between devices, shift(): lax.ppermute(values, 'head', [(i, (i + step) % zs) for i in range(zs)])  107 us
    dot_general x8, matrix products, tmm(): lax.dot_general(left, right, (((0,), (0,)), ((), ())), precision=PRECISE)  63 us
    ppermute x24, starting transfers between devices, swap(): return lax.ppermute(values, 'dp', [(i, i ^ bits) for i in range(ds)])  43.4 us
    pallas_call x1, Pallas kernels, write_stage(): pl.pallas_call(call, out_shape=outs, in_specs=[vmem] * 7 + [pl.BlockSpec(...  38.7 us
    pallas_call x4, Pallas kernels, run_whole(): pl.pallas_call(kernel, out_shape=outs, in_specs=[pl.BlockSpec(memory_spac...  35.3 us
    unnamed x149, local copies, waits for them, and re-layouts  22.8 us
    pallas_call x2, Pallas kernels, ffn_backward(): pl.pallas_call(ffn_back_kernel, grid=(inner // tile,), out_shape=[shape_o...  22.8 us
  transfers between devices with their start and end apart: 101, of which 51 were waited for; matrix products, arithmetic and copies ran while one was open for 21% of the time, Pallas kernels for 19%

profile of v2, /device:TPU:13, one launch (start us, length us, event | category | flops | bytes accessed | tf_op | source)
XLA Modules:
  0.0 712.4 jit_solution(15822665864863275195)
XLA Ops:
  29.5 32.8 %collective-permute-done.1 = f32[264,512]{1,0:T(8,128)} collective-permute-done((f32[264,512]{1,0:T(8,128)}, f32[264,512]{1,0:T(8,128)}, u32[]{:S(2)}, u32[]{:S(2)}) %collective-permute-start.1) | collective-permute-done | bytes 540704 | tf_op jit(solution)/shard_map/ppermute | solution.py:653
  70.4 8.6 %shard_map.458 = (f32[1024,512]{1,0:T(8,128)}, f32[128,256]{1,0:T(8,128)}, f32[512,1024]{1,0:T(8,128)}, f32[128,1024]{1,0:T(8,128)}) custom-call(f32[128,256]{1,0:T(8,128)} %fusion.71.q_ref, f32[4,264,512]{2,1,0:T(8,128)} %copy-done.5, f32[1,512]{1,0:T(1,128)} %get-tuple-element.481.gain_ref, s32[1,1024]{1,0:T(1,128)} %seg_ref.1, f32[512,512]{1,0:T(8,128)} %bitcast.447, ...), custom_call_target="tpu_custom_call" | custom-call | flops 3221225472 | bytes 9246720 | tf_op jit(solution)/shard_map/pallas_call | solution.py:61
  83.8 10.9 %collective-permute-done.5 = f32[32,1024]{1,0:T(8,128)S(1)} collective-permute-done((f32[32,1024]{1,0:T(8,128)S(1)}, f32[32,1024]{1,0:T(8,128)S(1)}, u32[]{:S(2)}, u32[]{:S(2)}) %collective-permute-start.5) | collective-permute-done | bytes 131104 | tf_op jit(solution)/shard_map/ppermute | solution.py:653
  94.6 2.5 collective-permute-done.4
  97.2 8.5 %collective-permute-done.3 = f32[32,1024]{1,0:T(8,128)S(1)} collective-permute-done((f32[32,1024]{1,0:T(8,128)S(1)}, f32[32,1024]{1,0:T(8,128)S(1)}, u32[]{:S(2)}, u32[]{:S(2)}) %collective-permute-start.3) | collective-permute-done | bytes 131104 | tf_op jit(solution)/shard_map/ppermute | solution.py:653
  106.7 3.8 collective-permute-start.6
  112.4 7.4 %collective-permute-done.6 = f32[32,1024]{1,0:T(8,128)S(1)} collective-permute-done((f32[32,1024]{1,0:T(8,128)S(1)}, f32[32,1024]{1,0:T(8,128)S(1)}, u32[]{:S(2)}, u32[]{:S(2)}) %collective-permute-start.6) | collective-permute-done | bytes 131104 | tf_op jit(solution)/shard_map/ppermute | solution.py:653
  119.8 9.0 %collective-permute-done.7 = f32[32,1024]{1,0:T(8,128)S(1)} collective-permute-done((f32[32,1024]{1,0:T(8,128)S(1)}, f32[32,1024]{1,0:T(8,128)S(1)}, u32[]{:S(2)}, u32[]{:S(2)}) %collective-permute-start.7) | collective-permute-done | bytes 131104 | tf_op jit(solution)/shard_map/ppermute | solution.py:653
  128.9 2.4 collective-permute-done.8
  132.1 7.6 %shard_map.459 = (f32[128,1024]{1,0:T(8,128)}, f32[128,1024]{1,0:T(8,128)}, f32[128,1024]{1,0:T(8,128)}, f32[128,1024]{1,0:T(8,128)}) custom-call(f32[128,1024]{1,0:T(8,128)} %bitcast.430, f32[1,1024]{1,0:T(1,128)} %bitcast.489, f32[1024,1024]{1,0:T(8,128)} %up_ref.3, f32[1024,1024]{1,0:T(8,128)} %down_ref.3), custom_call_target="tpu_custom_call" | custom-call | flops 1610612736 | bytes 8388608 | tf_op jit(solution)/shard_map/pallas_call | solution.py:142
  146.1 2.4 copy.100
  150.9 3.8 collective-permute-done.9
  160.3 12.1 %collective-permute-start.14 = (f32[32,1024]{1,0:T(8,128)S(1)}, f32[32,1024]{1,0:T(8,128)S(1)}, u32[]{:S(2)}, u32[]{:S(2)}) collective-permute-start(f32[32,1024]{1,0:T(8,128)S(1)} %fusion.54), channel_id=1, source_target_pairs={{0,3},{1,0},{2,1},{3,2},{4,7},{5,4},{6,5},{7,6},{8,11},{9,8},{10,9... | collective-permute-start | bytes 393224 | tf_op jit(solution)/shard_map/ppermute | solution.py:653
  172.5 4.0 collective-permute-done.14
  177.4 5.4 shard_map.460
  193.1 3.2 collective-permute-done.17
  201.8 8.1 %collective-permute-done.21 = f32[32,1024]{1,0:T(8,128)S(1)} collective-permute-done((f32[32,1024]{1,0:T(8,128)S(1)}, f32[32,1024]{1,0:T(8,128)S(1)}, u32[]{:S(2)}, u32[]{:S(2)}) %collective-permute-start.21) | collective-permute-done | bytes 131104 | tf_op jit(solution)/shard_map/ppermute | solution.py:653
  212.8 7.7 %shard_map.461 = (f32[128,1024]{1,0:T(8,128)}, f32[128,1024]{1,0:T(8,128)}, f32[128,1024]{1,0:T(8,128)}, f32[128,1024]{1,0:T(8,128)}) custom-call(f32[128,1024]{1,0:T(8,128)} %bitcast.414, f32[1,1024]{1,0:T(1,128)} %gain_ref.6, f32[1024,1024]{1,0:T(8,128)} %bitcast.401, f32[1024,1024]{1,0:T(8,128)} %bitcast.403), custom_call_target="tpu_custom_call" | custom-call | flops 1610612736 | bytes 8388608 | tf_op jit(solution)/shard_map/pallas_call | solution.py:142
  225.3 2.5 collective-permute-done.27
  228.8 5.0 collective-permute-done.25
  234.8 2.6 pad_maximum_fusion.1
  241.7 2.4 collective-permute-start.29
  246.7 3.8 collective-permute-done.29
  250.6 3.0 collective-permute-start.30
  260.1 38.7 %shard_map.462 = (f32[128,1024]{1,0:T(8,128)}, f32[256,512]{1,0:T(8,128)}, f32[256,512]{1,0:T(8,128)}, f32[256,512]{1,0:T(8,128)}, f32[256,512]{1,0:T(8,128)}, /...) custom-call(f32[128,1024]{1,0:T(8,128)} %bitcast.433, ...), custom_call_target="tpu_custom_call" | custom-call | flops 20000000000 | bytes 40000000 | tf_op jit(solution)/shard_map/pallas_call | solution.py:494
  306.4 5.8 collective-permute-done.37
  312.2 3.0 collective-permute-done.36
  319.8 12.4 %shard_map.463 = (f32[4,4,320,256]{3,2,1,0:T(8,128)}, f32[4,4,320,256]{3,2,1,0:T(8,128)}) custom-call(f32[256,512]{1,0:T(8,128)} %get-tuple-element.207.y_ref, f32[256,2048]{1,0:T(8,128)} %get-tuple-element.208.dpre_ref, f32[256,2048]{1,0:T(8,128)} %get-tuple-element.209.act_ref, f32[256,512]{1,0:T(8,128)} %bitcast.505, f32[256,512]{1,0:T(8,128)} %copy-done.10, ...), custom_call_target="tpu_custom_call" | custom-call | flops 10000000000 | bytes 20000000 | tf_op jit(solution)/shard_map/pallas_call | solution.py:549
  335.1 3.1 collective-permute-start.45
  339.5 11.4 %shard_map.464 = (f32[128,1024]{1,0:T(8,128)}, f32[1,1024]{1,0:T(1,128)}, f32[128,1024]{1,0:T(8,128)}, f32[128,1024]{1,0:T(8,128)}) custom-call(f32[128,1024]{1,0:T(8,128)} %bitcast.451, f32[128,1024]{1,0:T(8,128)} %bitcast.436, f32[128,1024]{1,0:T(8,128)} %bitcast.434, f32[1,1024]{1,0:T(1,128)} %bitcast.488, f32[128,1024]{1,0:T(8,128)} %get-tuple-element.217.pre_ref, ...), custom_call_target="tpu_custom_call" | custom-call | flops 1610612736 | bytes 8388608 | tf_op jit(solution)/shard_map/pallas_call | solution.py:185
  351.0 5.5 add.581
  362.0 6.6 collective-permute-done.47
  368.7 2.8 collective-permute-done.46
  378.3 7.9 %collective-permute-done.50 = f32[32,1024]{1,0:T(8,128)S(1)} collective-permute-done((f32[32,1024]{1,0:T(8,128)S(1)}, f32[32,1024]{1,0:T(8,128)S(1)}, u32[]{:S(2)}, u32[]{:S(2)}) %collective-permute-start.50) | collective-permute-done | bytes 131104 | tf_op jit(solution)/shard_map/ppermute | solution.py:653
  388.8 7.7 %shard_map.465 = (f32[128,1024]{1,0:T(8,128)}, f32[1,1024]{1,0:T(1,128)}, f32[128,768]{1,0:T(8,128)}, f32[128,1024]{1,0:T(8,128)}) custom-call(f32[128,1024]{1,0:T(8,128)} %get-tuple-element.259.base_ref, f32[128,1024]{1,0:T(8,128)} %bitcast.442, f32[128,1024]{1,0:T(8,128)} %bitcast.416, f32[1,1024]{1,0:T(1,128)} %gain_ref.6, ...), custom_call_target="tpu_custom_call" | custom-call | flops 805306368 | bytes 7872512 | tf_op jit(solution)/shard_map/pallas_call | solution.py:61
  402.8 3.1 collective-permute-done.53
  405.8 4.0 collective-permute-done.52
  415.6 7.9 %collective-permute-done.56 = f32[32,1024]{1,0:T(8,128)S(1)} collective-permute-done((f32[32,1024]{1,0:T(8,128)S(1)}, f32[32,1024]{1,0:T(8,128)S(1)}, u32[]{:S(2)}, u32[]{:S(2)}) %collective-permute-start.56) | collective-permute-done | bytes 131104 | tf_op jit(solution)/shard_map/ppermute | solution.py:653
  426.4 11.4 %shard_map.466 = (f32[128,1024]{1,0:T(8,128)}, f32[1,1024]{1,0:T(1,128)}, f32[128,1024]{1,0:T(8,128)}, f32[128,1024]{1,0:T(8,128)}) custom-call(f32[128,1024]{1,0:T(8,128)} %get-tuple-element.274.base_ref, f32[128,1024]{1,0:T(8,128)} %bitcast.437, f32[128,1024]{1,0:T(8,128)} %bitcast.413, f32[1,1024]{1,0:T(1,128)} %gain_ref.7, ...), custom_call_target="tpu_custom_call" | custom-call | flops 1610612736 | bytes 8388608 | tf_op jit(solution)/shard_map/pallas_call | solution.py:185
  442.0 2.5 collective-permute-done.60
  445.5 5.0 collective-permute-done.58
  451.5 2.8 pad_maximum_fusion
  463.7 7.7 %collective-permute-done.62 = f32[32,1024]{1,0:T(8,128)S(1)} collective-permute-done((f32[32,1024]{1,0:T(8,128)S(1)}, f32[32,1024]{1,0:T(8,128)S(1)}, u32[]{:S(2)}, u32[]{:S(2)}) %collective-permute-start.62) | collective-permute-done | bytes 131104 | tf_op jit(solution)/shard_map/ppermute | solution.py:653
  477.0 2.5 collective-permute-start.64
  479.5 13.7 %shard_map.467 = (f32[128,1024]{1,0:T(8,128)}, f32[1,1024]{1,0:T(1,128)}, f32[128,256]{1,0:T(8,128)}, f32[1024,512]{1,0:T(8,128)}, f32[128,1024]{1,0:T(8,128)}, ...) custom-call(f32[128,1024]{1,0:T(8,128)} %get-tuple-element.276.base_ref, f32[128,1024]{1,0:T(8,128)} %bitcast.454, ...), custom_call_target="tpu_custom_call" | custom-call | flops 6442450944 | bytes 17119232 | tf_op jit(solution)/shard_map/pallas_call | solution.py:61
  495.4 3.4 fusion.19
  513.2 3.7 collective-permute-done.68
  516.9 2.8 collective-permute-done.67
  520.4 11.2 %fusion.15 = f32[1024,1024]{1,0:T(8,128)} fusion(f32[1024,3328]{1,0:T(8,128)} %all-gather.16.cloned.1.call-done, f32[1024,3328]{1,0:T(8,128)} %all-gather.14.cloned.1.call-done), kind=kOutput, calls=%fused_computation.15 | convolution fusion | flops 6442450944 | bytes 12582912 | tf_op jit(solution)/shard_map/dot_general | solution.py:28
  531.6 10.0 %fusion.12 = f32[1024,1024]{1,0:T(8,128)} fusion(f32[1024,3328]{1,0:T(8,128)S(1)} %copy-done.23, f32[1024,3328]{1,0:T(8,128)} %all-gather.14.cloned.1.call-done), kind=kOutput, calls=%fused_computation.12 | convolution fusion | flops 6442450944 | bytes 12582912 | tf_op jit(solution)/shard_map/dot_general | solution.py:28
  541.7 3.5 fusion.10
  558.5 20.2 %collective-permute-start.79 = (f32[64,1408]{1,0:T(8,128)S(1)}, f32[64,1408]{1,0:T(8,128)S(1)}, u32[]{:S(2)}, u32[]{:S(2)}) collective-permute-start(f32[64,1408]{1,0:T(8,128)S(1)} %slice.214), channel_id=1, source_target_pairs={{0,16},{4,20},{8,24},{12,28},{16,0},{20,4},{24,8},{28,12},{1,17},{... | collective-permute-start | bytes 1081352 | tf_op jit(solution)/shard_map/ppermute | solution.py:698
  580.3 11.0 %collective-permute-done.77 = f32[256,512]{1,0:T(8,128)S(1)} collective-permute-done((f32[256,512]{1,0:T(8,128)S(1)}, f32[256,512]{1,0:T(8,128)S(1)}, u32[]{:S(2)}, u32[]{:S(2)}) %collective-permute-start.77) | collective-permute-done | bytes 524320 | tf_op jit(solution)/shard_map/ppermute | solution.py:653
  593.5 9.0 %collective-permute-done.76 = f32[256,512]{1,0:T(8,128)S(1)} collective-permute-done((f32[256,512]{1,0:T(8,128)S(1)}, f32[256,512]{1,0:T(8,128)S(1)}, u32[]{:S(2)}, u32[]{:S(2)}) %collective-permute-start.76) | collective-permute-done | bytes 524320 | tf_op jit(solution)/shard_map/ppermute | solution.py:653
  604.2 9.3 %all-gather.18.cloned.1.call-done = f32[1024,3840]{1,0:T(8,128)} async-done(((f32[128,3840]{1,0:T(8,128)}), f32[1024,3840]{1,0:T(8,128)}) %all-gather.18.cloned.1.call-update) | async-done | bytes 15728656 | tf_op jit(solution)/shard_map/all_gather | solution.py:692
  627.7 2.5 add_bitcast_fusion.1
  630.2 9.6 %fusion.2 = f32[1024,768]{0,1:T(8,128)} fusion(f32[1024,3328]{1,0:T(8,128)} %all-gather.14.cloned.1.call-done, f32[1024,3840]{1,0:T(8,128)} %all-gather.18.cloned.1.call-done), kind=kOutput, calls=%fused_computation.2 | convolution fusion | flops 4831838208 | bytes 10485760 | tf_op jit(solution)/shard_map/dot_general | solution.py:28
  639.8 9.9 %fusion.7 = f32[1024,1024]{1,0:T(8,128)} fusion(f32[1024,3840]{1,0:T(8,128)} %all-gather.18.cloned.1.call-done, f32[1024,2304]{1,0:T(8,128)S(1)} %bitcast.408), kind=kOutput, calls=%fused_computation.7 | convolution fusion | flops 6442450944 | bytes 12582912 | tf_op jit(solution)/shard_map/dot_general | solution.py:28
  649.7 10.0 %fusion.4 = f32[1024,1024]{1,0:T(8,128)} fusion(f32[1024,3840]{1,0:T(8,128)} %all-gather.18.cloned.1.call-done, f32[1024,2304]{1,0:T(8,128)S(1)} %bitcast.408), kind=kOutput, calls=%fused_computation.4 | convolution fusion | flops 6442450944 | bytes 12582912 | tf_op jit(solution)/shard_map/dot_general | solution.py:28
  660.7 3.7 copy.110
  664.4 5.4 fusion.21
  670.9 9.9 %shard_map.468 = (f32[1024,256]{1,0:T(8,128)}, f32[256,1024]{1,0:T(8,128)}, f32[128,128]{1,0:T(8,128)}) custom-call(s32[1]{0:T(128)} %bitcast.68.refs_7_.place_ref, f32[128,1408]{1,0:T(8,128)} %copy-done.11, f32[128,1408]{1,0:T(8,128)} %collective-permute-done.70.refs_1_, f32[128,1408]{1,0:T(8,128)} %collective-permute-done.71.refs_2_, ...), custom_call_target="tpu_custom_call" | custom-call | flops 3221225472 | bytes 20000000 | tf_op jit(solution)/shard_map/pallas_call | solution.py:604
  686.4 3.6 collective-permute-done.90
  691.4 2.7 fusion.62
  (483 shorter events, 229.8 us)
Async XLA Ops:
  7.3 59.0 %all-gather.10.cloned.1.call-start = ((), (), s32[]{:S(2)}) async-start(), calls=%async_computation.1 | async-start | bytes 4718592 | tf_op jit(solution)/shard_map/all_gather | solution.py:692
  12.4 127.4 %all-gather.20.cloned.1.call-start = ((), (), s32[]{:S(2)}) async-start(), calls=%async_computation.6 | async-start | bytes 2293760 | tf_op jit(solution)/shard_map/all_gather | solution.py:777
  15.0 13.5 %collective-permute-start = (f32[264,512]{1,0:T(8,128)}, f32[264,512]{1,0:T(8,128)}, u32[]{:S(2)}, u32[]{:S(2)}) collective-permute-start(f32[264,512]{1,0:T(8,128)} %pad_maximum_fusion.6), channel_id=1, source_target_pairs={{0,1},{1,2},{2,3},{3,0},{4,5},{5,6},{6,7},{7,4},{8,9},{9,10},{10,1... | collective-permute-start | bytes 1622024 | tf_op jit(solution)/shard_map/ppermute | solution.py:653
  16.3 46.0 %collective-permute-start.1 = (f32[264,512]{1,0:T(8,128)}, f32[264,512]{1,0:T(8,128)}, u32[]{:S(2)}, u32[]{:S(2)}) collective-permute-start(f32[264,512]{1,0:T(8,128)} %pad_maximum_fusion.6), channel_id=1, source_target_pairs={{0,2},{1,3},{2,0},{3,1},{4,6},{5,7},{6,4},{7,5},{8,10},{9,11},{10,... | collective-permute-start | bytes 1622024 | tf_op jit(solution)/shard_map/ppermute | solution.py:653
  17.3 47.8 %collective-permute-start.2 = (f32[264,512]{1,0:T(8,128)}, f32[264,512]{1,0:T(8,128)}, u32[]{:S(2)}, u32[]{:S(2)}) collective-permute-start(f32[264,512]{1,0:T(8,128)} %pad_maximum_fusion.6), channel_id=1, source_target_pairs={{0,3},{1,0},{2,1},{3,2},{4,7},{5,4},{6,5},{7,6},{8,11},{9,8},{10,9... | collective-permute-start | bytes 1622024 | tf_op jit(solution)/shard_map/ppermute | solution.py:653
  67.4 320.6 %all-gather.12.cloned.1.call-start = ((), (), s32[]{:S(2)}) async-start(), calls=%async_computation.2 | async-start | bytes 10616832 | tf_op jit(solution)/shard_map/all_gather | solution.py:692
  80.0 14.6 %collective-permute-start.5 = (f32[32,1024]{1,0:T(8,128)S(1)}, f32[32,1024]{1,0:T(8,128)S(1)}, u32[]{:S(2)}, u32[]{:S(2)}) collective-permute-start(f32[32,1024]{1,0:T(8,128)S(1)} %get-tuple-element.467), channel_id=1, source_target_pairs={{0,3},{1,0},{2,1},{3,2},{4,7},{5,4},{6,5},{7,6},{8,11},{9,8},{10,9... | collective-permute-start | bytes 393224 | tf_op jit(solution)/shard_map/ppermute | solution.py:653
  80.1 17.1 %collective-permute-start.4 = (f32[32,1024]{1,0:T(8,128)S(1)}, f32[32,1024]{1,0:T(8,128)S(1)}, u32[]{:S(2)}, u32[]{:S(2)}) collective-permute-start(f32[32,1024]{1,0:T(8,128)S(1)} %get-tuple-element.468), channel_id=1, source_target_pairs={{0,2},{1,3},{2,0},{3,1},{4,6},{5,7},{6,4},{7,5},{8,10},{9,11},{10,... | collective-permute-start | bytes 393224 | tf_op jit(solution)/shard_map/ppermute | solution.py:653
  81.5 24.2 %collective-permute-start.3 = (f32[32,1024]{1,0:T(8,128)S(1)}, f32[32,1024]{1,0:T(8,128)S(1)}, u32[]{:S(2)}, u32[]{:S(2)}) collective-permute-start(f32[32,1024]{1,0:T(8,128)S(1)} %get-tuple-element.466), channel_id=1, source_target_pairs={{0,1},{1,2},{2,3},{3,0},{4,5},{5,6},{6,7},{7,4},{8,9},{9,10},{10,1... | collective-permute-start | bytes 393224 | tf_op jit(solution)/shard_map/ppermute | solution.py:653
  106.7 13.2 %collective-permute-start.6 = (f32[32,1024]{1,0:T(8,128)S(1)}, f32[32,1024]{1,0:T(8,128)S(1)}, u32[]{:S(2)}, u32[]{:S(2)}) collective-permute-start(f32[32,1024]{1,0:T(8,128)S(1)} %bitcast_add_fusion.13), channel_id=1, source_target_pairs={{0,1},{1,2},{2,3},{3,0},{4,5},{5,6},{6,7},{7,4},{8,9},{9,10},{10,1... | collective-permute-start | bytes 393224 | tf_op jit(solution)/shard_map/ppermute | solution.py:653
  110.5 18.3 %collective-permute-start.7 = (f32[32,1024]{1,0:T(8,128)S(1)}, f32[32,1024]{1,0:T(8,128)S(1)}, u32[]{:S(2)}, u32[]{:S(2)}) collective-permute-start(f32[32,1024]{1,0:T(8,128)S(1)} %bitcast_add_fusion.13), channel_id=1, source_target_pairs={{0,2},{1,3},{2,0},{3,1},{4,6},{5,7},{6,4},{7,5},{8,10},{9,11},{10,... | collective-permute-start | bytes 393224 | tf_op jit(solution)/shard_map/ppermute | solution.py:653
  112.4 18.9 %collective-permute-start.8 = (f32[32,1024]{1,0:T(8,128)S(1)}, f32[32,1024]{1,0:T(8,128)S(1)}, u32[]{:S(2)}, u32[]{:S(2)}) collective-permute-start(f32[32,1024]{1,0:T(8,128)S(1)} %bitcast_add_fusion.13), channel_id=1, source_target_pairs={{0,3},{1,0},{2,1},{3,2},{4,7},{5,4},{6,5},{7,6},{8,11},{9,8},{10,9... | collective-permute-start | bytes 393224 | tf_op jit(solution)/shard_map/ppermute | solution.py:653
  139.8 43.0 %collective-permute-start.15 = (f32[4,448,256]{2,1,0:T(8,128)}, f32[4,448,256]{2,1,0:T(8,128)}, u32[]{:S(2)}, u32[]{:S(2)}) collective-permute-start(f32[4,448,256]{2,1,0:T(8,128)} %bitcast.500), channel_id=1, source_target_pairs={{0,8},{4,12},{8,0},{12,4},{16,24},{20,28},{24,16},{28,20},{1,9},{5... | collective-permute-start | bytes 5505032 | tf_op jit(solution)/shard_map/ppermute | solution.py:698
  141.0 41.8 %collective-permute-start.16 = (f32[4,448,256]{2,1,0:T(8,128)}, f32[4,448,256]{2,1,0:T(8,128)}, u32[]{:S(2)}, u32[]{:S(2)}) collective-permute-start(f32[4,448,256]{2,1,0:T(8,128)} %bitcast.501), channel_id=1, source_target_pairs={{0,16},{4,20},{8,24},{12,28},{16,0},{20,4},{24,8},{28,12},{1,17},{... | collective-permute-start | bytes 5505032 | tf_op jit(solution)/shard_map/ppermute | solution.py:698
  143.8 10.9 %collective-permute-start.9 = (f32[32,1024]{1,0:T(8,128)S(1)}, f32[32,1024]{1,0:T(8,128)}, u32[]{:S(2)}, u32[]{:S(2)}) collective-permute-start(f32[32,1024]{1,0:T(8,128)S(1)} %get-tuple-element.463), channel_id=1, source_target_pairs={{0,1},{1,2},{2,3},{3,0},{4,5},{5,6},{6,7},{7,4},{8,9},{9,10},{10,1... | collective-permute-start | bytes 393224 | tf_op jit(solution)/shard_map/ppermute | solution.py:653
  155.7 16.7 %collective-permute-start.12 = (f32[32,1024]{1,0:T(8,128)S(1)}, f32[32,1024]{1,0:T(8,128)S(1)}, u32[]{:S(2)}, u32[]{:S(2)}) collective-permute-start(f32[32,1024]{1,0:T(8,128)S(1)} %fusion.54), channel_id=1, source_target_pairs={{0,1},{1,2},{2,3},{3,0},{4,5},{5,6},{6,7},{7,4},{8,9},{9,10},{10,1... | collective-permute-start | bytes 393224 | tf_op jit(solution)/shard_map/ppermute | solution.py:653
  158.1 14.4 %collective-permute-start.13 = (f32[32,1024]{1,0:T(8,128)S(1)}, f32[32,1024]{1,0:T(8,128)S(1)}, u32[]{:S(2)}, u32[]{:S(2)}) collective-permute-start(f32[32,1024]{1,0:T(8,128)S(1)} %fusion.54), channel_id=1, source_target_pairs={{0,2},{1,3},{2,0},{3,1},{4,6},{5,7},{6,4},{7,5},{8,10},{9,11},{10,... | collective-permute-start | bytes 393224 | tf_op jit(solution)/shard_map/ppermute | solution.py:653
  160.3 16.3 %collective-permute-start.14 = (f32[32,1024]{1,0:T(8,128)S(1)}, f32[32,1024]{1,0:T(8,128)S(1)}, u32[]{:S(2)}, u32[]{:S(2)}) collective-permute-start(f32[32,1024]{1,0:T(8,128)S(1)} %fusion.54), channel_id=1, source_target_pairs={{0,3},{1,0},{2,1},{3,2},{4,7},{5,4},{6,5},{7,6},{8,11},{9,8},{10,9... | collective-permute-start | bytes 393224 | tf_op jit(solution)/shard_map/ppermute | solution.py:653
  190.3 30.2 %collective-permute-start.23 = (f32[4,256,256]{2,1,0:T(8,128)S(1)}, f32[4,256,256]{2,1,0:T(8,128)S(1)}, u32[]{:S(2)}, u32[]{:S(2)}) collective-permute-start(f32[4,256,256]{2,1,0:T(8,128)S(1)} %slice.201), channel_id=1, source_target_pairs={{0,16},{4,20},{8,24},{12,28},{16,0},{20,4},{24,8},{28,12},{1,17},{... | collective-permute-start | bytes 3145736 | tf_op jit(solution)/shard_map/ppermute | solution.py:698
  192.8 27.7 %collective-permute-start.24 = (f32[4,192,256]{2,1,0:T(8,128)S(1)}, f32[4,192,256]{2,1,0:T(8,128)S(1)}, u32[]{:S(2)}, u32[]{:S(2)}) collective-permute-start(f32[4,192,256]{2,1,0:T(8,128)S(1)} %slice.202), channel_id=1, source_target_pairs={{0,8},{4,12},{8,0},{12,4},{16,24},{20,28},{24,16},{28,20},{1,9},{5... | collective-permute-start | bytes 2359304 | tf_op jit(solution)/shard_map/ppermute | solution.py:698
  200.1 11.8 %collective-permute-start.22 = (f32[32,1024]{1,0:T(8,128)S(1)}, f32[32,1024]{1,0:T(8,128)S(1)}, u32[]{:S(2)}, u32[]{:S(2)}) collective-permute-start(f32[32,1024]{1,0:T(8,128)S(1)} %fusion.51), channel_id=1, source_target_pairs={{0,3},{1,0},{2,1},{3,2},{4,7},{5,4},{6,5},{7,6},{8,11},{9,8},{10,9... | collective-permute-start | bytes 393224 | tf_op jit(solution)/shard_map/ppermute | solution.py:653
  220.5 205.1 %all-gather.14.cloned.1.call-start = ((), (), s32[]{:S(2)}) async-start(), calls=%async_computation.3 | async-start | bytes 15335424 | tf_op jit(solution)/shard_map/all_gather | solution.py:692
  237.5 236.4 %reduce-scatter.4.cloned.1.call-start = ((), (), s32[]{:S(2)}) async-start(), calls=%async_computation.8 | async-start | bytes 6553600
  237.5 21.7 %collective-permute-start.31 = (f32[4,448,256]{2,1,0:T(8,128)}, f32[4,448,256]{2,1,0:T(8,128)}, u32[]{:S(2)}, u32[]{:S(2)}) collective-permute-start(f32[4,448,256]{2,1,0:T(8,128)} %bitcast.502), channel_id=1, source_target_pairs={{0,4},{4,0},{8,12},{12,8},{16,20},{20,16},{24,28},{28,24},{1,5},{5... | collective-permute-start | bytes 5505032 | tf_op jit(solution)/shard_map/ppermute | solution.py:698
  239.0 20.3 %collective-permute-start.32 = (f32[4,448,256]{2,1,0:T(8,128)}, f32[4,448,256]{2,1,0:T(8,128)}, u32[]{:S(2)}, u32[]{:S(2)}) collective-permute-start(f32[4,448,256]{2,1,0:T(8,128)} %collective-permute-done.15.refs_9_), channel_id=1, source_target_pairs={{0,4},{4,0},{8,12},{12,8},{16,20},{20,16},{24,28},{28,24},{1,5},{5... | collective-permute-start | bytes 5505032 | tf_op jit(solution)/shard_map/ppermute | solution.py:698
  239.0 20.2 %collective-permute-start.33 = (f32[4,448,256]{2,1,0:T(8,128)}, f32[4,448,256]{2,1,0:T(8,128)}, u32[]{:S(2)}, u32[]{:S(2)}) collective-permute-start(f32[4,448,256]{2,1,0:T(8,128)} %collective-permute-done.16.refs_10_), channel_id=1, source_target_pairs={{0,4},{4,0},{8,12},{12,8},{16,20},{20,16},{24,28},{28,24},{1,5},{5... | collective-permute-start | bytes 5505032 | tf_op jit(solution)/shard_map/ppermute | solution.py:698
  245.8 13.4 %collective-permute-start.34 = (f32[4,256,256]{2,1,0:T(8,128)S(1)}, f32[4,256,256]{2,1,0:T(8,128)}, u32[]{:S(2)}, u32[]{:S(2)}) collective-permute-start(f32[4,256,256]{2,1,0:T(8,128)S(1)} %collective-permute-done.23.refs_11_), channel_id=1, source_target_pairs={{0,4},{4,0},{8,12},{12,8},{16,20},{20,16},{24,28},{28,24},{1,5},{5... | collective-permute-start | bytes 3145736 | tf_op jit(solution)/shard_map/ppermute | solution.py:698
  304.1 11.0 %collective-permute-start.36 = (f32[32,1024]{1,0:T(8,128)S(1)}, f32[32,1024]{1,0:T(8,128)S(1)}, u32[]{:S(2)}, u32[]{:S(2)}) collective-permute-start(f32[32,1024]{1,0:T(8,128)S(1)} %get-tuple-element.454), channel_id=1, source_target_pairs={{0,1},{1,2},{2,3},{3,0},{4,5},{5,6},{6,7},{7,4},{8,9},{9,10},{10,1... | collective-permute-start | bytes 393224 | tf_op jit(solution)/shard_map/ppermute | solution.py:653
  316.1 16.1 %collective-permute-start.39 = (f32[32,1024]{1,0:T(8,128)S(1)}, f32[32,1024]{1,0:T(8,128)S(1)}, u32[]{:S(2)}, u32[]{:S(2)}) collective-permute-start(f32[32,1024]{1,0:T(8,128)S(1)} %fusion.45), channel_id=1, source_target_pairs={{0,1},{1,2},{2,3},{3,0},{4,5},{5,6},{6,7},{7,4},{8,9},{9,10},{10,1... | collective-permute-start | bytes 393224 | tf_op jit(solution)/shard_map/ppermute | solution.py:653
  318.4 13.9 %collective-permute-start.40 = (f32[32,1024]{1,0:T(8,128)S(1)}, f32[32,1024]{1,0:T(8,128)S(1)}, u32[]{:S(2)}, u32[]{:S(2)}) collective-permute-start(f32[32,1024]{1,0:T(8,128)S(1)} %fusion.45), channel_id=1, source_target_pairs={{0,2},{1,3},{2,0},{3,1},{4,6},{5,7},{6,4},{7,5},{8,10},{9,11},{10,... | collective-permute-start | bytes 393224 | tf_op jit(solution)/shard_map/ppermute | solution.py:653
  319.8 12.5 %collective-permute-start.41 = (f32[32,1024]{1,0:T(8,128)S(1)}, f32[32,1024]{1,0:T(8,128)S(1)}, u32[]{:S(2)}, u32[]{:S(2)}) collective-permute-start(f32[32,1024]{1,0:T(8,128)S(1)} %fusion.45), channel_id=1, source_target_pairs={{0,3},{1,0},{2,1},{3,2},{4,7},{5,4},{6,5},{7,6},{8,11},{9,8},{10,9... | collective-permute-start | bytes 393224 | tf_op jit(solution)/shard_map/ppermute | solution.py:653
  332.4 18.6 %collective-permute-start.42 = (f32[4,1280,256]{2,1,0:T(8,128)}, f32[4,1280,256]{2,1,0:T(8,128)}, u32[]{:S(2)}, u32[]{:S(2)}) collective-permute-start(f32[4,1280,256]{2,1,0:T(8,128)} %bitcast.499), channel_id=1, source_target_pairs={{0,4},{4,0},{8,12},{12,8},{16,20},{20,16},{24,28},{28,24},{1,5},{5... | collective-permute-start | bytes 15728648 | tf_op jit(solution)/shard_map/ppermute | solution.py:698
  335.1 15.8 %collective-permute-start.45 = (f32[128,256]{1,0:T(8,128)S(1)}, f32[128,256]{1,0:T(8,128)S(1)}, u32[]{:S(2)}, u32[]{:S(2)}) collective-permute-start(f32[128,256]{1,0:T(8,128)S(1)} %get-tuple-element.452), channel_id=1, source_target_pairs={{0,3},{1,0},{2,1},{3,2},{4,7},{5,4},{6,5},{7,6},{8,11},{9,8},{10,9... | collective-permute-start | bytes 393224 | tf_op jit(solution)/shard_map/ppermute | solution.py:653
  338.3 12.7 %collective-permute-start.44 = (f32[128,256]{1,0:T(8,128)S(1)}, f32[128,256]{1,0:T(8,128)S(1)}, u32[]{:S(2)}, u32[]{:S(2)}) collective-permute-start(f32[128,256]{1,0:T(8,128)S(1)} %get-tuple-element.453), channel_id=1, source_target_pairs={{0,2},{1,3},{2,0},{3,1},{4,6},{5,7},{6,4},{7,5},{8,10},{9,11},{10,... | collective-permute-start | bytes 393224 | tf_op jit(solution)/shard_map/ppermute | solution.py:653
  338.6 12.3 %collective-permute-start.43 = (f32[128,256]{1,0:T(8,128)S(1)}, f32[128,256]{1,0:T(8,128)S(1)}, u32[]{:S(2)}, u32[]{:S(2)}) collective-permute-start(f32[128,256]{1,0:T(8,128)S(1)} %get-tuple-element.451), channel_id=1, source_target_pairs={{0,1},{1,2},{2,3},{3,0},{4,5},{5,6},{6,7},{7,4},{8,9},{9,10},{10,1... | collective-permute-start | bytes 393224 | tf_op jit(solution)/shard_map/ppermute | solution.py:653
  356.5 163.9 %all-gather.16.cloned.1.call-start = ((), (), s32[]{:S(2)}) async-start(), calls=%async_computation.4 | async-start | bytes 15335424 | tf_op jit(solution)/shard_map/all_gather | solution.py:692
  360.2 11.3 %collective-permute-start.46 = (f32[32,1024]{1,0:T(8,128)S(1)}, f32[32,1024]{1,0:T(8,128)S(1)}, u32[]{:S(2)}, u32[]{:S(2)}) collective-permute-start(f32[32,1024]{1,0:T(8,128)S(1)} %get-tuple-element.448), channel_id=1, source_target_pairs={{0,1},{1,2},{2,3},{3,0},{4,5},{5,6},{6,7},{7,4},{8,9},{9,10},{10,1... | collective-permute-start | bytes 393224 | tf_op jit(solution)/shard_map/ppermute | solution.py:653
  372.9 240.6 %all-gather.18.cloned.1.call-start = ((), (), s32[]{:S(2)}) async-start(), calls=%async_computation.5 | async-start | bytes 17694720 | tf_op jit(solution)/shard_map/all_gather | solution.py:692
  375.3 10.9 %collective-permute-start.50 = (f32[32,1024]{1,0:T(8,128)S(1)}, f32[32,1024]{1,0:T(8,128)S(1)}, u32[]{:S(2)}, u32[]{:S(2)}) collective-permute-start(f32[32,1024]{1,0:T(8,128)S(1)} %fusion.41), channel_id=1, source_target_pairs={{0,2},{1,3},{2,0},{3,1},{4,6},{5,7},{6,4},{7,5},{8,10},{9,11},{10,... | collective-permute-start | bytes 393224 | tf_op jit(solution)/shard_map/ppermute | solution.py:653
  375.8 12.3 %collective-permute-start.51 = (f32[32,1024]{1,0:T(8,128)S(1)}, f32[32,1024]{1,0:T(8,128)S(1)}, u32[]{:S(2)}, u32[]{:S(2)}) collective-permute-start(f32[32,1024]{1,0:T(8,128)S(1)} %fusion.41), channel_id=1, source_target_pairs={{0,3},{1,0},{2,1},{3,2},{4,7},{5,4},{6,5},{7,6},{8,11},{9,8},{10,9... | collective-permute-start | bytes 393224 | tf_op jit(solution)/shard_map/ppermute | solution.py:653
  439.7 10.8 %collective-permute-start.58 = (f32[32,1024]{1,0:T(8,128)S(1)}, f32[32,1024]{1,0:T(8,128)S(1)}, u32[]{:S(2)}, u32[]{:S(2)}) collective-permute-start(f32[32,1024]{1,0:T(8,128)S(1)} %get-tuple-element.442), channel_id=1, source_target_pairs={{0,1},{1,2},{2,3},{3,0},{4,5},{5,6},{6,7},{7,4},{8,9},{9,10},{10,1... | collective-permute-start | bytes 393224 | tf_op jit(solution)/shard_map/ppermute | solution.py:653
  454.3 237.2 %all-gather.22.cloned.1.call-start = ((), (), s32[]{:S(2)}) async-start(), calls=%async_computation.7 | async-start | bytes 4128768 | tf_op jit(solution)/shard_map/all_gather | solution.py:977
  463.0 10.8 %collective-permute-start.63 = (f32[32,1024]{1,0:T(8,128)S(1)}, f32[32,1024]{1,0:T(8,128)S(1)}, u32[]{:S(2)}, u32[]{:S(2)}) collective-permute-start(f32[32,1024]{1,0:T(8,128)S(1)} %fusion.37), channel_id=1, source_target_pairs={{0,3},{1,0},{2,1},{3,2},{4,7},{5,4},{6,5},{7,6},{8,11},{9,8},{10,9... | collective-permute-start | bytes 393224 | tf_op jit(solution)/shard_map/ppermute | solution.py:653
  476.2 25.9 %collective-permute-start.66 = (f32[320,256]{1,0:T(8,128)}, f32[320,256]{1,0:T(8,128)S(1)}, u32[]{:S(2)}, u32[]{:S(2)}) collective-permute-start(f32[320,256]{1,0:T(8,128)} %get-tuple-element.427), channel_id=1, source_target_pairs={{0,3},{1,0},{2,1},{3,2},{4,7},{5,4},{6,5},{7,6},{8,11},{9,8},{10,9... | collective-permute-start | bytes 983048 | tf_op jit(solution)/shard_map/ppermute | solution.py:653
  476.2 25.9 %collective-permute-start.65 = (f32[320,256]{1,0:T(8,128)}, f32[320,256]{1,0:T(8,128)}, u32[]{:S(2)}, u32[]{:S(2)}) collective-permute-start(f32[320,256]{1,0:T(8,128)} %get-tuple-element.428), channel_id=1, source_target_pairs={{0,2},{1,3},{2,0},{3,1},{4,6},{5,7},{6,4},{7,5},{8,10},{9,11},{10,... | collective-permute-start | bytes 983048 | tf_op jit(solution)/shard_map/ppermute | solution.py:653
  477.0 27.9 %collective-permute-start.64 = (f32[320,256]{1,0:T(8,128)}, f32[320,256]{1,0:T(8,128)}, u32[]{:S(2)}, u32[]{:S(2)}) collective-permute-start(f32[320,256]{1,0:T(8,128)} %get-tuple-element.426), channel_id=1, source_target_pairs={{0,1},{1,2},{2,3},{3,0},{4,5},{5,6},{6,7},{7,4},{8,9},{9,10},{10,1... | collective-permute-start | bytes 983048 | tf_op jit(solution)/shard_map/ppermute | solution.py:653
  499.8 45.4 %collective-permute-start.72 = (f32[4,64,512]{2,1,0:T(8,128)}, f32[4,64,512]{2,1,0:T(8,128)}, u32[]{:S(2)}, u32[]{:S(2)}) collective-permute-start(f32[4,64,512]{2,1,0:T(8,128)} %get-tuple-element.429), channel_id=1, source_target_pairs={{0,4},{4,0},{8,12},{12,8},{16,20},{20,16},{24,28},{28,24},{1,5},{5... | collective-permute-start | bytes 1572872 | tf_op jit(solution)/shard_map/ppermute | solution.py:698
  510.0 35.2 %collective-permute-start.70 = (f32[128,1408]{1,0:T(8,128)S(1)}, f32[128,1408]{1,0:T(8,128)}, u32[]{:S(2)}, u32[]{:S(2)}) collective-permute-start(f32[128,1408]{1,0:T(8,128)S(1)} %select_maximum_fusion.refs_0_), channel_id=1, source_target_pairs={{0,8},{4,12},{8,0},{12,4},{16,24},{20,28},{24,16},{28,20},{1,9},{5... | collective-permute-start | bytes 2162696 | tf_op jit(solution)/shard_map/ppermute | solution.py:698
  510.9 34.3 %collective-permute-start.71 = (f32[128,1408]{1,0:T(8,128)S(1)}, f32[128,1408]{1,0:T(8,128)}, u32[]{:S(2)}, u32[]{:S(2)}) collective-permute-start(f32[128,1408]{1,0:T(8,128)S(1)} %select_maximum_fusion.refs_0_), channel_id=1, source_target_pairs={{0,16},{4,20},{8,24},{12,28},{16,0},{20,4},{24,8},{28,12},{1,17},{... | collective-permute-start | bytes 2162696 | tf_op jit(solution)/shard_map/ppermute | solution.py:698
  545.2 12.0 %collective-permute-start.73 = (f32[32,1024]{1,0:T(8,128)}, f32[32,1024]{1,0:T(8,128)S(1)}, u32[]{:S(2)}, u32[]{:S(2)}) collective-permute-start(f32[32,1024]{1,0:T(8,128)} %fusion.35), channel_id=1, source_target_pairs={{0,1},{1,2},{2,3},{3,0},{4,5},{5,6},{6,7},{7,4},{8,9},{9,10},{10,1... | collective-permute-start | bytes 393224 | tf_op jit(solution)/shard_map/ppermute | solution.py:653
  547.5 10.9 %collective-permute-start.74 = (f32[32,1024]{1,0:T(8,128)}, f32[32,1024]{1,0:T(8,128)S(1)}, u32[]{:S(2)}, u32[]{:S(2)}) collective-permute-start(f32[32,1024]{1,0:T(8,128)} %fusion.35), channel_id=1, source_target_pairs={{0,2},{1,3},{2,0},{3,1},{4,6},{5,7},{6,4},{7,5},{8,10},{9,11},{10,... | collective-permute-start | bytes 393224 | tf_op jit(solution)/shard_map/ppermute | solution.py:653
  548.8 29.8 %collective-permute-start.75 = (f32[32,1024]{1,0:T(8,128)}, f32[32,1024]{1,0:T(8,128)S(1)}, u32[]{:S(2)}, u32[]{:S(2)}) collective-permute-start(f32[32,1024]{1,0:T(8,128)} %fusion.35), channel_id=1, source_target_pairs={{0,3},{1,0},{2,1},{3,2},{4,7},{5,4},{6,5},{7,6},{8,11},{9,8},{10,9... | collective-permute-start | bytes 393224 | tf_op jit(solution)/shard_map/ppermute | solution.py:653
  549.0 29.8 %collective-permute-start.78 = (f32[256,512]{1,0:T(8,128)S(1)}, f32[256,512]{1,0:T(8,128)S(1)}, u32[]{:S(2)}, u32[]{:S(2)}) collective-permute-start(f32[256,512]{1,0:T(8,128)S(1)} %get-tuple-element.424), channel_id=1, source_target_pairs={{0,3},{1,0},{2,1},{3,2},{4,7},{5,4},{6,5},{7,6},{8,11},{9,8},{10,9... | collective-permute-start | bytes 1572872 | tf_op jit(solution)/shard_map/ppermute | solution.py:653
  551.3 40.0 %collective-permute-start.77 = (f32[256,512]{1,0:T(8,128)S(1)}, f32[256,512]{1,0:T(8,128)S(1)}, u32[]{:S(2)}, u32[]{:S(2)}) collective-permute-start(f32[256,512]{1,0:T(8,128)S(1)} %get-tuple-element.425), channel_id=1, source_target_pairs={{0,2},{1,3},{2,0},{3,1},{4,6},{5,7},{6,4},{7,5},{8,10},{9,11},{10,... | collective-permute-start | bytes 1572872 | tf_op jit(solution)/shard_map/ppermute | solution.py:653
  557.2 45.3 %collective-permute-start.76 = (f32[256,512]{1,0:T(8,128)S(1)}, f32[256,512]{1,0:T(8,128)S(1)}, u32[]{:S(2)}, u32[]{:S(2)}) collective-permute-start(f32[256,512]{1,0:T(8,128)S(1)} %get-tuple-element.423), channel_id=1, source_target_pairs={{0,1},{1,2},{2,3},{3,0},{4,5},{5,6},{6,7},{7,4},{8,9},{9,10},{10,1... | collective-permute-start | bytes 1572872 | tf_op jit(solution)/shard_map/ppermute | solution.py:653
  558.5 44.3 %collective-permute-start.79 = (f32[64,1408]{1,0:T(8,128)S(1)}, f32[64,1408]{1,0:T(8,128)S(1)}, u32[]{:S(2)}, u32[]{:S(2)}) collective-permute-start(f32[64,1408]{1,0:T(8,128)S(1)} %slice.214), channel_id=1, source_target_pairs={{0,16},{4,20},{8,24},{12,28},{16,0},{20,4},{24,8},{28,12},{1,17},{... | collective-permute-start | bytes 1081352 | tf_op jit(solution)/shard_map/ppermute | solution.py:698
  578.7 25.5 %collective-permute-start.80 = (f32[64,1408]{1,0:T(8,128)S(1)}, f32[64,1408]{1,0:T(8,128)}, u32[]{:S(2)}, u32[]{:S(2)}) collective-permute-start(f32[64,1408]{1,0:T(8,128)S(1)} %slice.215), channel_id=1, source_target_pairs={{0,8},{4,12},{8,0},{12,4},{16,24},{20,28},{24,16},{28,20},{1,9},{5... | collective-permute-start | bytes 1081352 | tf_op jit(solution)/shard_map/ppermute | solution.py:698
  578.8 23.9 %collective-permute-start.81 = (f32[2,32,512]{2,1,0:T(8,128)S(1)}, f32[2,32,512]{2,1,0:T(8,128)S(1)}, u32[]{:S(2)}, u32[]{:S(2)}) collective-permute-start(f32[2,32,512]{2,1,0:T(8,128)S(1)} %get-tuple-element.433), channel_id=1, source_target_pairs={{0,8},{4,12},{8,0},{12,4},{16,24},{20,28},{24,16},{28,20},{1,9},{5... | collective-permute-start | bytes 393224 | tf_op jit(solution)/shard_map/ppermute | solution.py:698
  591.3 11.5 %collective-permute-start.82 = (f32[2,32,512]{2,1,0:T(8,128)S(1)}, f32[2,32,512]{2,1,0:T(8,128)S(1)}, u32[]{:S(2)}, u32[]{:S(2)}) collective-permute-start(f32[2,32,512]{2,1,0:T(8,128)S(1)} %get-tuple-element.431), channel_id=1, source_target_pairs={{0,16},{4,20},{8,24},{12,28},{16,0},{20,4},{24,8},{28,12},{1,17},{... | collective-permute-start | bytes 393224 | tf_op jit(solution)/shard_map/ppermute | solution.py:698
  623.8 46.0 %collective-permute-start.83 = (f32[128,1408]{1,0:T(8,128)}, f32[128,1408]{1,0:T(8,128)S(1)}, u32[]{:S(2)}, u32[]{:S(2)}) collective-permute-start(f32[128,1408]{1,0:T(8,128)} %copy-done.11), channel_id=1, source_target_pairs={{0,4},{4,0},{8,12},{12,8},{16,20},{20,16},{24,28},{28,24},{1,5},{5... | collective-permute-start | bytes 2162696 | tf_op jit(solution)/shard_map/ppermute | solution.py:698
  625.5 44.4 %collective-permute-start.84 = (f32[128,1408]{1,0:T(8,128)}, f32[128,1408]{1,0:T(8,128)S(1)}, u32[]{:S(2)}, u32[]{:S(2)}) collective-permute-start(f32[128,1408]{1,0:T(8,128)} %collective-permute-done.70.refs_1_), channel_id=1, source_target_pairs={{0,4},{4,0},{8,12},{12,8},{16,20},{20,16},{24,28},{28,24},{1,5},{5... | collective-permute-start | bytes 2162696 | tf_op jit(solution)/shard_map/ppermute | solution.py:698
  625.5 44.4 %collective-permute-start.85 = (f32[128,1408]{1,0:T(8,128)}, f32[128,1408]{1,0:T(8,128)}, u32[]{:S(2)}, u32[]{:S(2)}) collective-permute-start(f32[128,1408]{1,0:T(8,128)} %collective-permute-done.71.refs_2_), channel_id=1, source_target_pairs={{0,4},{4,0},{8,12},{12,8},{16,20},{20,16},{24,28},{28,24},{1,5},{5... | collective-permute-start | bytes 2162696 | tf_op jit(solution)/shard_map/ppermute | solution.py:698
  626.0 43.8 %collective-permute-start.86 = (f32[64,1408]{1,0:T(8,128)}, f32[64,1408]{1,0:T(8,128)}, u32[]{:S(2)}, u32[]{:S(2)}) collective-permute-start(f32[64,1408]{1,0:T(8,128)} %copy-done.36), channel_id=1, source_target_pairs={{0,4},{4,0},{8,12},{12,8},{16,20},{20,16},{24,28},{28,24},{1,5},{5... | collective-permute-start | bytes 1081352 | tf_op jit(solution)/shard_map/ppermute | solution.py:698
  626.0 43.8 %collective-permute-start.87 = (f32[64,1408]{1,0:T(8,128)}, f32[64,1408]{1,0:T(8,128)}, u32[]{:S(2)}, u32[]{:S(2)}) collective-permute-start(f32[64,1408]{1,0:T(8,128)} %collective-permute-done.80.refs_4_), channel_id=1, source_target_pairs={{0,4},{4,0},{8,12},{12,8},{16,20},{20,16},{24,28},{28,24},{1,5},{5... | collective-permute-start | bytes 1081352 | tf_op jit(solution)/shard_map/ppermute | solution.py:698
  (103 other events, 1311.1 us)
Sparse Core Ops, SparseCore 0:
  12.5 38.0 all-gather.9
  67.6 60.9 all-gather.19
  220.7 58.9 all-gather.11
  281.4 76.3 all-gather.13
  360.6 61.4 reduce-scatter.3
  423.9 76.4 all-gather.15
  502.3 111.0 all-gather.17
  621.3 36.0 all-gather.21

commit v3 on v2

--- a/solution.py
+++ b/solution.py
@@ -55,8 +55,8 @@
     return jax.ShapeDtypeStruct(dims, jnp.float32)
 
 
-def run_whole(kernel, outs, args, flops=1e9, scratch=(), anywhere=0):
-    moved = sum(a.size * 4 for a in args) + sum(int(functools.reduce(lambda x, y: x * y, o.shape)) * 4 for o in outs)
+def run_whole(kernel, outs, args, flops=1e9, moved=None, scratch=(), anywhere=0):
+    moved = moved or sum(a.size * 4 for a in args) + sum(int(functools.reduce(lambda x, y: x * y, o.shape)) * 4 for o in outs)
     fast = len(args) - anywhere
     return pl.pallas_call(
         kernel,
@@ -280,6 +280,8 @@
     wout_ref,
     latents_ref,
     hat_ref,
+    int_gain_ref,
+    att_ref,
     grad_ref,
     dgain_ref,
     dq_ref,
@@ -288,6 +290,8 @@
     dint_ref,
     dgain_lat_ref,
     dgain_int_ref,
+    dkeyval_ref,
+    dout_ref,
 ):
     residual_back(base_ref, dsum_ref, state_ref, gain_ref, grad_ref, dgain_ref)
     part = dq_ref.shape[1]
@@ -310,6 +314,11 @@
     for z in range(hat_ref.shape[0]):
         dgain_int += jnp.sum(dint[z * patches : (z + 1) * patches] * hat_ref[z, :patches], axis=0, keepdims=True)
     dgain_int_ref[...] = dgain_int
+    dout_ref[...] = tmm(att_ref[...], grad_ref[...])
+    total = jnp.zeros_like(dkeyval_ref)
+    for z in range(hat_ref.shape[0]):
+        total += tmm(hat_ref[z, :patches] * int_gain_ref[...], dkv_ref[z * patches : (z + 1) * patches])
+    dkeyval_ref[...] = total
 
 
 def write_kernel(
@@ -659,6 +668,13 @@
             total = total + shift(sent, step)
         return total
 
+    def z_pieces(parts):
+        pieces = [lax.dynamic_index_in_dim(parts, me, 0, keepdims=False)]
+        for step in range(1, zs):
+            sent = lax.dynamic_index_in_dim(parts, (me + step) % zs, 0, keepdims=False)
+            pieces.append(shift(sent, step))
+        return pieces
+
     def z_gather(own):
         out = jnp.zeros((zs,) + own.shape, own.dtype)
         out = lax.dynamic_update_index_in_dim(out, own, me, 0)
@@ -795,8 +811,8 @@
     part1, shares = tie(part1, shares)
     if direct:
         by_x, by_y = swap(shares, 2), swap(shares, 4)
-    state2, read_attended, normed1, act1 = sum_over_head(part1, state1, (read_attended, normed1, act1))
-    read_joined = join([read_attended, normed1, act1])
+    state2, normed1, act1 = sum_over_head(part1, state1, (normed1, act1))
+    read_joined = join([normed1, act1])
 
     normed2, packed, self_attended, self_weights, part2 = run_whole(
         functools.partial(self_kernel, deep // HEADS),
@@ -833,10 +849,8 @@
         full_out = jnp.transpose(widen(everything, at, wq_rows, wide), (1, 0, 2, 3)).reshape(zs, -1, wide)
         pieces = [full_kv, full_query, full_out, full_up, full_down]
     read_all = d_gather([read_joined])
-    state4, normed2, self_attended, normed3, act3 = sum_over_head(
-        part3, state3, (normed2, self_attended, normed3, act3)
-    )
-    layer_all = d_gather([normed2, self_attended, normed3, act3])
+    state4, normed2, normed3, act3 = sum_over_head(part3, state3, (normed2, normed3, act3))
+    layer_all = d_gather([normed2, normed3, act3])
 
     (
         normed4, interface_new, dafter, dwrite_q, write_attended, after_normed, act5, dpre5, dkv4, dgain_mlp, part4,
@@ -914,17 +928,18 @@
         (dstate4, dsum3, state3, layer_gain_mlp[None], packed, self_weights, qkv, layer_out),
         flops=8 * count * deep * part,
     )
-    dsum2, released3, dpacked = sum_over_head(part6, None, (dstate3, dpacked))
+    dsum2, dpacked = sum_over_head(part6, None, (dpacked,))
+    dlayer_out = tmm(self_attended, dstate3)
     dsum2, layer_all = tie(dsum2, layer_all)
 
     dstate2, dgain2, dpre1, part7 = ffn_backward(
         dstate3, dsum2, state2, layer_gain_att, pre1, read_up, read_down
     )
     dsum1, released2, dpre1 = sum_over_head(part7, None, (dstate2, dpre1))
-    both_all = d_gather([released3, dpacked, released2, dpre1])
+    both_all = d_gather([dpacked, released2, dpre1])
     dsum1, grads_mine = tie(dsum1, grads_mine)
     grads_mine = z_scatter(grads_mine.reshape(zs, -1, pack))
-    dstate1, dgain1, dquery0, dread_kv, dlat_part, dint_part, dgain_lat, dgain_int = run_whole(
+    dstate1, dgain1, dquery0, dread_kv, dlat_part, dint_part, dgain_lat, dgain_int, dkeyval, dread_out = run_whole(
         functools.partial(read_back_kernel, deep // HEADS),
         [
             shape_of(count, deep),
@@ -935,11 +950,14 @@
             shape_of(zs * patches, wide),
             shape_of(1, deep),
             shape_of(1, wide),
+            shape_of(wide, 2 * part),
+            shape_of(part, deep),
         ],
-        (dstate2, dsum1, state1, read_gain_mlp[None], query, kv0, read_weights, read_query, keyval, read_out, latents, int_pack),
-        flops=16 * zs * patches * wide * part,
-    )
-    dlat_part, dstate1, grads_mine = tie(dlat_part, dstate1, grads_mine)
+        (dstate2, dsum1, state1, read_gain_mlp[None], query, kv0, read_weights, read_query, keyval, read_out, latents, int_pack,
+         gain_read[None], read_attended),
+        flops=1e6,
+        moved=1e6,
+    )
 
     first = (me == 0).astype(jnp.float32)
     small = jnp.concatenate(
@@ -947,59 +965,75 @@
         + [g[0] * first for g in (dgain1, dgain2, dgain3, dgain4)]
         + [dgain_int[0], jnp.sum(dwrite_normed * int_hat, axis=0), dgain_mlp[0]]
     )
+    dlat_part, dstate1, grads_mine, small = tie(dlat_part, dstate1, grads_mine, small)
     lanes = small.size // count
-    fill = jnp.pad(small.reshape(count, lanes), ((0, 0), (0, -lanes % 128)))
-    late = [join([dstate1, dquery0, fill])]
-
-    dkeyval = tmm(int_pack[:, :patches].reshape(zs * patches, wide) * gain_read, dread_kv)
+    small = jnp.sum(z_gather(small.reshape(count, lanes)), axis=0)
+    fill = jnp.pad(small, ((0, 0), (0, -lanes % 128)))
+    late = [join([dquery0, fill])]
+
     half = z_scatter(dlat_part.reshape(zs, count // zs, deep))
-    wide_lat = read_attended.shape[1]
     write_all = tie(write_all, dgain_int)[0]
     normed4_all, dkv_all, dstate4_all, dpre3_all = cut_up(write_all, [normed4, dkv_mine, dstate4, dpre3])
-    normed2_all, self_att_all, normed3_all, act3_all = cut_up(layer_all, [normed2, self_attended, normed3, act3])
-    grad_layer_up, grad_layer_down = tmm(normed3_all, dpre3_all), tmm(act3_all, dstate4_all)
-    grad_write_keyval = tmm(normed4_all, dkv_all)
+    normed2_all, normed3_all, act3_all = cut_up(layer_all, [normed2, normed3, act3])
+    grad_layer_up = tmm(normed3_all, dpre3_all)
     if direct:
         late = to_sides(*late)
+        dkeyval = [dkeyval] + [
+            grad.reshape(ds, -1, deep)[:, :, at : at + 2 * part].reshape(-1, 2 * part)
+            for grad in (dlayer_out, dread_out)
+            for at in range(0, deep, 2 * part)
+        ]
+        dkeyval = jnp.concatenate([grad.reshape(ds, -1, 2 * part) for grad in dkeyval], axis=1)
         dkeyval = dkeyval.reshape(4, 2, -1, 2 * part)
         pair = [pick(dkeyval, core, 1), swap(pick(dkeyval, 1 - core, 1), 1)]
-        half, dint_part, grad_layer_up, grad_layer_down, grad_write_keyval, *held = tie(
-            half, dint_part, grad_layer_up, grad_layer_down, grad_write_keyval, *late, *pair
+        half, dint_part, grad_layer_up, act3_all, normed4_all, *held = tie(
+            half, dint_part, grad_layer_up, act3_all, normed4_all, *late, *pair
         )
         late, pair = to_across(*held[:3]), scatter_one(*held[3:])
-    dint_normed = z_scatter(dint_part.reshape(zs, patches, wide))
+    dint_own, *dint_got = z_pieces(dint_part.reshape(zs, patches, wide))
+    near, middle_got, far = dint_got[0], dint_got[1:-1], dint_got[-1]
     dlat = z_gather(half).reshape(count, deep)
+    grad_layer_down, grad_write_keyval = tmm(act3_all, dstate4_all), tmm(normed4_all, dkv_all)
     if direct:
-        dlat, dint_normed, both_all, *held = tie(dlat, dint_normed, both_all, *late, *pair)
-        late, pair = held[:5], held[5:]
-        late, dkeyval = to_core(*late), scatter_two(*pair)
+        grad_layer_down, both_all, near, *held = tie(grad_layer_down, both_all, near, *late, *pair)
+        late, dkeyval = to_core(*held[:5]), scatter_two(*held[5:])
+    dpacked_all, dstate2_all, dpre1_all = cut_up(both_all, [dpacked, dstate2, dpre1])
+    normed1_all, act1_all = cut_up(read_all, [normed1, act1])
+    grad_layer_qkv, grad_read_up = tmm(normed2_all, dpacked_all), tmm(normed1_all, dpre1_all)
+    if direct:
+        dkeyval, grad_layer_qkv, dstate2_all, far, *late = tie(dkeyval, grad_layer_qkv, dstate2_all, far, *late)
+    grad_read_down = tmm(act1_all, dstate2_all)
+    if direct:
+        dlat, grad_write_keyval, grad_read_up, grad_read_down, *middle_got = tie(
+            dlat, grad_write_keyval, grad_read_up, grad_read_down, *middle_got
+        )
         flat = jnp.concatenate([grads_mine] + [dkeyval[:, at : at + pack] for at in range(0, 2 * part, pack)], axis=0)
         grads_all = lax.all_gather(flat, "dp", axis=0, tiled=False)
-        grad_read_keyval = widen(grads_all[:, None], piece_rows, dkeyval.shape[0], 2 * part)
+        grad_read_query, small = outer_products(
+            late, place, [early_all], [(0, 0, deep, 0, part)], (part, fill.shape[1])
+        )
+        small = small[:, :lanes]
+        sums = widen(grads_all[:, None], piece_rows, dkeyval.shape[0], 2 * part)[:, 0]
+        at, few = read_keyval.shape[0] // ds, part // ds
+        grad_read_keyval = sums[:, :at]
+        found = []
+        for _ in range(2):
+            blocks = [sums[:, at + n * few : at + (n + 1) * few] for n in range(deep // (2 * part))]
+            found.append(jnp.concatenate(blocks, axis=-1).reshape(part, deep))
+            at += few * len(blocks)
+        grad_layer_out, grad_read_out = found
     else:
         grads_all = lax.all_gather(grads_mine, "dp", axis=0, tiled=False)
-        grad_read_keyval = lax.psum(dkeyval, "dp")
-    dstate3_all, dpacked_all, dstate2_all, dpre1_all = cut_up(both_all, [dstate3, dpacked, dstate2, dpre1])
-    grad_layer_qkv, grad_layer_out = tmm(normed2_all, dpacked_all), tmm(self_att_all, dstate3_all)
-    read_att_all, normed1_all, act1_all = cut_up(read_all, [read_attended, normed1, act1])
-    if direct:
-        grad_read_query, grad_read_out, small = outer_products(
-            late,
-            place,
-            [early_all, read_all],
-            [(0, 0, deep, deep, part), (1, 0, part, 0, deep)],
-            (deep + part, fill.shape[1]),
-        )
-        small = small[:, :lanes]
-    else:
-        late_all = d_gather(late)
-        dstate1_all, dquery0_all, small = cut_up(late_all, [dstate1, dquery0, fill])
-        grad_read_query, grad_read_out = tmm(early_all, dquery0_all), tmm(read_att_all, dstate1_all)
+        grad_read_keyval, grad_layer_out, grad_read_out = lax.psum((dkeyval, dlayer_out, dread_out), "dp")
+        dquery0_all, small = cut_up(d_gather(late), [dquery0, fill])
+        grad_read_query = tmm(early_all, dquery0_all)
         small = jnp.sum(small.reshape(ds, count, -1)[:, :, :lanes], axis=0)
-    grad_read_up, grad_read_down = tmm(normed1_all, dpre1_all), tmm(act1_all, dstate2_all)
     latents_grad = dstate1 + norm_back(dlat, lat_hat, lat_root, read_gain_lat)
+    dint_normed = dint_own + near + far
+    for piece in middle_got:
+        dint_normed = dint_normed + piece
     interface_grad = dint + norm_back(dint_normed, int_hat, int_root, gain_read)
-    small = jnp.sum(z_gather(small), axis=0).reshape(-1)
+    small = small.reshape(-1)
     lat_gains = small[: 5 * deep].reshape(5, deep)
     int_gains = small[5 * deep :].reshape(3, zs, wide // zs)
     int_gains = lax.dynamic_index_in_dim(int_gains, me, 1, keepdims=False)

time: 723 us -> 712 us (0.985)
  starting transfers between devices: 151 us -> 126 us
  local copies, waits for them, and re-layouts: 69.8 us -> 88.4 us
    ppermute x24, starting transfers between devices: 43.4 us -> 21.2 us  [swap(): return lax.ppermute(values, 'dp', [(i, i ^ bits) for i in range(ds)])]
    ppermute x24, waiting for transfers between devices: 2.84 us -> 16.2 us  [swap(): return lax.ppermute(values, 'dp', [(i, i ^ bits) for i in range(ds)])]
    slice x1 -> x9, local copies, waits for them, and re-layouts: 0.2 us -> 9.33 us  [the longest x4 7.69 us: cut_up(): out.append(full[:, at:at + part.shape[1]])]
    dot_general x8 -> x7, matrix products: 63 us -> 58.2 us  [tmm(): lax.dot_general(left, right, (((0,), (0,)), ((), ())), precision=PRECISE)]
    unnamed x149 -> x177, local copies, waits for them, and re-layouts: 22.8 us -> 25.7 us
  transfers between devices with their start and end apart: 101 -> 101, of which waited for: 51 -> 52; matrix products, arithmetic and copies ran while one was open for 21% -> 22% of each run, Pallas kernels for 19% -> 19%
where the time goes in v3:
time: 712 us; the launch traced here: 701 us
  waiting for transfers between devices  231 us (32%)
  Pallas kernels  134 us (19%)
  starting transfers between devices  126 us (18%)
  local copies, waits for them, and re-layouts  88.4 us (12%)
  matrix products  59.2 us (8%)
  other arithmetic  46.2 us (6%)
  between operations  16.5 us (2%)
    ppermute x69, waiting for transfers between devices, shift(): lax.ppermute(values, 'head', [(i, (i + step) % zs) for i in range(zs)])  208 us
    ppermute x69, starting transfers between devices, shift(): lax.ppermute(values, 'head', [(i, (i + step) % zs) for i in range(zs)])  104 us
    dot_general x7, matrix products, tmm(): lax.dot_general(left, right, (((0,), (0,)), ((), ())), precision=PRECISE)  58.2 us
    pallas_call x1, Pallas kernels, write_stage(): pl.pallas_call(call, out_shape=outs, in_specs=[vmem] * 7 + [pl.BlockSpec(...  38.8 us
    pallas_call x4, Pallas kernels, run_whole(): pl.pallas_call(kernel, out_shape=outs, in_specs=[pl.BlockSpec(memory_spac...  36.9 us
    unnamed x177, local copies, waits for them, and re-layouts  25.7 us
    pallas_call x2, Pallas kernels, ffn_backward(): pl.pallas_call(ffn_back_kernel, grid=(inner // tile,), out_shape=[shape_o...  23.5 us
    ppermute x24, starting transfers between devices, swap(): return lax.ppermute(values, 'dp', [(i, i ^ bits) for i in range(ds)])  21.2 us
  transfers between devices with their start and end apart: 101, of which 52 were waited for; matrix products, arithmetic and copies ran while one was open for 22% of the time, Pallas kernels for 19%

profile of v3, /device:TPU:13, one launch (start us, length us, event | category | flops | bytes accessed | tf_op | source)
XLA Modules:
  0.0 701.2 jit_solution(17780073729468330623)
XLA Ops:
  19.0 2.5 copy.95
  30.4 32.1 %collective-permute-done.1 = f32[264,512]{1,0:T(8,128)} collective-permute-done((f32[264,512]{1,0:T(8,128)}, f32[264,512]{1,0:T(8,128)}, u32[]{:S(2)}, u32[]{:S(2)}) %collective-permute-start.1) | collective-permute-done | bytes 540704 | tf_op jit(solution)/shard_map/ppermute | solution.py:662
  70.7 8.6 %shard_map.458 = (f32[1024,512]{1,0:T(8,128)}, f32[128,256]{1,0:T(8,128)}, f32[512,1024]{1,0:T(8,128)}, f32[128,1024]{1,0:T(8,128)}) custom-call(f32[128,256]{1,0:T(8,128)} %fusion.66.q_ref, f32[4,264,512]{2,1,0:T(8,128)} %copy-done.5, f32[1,512]{1,0:T(1,128)} %get-tuple-element.526.gain_ref.int_gain_ref, s32[1,1024]{1,0:T(1,128)} %seg_ref.1, ...), custom_call_target="tpu_custom_call" | custom-call | flops 3221225472 | bytes 9246720 | tf_op jit(solution)/shard_map/pallas_call | solution.py:61
  84.1 10.9 %collective-permute-done.5 = f32[32,1024]{1,0:T(8,128)S(1)} collective-permute-done((f32[32,1024]{1,0:T(8,128)S(1)}, f32[32,1024]{1,0:T(8,128)S(1)}, u32[]{:S(2)}, u32[]{:S(2)}) %collective-permute-start.5) | collective-permute-done | bytes 131104 | tf_op jit(solution)/shard_map/ppermute | solution.py:662
  95.0 2.5 collective-permute-done.4
  97.5 8.5 %collective-permute-done.3 = f32[32,1024]{1,0:T(8,128)S(1)} collective-permute-done((f32[32,1024]{1,0:T(8,128)S(1)}, f32[32,1024]{1,0:T(8,128)S(1)}, u32[]{:S(2)}, u32[]{:S(2)}) %collective-permute-start.3) | collective-permute-done | bytes 131104 | tf_op jit(solution)/shard_map/ppermute | solution.py:662
  107.0 3.8 collective-permute-start.6
  112.8 7.4 %collective-permute-done.6 = f32[32,1024]{1,0:T(8,128)S(1)} collective-permute-done((f32[32,1024]{1,0:T(8,128)S(1)}, f32[32,1024]{1,0:T(8,128)S(1)}, u32[]{:S(2)}, u32[]{:S(2)}) %collective-permute-start.6) | collective-permute-done | bytes 131104 | tf_op jit(solution)/shard_map/ppermute | solution.py:662
  120.2 9.0 %collective-permute-done.7 = f32[32,1024]{1,0:T(8,128)S(1)} collective-permute-done((f32[32,1024]{1,0:T(8,128)S(1)}, f32[32,1024]{1,0:T(8,128)S(1)}, u32[]{:S(2)}, u32[]{:S(2)}) %collective-permute-start.7) | collective-permute-done | bytes 131104 | tf_op jit(solution)/shard_map/ppermute | solution.py:662
  132.5 7.6 %shard_map.459 = (f32[128,1024]{1,0:T(8,128)}, f32[128,1024]{1,0:T(8,128)}, f32[128,1024]{1,0:T(8,128)}, f32[128,1024]{1,0:T(8,128)}) custom-call(f32[128,1024]{1,0:T(8,128)} %bitcast.414, f32[1,1024]{1,0:T(1,128)} %bitcast.486, f32[1024,1024]{1,0:T(8,128)} %up_ref.3, f32[1024,1024]{1,0:T(8,128)} %down_ref.3), custom_call_target="tpu_custom_call" | custom-call | flops 1610612736 | bytes 8388608 | tf_op jit(solution)/shard_map/pallas_call | solution.py:142
  145.8 3.5 copy.101
  149.4 3.5 copy.102.qkv_ref
  159.6 12.1 %collective-permute-start.14 = (f32[32,1024]{1,0:T(8,128)S(1)}, f32[32,1024]{1,0:T(8,128)S(1)}, u32[]{:S(2)}, u32[]{:S(2)}) collective-permute-start(f32[32,1024]{1,0:T(8,128)S(1)} %fusion.43), channel_id=1, source_target_pairs={{0,3},{1,0},{2,1},{3,2},{4,7},{5,4},{6,5},{7,6},{8,11},{9,8},{10,9... | collective-permute-start | bytes 393224 | tf_op jit(solution)/shard_map/ppermute | solution.py:662
  171.9 4.0 collective-permute-done.14
  176.7 5.4 shard_map.460
  191.8 4.5 collective-permute-done.17
  201.8 8.1 %collective-permute-done.21 = f32[32,1024]{1,0:T(8,128)S(1)} collective-permute-done((f32[32,1024]{1,0:T(8,128)S(1)}, f32[32,1024]{1,0:T(8,128)S(1)}, u32[]{:S(2)}, u32[]{:S(2)}) %collective-permute-start.21) | collective-permute-done | bytes 131104 | tf_op jit(solution)/shard_map/ppermute | solution.py:662
  212.8 7.7 %shard_map.461 = (f32[128,1024]{1,0:T(8,128)}, f32[128,1024]{1,0:T(8,128)}, f32[128,1024]{1,0:T(8,128)}, f32[128,1024]{1,0:T(8,128)}) custom-call(f32[128,1024]{1,0:T(8,128)} %bitcast.420, f32[1,1024]{1,0:T(1,128)} %gain_ref.6, f32[1024,1024]{1,0:T(8,128)} %bitcast.403, f32[1024,1024]{1,0:T(8,128)} %bitcast.405), custom_call_target="tpu_custom_call" | custom-call | flops 1610612736 | bytes 8388608 | tf_op jit(solution)/shard_map/pallas_call | solution.py:142
  226.7 2.5 collective-permute-done.27
  230.1 5.0 collective-permute-done.25
  236.2 2.5 pad_maximum_fusion.1
  248.0 3.8 collective-permute-done.29
  251.8 3.0 collective-permute-start.30
  261.8 38.8 %shard_map.462 = (f32[128,1024]{1,0:T(8,128)}, f32[256,512]{1,0:T(8,128)}, f32[256,512]{1,0:T(8,128)}, f32[256,512]{1,0:T(8,128)}, f32[256,512]{1,0:T(8,128)}, /...) custom-call(f32[128,1024]{1,0:T(8,128)} %bitcast.435, ...), custom_call_target="tpu_custom_call" | custom-call | flops 20000000000 | bytes 40000000 | tf_op jit(solution)/shard_map/pallas_call | solution.py:503
  307.6 5.8 collective-permute-done.37
  313.4 3.0 collective-permute-done.36
  321.0 12.6 %shard_map.463 = (f32[4,4,320,256]{3,2,1,0:T(8,128)}, f32[4,4,320,256]{3,2,1,0:T(8,128)}) custom-call(f32[256,512]{1,0:T(8,128)} %get-tuple-element.221.y_ref, f32[256,2048]{1,0:T(8,128)} %get-tuple-element.222.dpre_ref, f32[256,2048]{1,0:T(8,128)} %get-tuple-element.223.act_ref, f32[256,512]{1,0:T(8,128)} %bitcast.509, f32[256,512]{1,0:T(8,128)} %copy-done.10, ...), custom_call_target="tpu_custom_call" | custom-call | flops 10000000000 | bytes 20000000 | tf_op jit(solution)/shard_map/pallas_call | solution.py:558
  336.6 2.8 collective-permute-start.45
  340.7 11.4 %shard_map.464 = (f32[128,1024]{1,0:T(8,128)}, f32[1,1024]{1,0:T(1,128)}, f32[128,1024]{1,0:T(8,128)}, f32[128,1024]{1,0:T(8,128)}) custom-call(f32[128,1024]{1,0:T(8,128)} %bitcast.459, f32[128,1024]{1,0:T(8,128)} %bitcast.438, f32[128,1024]{1,0:T(8,128)} %bitcast.436, f32[1,1024]{1,0:T(1,128)} %bitcast.494, f32[128,1024]{1,0:T(8,128)} %get-tuple-element.231.pre_ref, ...), custom_call_target="tpu_custom_call" | custom-call | flops 1610612736 | bytes 8388608 | tf_op jit(solution)/shard_map/pallas_call | solution.py:185
  352.2 5.5 add.581
  363.3 6.8 collective-permute-done.47
  370.1 2.8 collective-permute-done.46
  379.7 7.9 %collective-permute-done.50 = f32[32,1024]{1,0:T(8,128)S(1)} collective-permute-done((f32[32,1024]{1,0:T(8,128)S(1)}, f32[32,1024]{1,0:T(8,128)S(1)}, u32[]{:S(2)}, u32[]{:S(2)}) %collective-permute-start.50) | collective-permute-done | bytes 131104 | tf_op jit(solution)/shard_map/ppermute | solution.py:662
  390.2 7.8 %shard_map.465 = (f32[128,1024]{1,0:T(8,128)}, f32[1,1024]{1,0:T(1,128)}, f32[128,768]{1,0:T(8,128)}, f32[128,1024]{1,0:T(8,128)}) custom-call(f32[128,1024]{1,0:T(8,128)} %get-tuple-element.280.base_ref, f32[128,1024]{1,0:T(8,128)} %bitcast.448, f32[128,1024]{1,0:T(8,128)} %bitcast.422, f32[1,1024]{1,0:T(1,128)} %gain_ref.6, ...), custom_call_target="tpu_custom_call" | custom-call | flops 805306368 | bytes 7872512 | tf_op jit(solution)/shard_map/pallas_call | solution.py:61
  404.4 2.8 collective-permute-done.53
  407.2 4.1 collective-permute-done.52
  417.0 7.9 %collective-permute-done.56 = f32[32,1024]{1,0:T(8,128)S(1)} collective-permute-done((f32[32,1024]{1,0:T(8,128)S(1)}, f32[32,1024]{1,0:T(8,128)S(1)}, u32[]{:S(2)}, u32[]{:S(2)}) %collective-permute-start.56) | collective-permute-done | bytes 131104 | tf_op jit(solution)/shard_map/ppermute | solution.py:662
  427.8 12.1 %shard_map.466 = (f32[128,1024]{1,0:T(8,128)}, f32[1,1024]{1,0:T(1,128)}, f32[128,1024]{1,0:T(8,128)}, f32[128,1024]{1,0:T(8,128)}) custom-call(f32[128,1024]{1,0:T(8,128)} %get-tuple-element.246.base_ref, f32[128,1024]{1,0:T(8,128)} %bitcast.439, f32[128,1024]{1,0:T(8,128)} %bitcast.419, f32[1,1024]{1,0:T(1,128)} %gain_ref.7, ...), custom_call_target="tpu_custom_call" | custom-call | flops 1610612736 | bytes 8388608 | tf_op jit(solution)/shard_map/pallas_call | solution.py:185
  444.1 2.7 collective-permute-done.60
  447.5 5.1 collective-permute-done.58
  460.6 2.5 collective-permute-start.62
  463.8 7.4 %collective-permute-done.62 = f32[32,1024]{1,0:T(8,128)S(1)} collective-permute-done((f32[32,1024]{1,0:T(8,128)S(1)}, f32[32,1024]{1,0:T(8,128)S(1)}, u32[]{:S(2)}, u32[]{:S(2)}) %collective-permute-start.62) | collective-permute-done | bytes 131104 | tf_op jit(solution)/shard_map/ppermute | solution.py:662
  471.2 2.7 collective-permute-done.63
  478.3 15.2 %shard_map.467 = (f32[128,1024]{1,0:T(8,128)}, f32[1,1024]{1,0:T(1,128)}, f32[128,256]{1,0:T(8,128)}, f32[1024,512]{1,0:T(8,128)}, f32[128,1024]{1,0:T(8,128)}, ...) custom-call(f32[128,1024]{1,0:T(8,128)} %get-tuple-element.291.base_, ...), custom_call_target="tpu_custom_call" | custom-call | flops 3000000 | bytes 1000000 | tf_op jit(solution)/shard_map/pallas_call | solution.py:61
  496.8 2.6 collective-permute-start.75
  499.5 4.1 collective-permute-done.64
  514.6 5.0 collective-permute-done.71
  522.5 4.2 collective-permute-done.67
  527.8 11.3 %fusion.9 = f32[1024,1024]{1,0:T(8,128)} fusion(f32[1024,3328]{1,0:T(8,128)} %all-gather.16.cloned.1.call-done, f32[1024,3072]{1,0:T(8,128)} %all-gather.14.cloned.1.call-done), kind=kOutput, calls=%fused_computation.9 | convolution fusion | flops 6442450944 | bytes 12582912 | tf_op jit(solution)/shard_map/dot_general | solution.py:28
  539.1 2.7 slice.228
  552.2 8.4 %fusion.7 = f32[1024,1024]{1,0:T(8,128)} fusion(f32[1024,1024]{1,0:T(8,128)S(1)} %slice-done.2, f32[1024,3328]{1,0:T(8,128)S(1)} %copy-done.23), kind=kOutput, calls=%fused_computation.7 | convolution fusion | flops 6442450944 | bytes 12582912 | tf_op jit(solution)/shard_map/dot_general | solution.py:28
  561.0 10.0 %collective-permute-done.79 = f32[2,96,512]{2,1,0:T(8,128)S(1)} collective-permute-done((f32[2,96,512]{2,1,0:T(8,128)S(1)}, f32[2,96,512]{2,1,0:T(8,128)S(1)}, u32[]{:S(2)}, u32[]{:S(2)}) %collective-permute-start.79) | collective-permute-done | bytes 393248 | tf_op jit(solution)/shard_map/ppermute | solution.py:714
  571.1 6.9 all-gather.18.cloned.1.call-done
  579.8 9.6 %fusion.5 = f32[1024,768]{1,0:T(8,128)} fusion(f32[1024,3072]{1,0:T(8,128)} %all-gather.14.cloned.1.call-done, f32[1024,2816]{1,0:T(8,128)} %all-gather.18.cloned.1.call-done), kind=kOutput, calls=%fused_computation.5 | convolution fusion | flops 4831838208 | bytes 10485760 | tf_op jit(solution)/shard_map/dot_general | solution.py:28
  589.4 4.8 slice.242
  597.7 2.4 collective-permute-done.81
  608.7 5.9 fusion.13
  614.8 13.7 %collective-permute-done.90 = f32[32,1024]{1,0:T(8,128)S(1)} collective-permute-done((f32[32,1024]{1,0:T(8,128)S(1)}, f32[32,1024]{1,0:T(8,128)S(1)}, u32[]{:S(2)}, u32[]{:S(2)}) %collective-permute-start.90) | collective-permute-done | bytes 131104 | tf_op jit(solution)/shard_map/ppermute | solution.py:662
  628.5 2.4 collective-permute-done.91
  631.0 11.3 %fusion.2 = f32[1024,1024]{1,0:T(8,128)} fusion(f32[1024,2816]{1,0:T(8,128)} %all-gather.18.cloned.1.call-done, f32[1024,2048]{1,0:T(8,128)} %all-gather.12.cloned.1.call-done), kind=kOutput, calls=%fused_computation.2 | convolution fusion | flops 6442450944 | bytes 12582912 | tf_op jit(solution)/shard_map/dot_general | solution.py:28
  642.3 6.9 shard_map.468
  651.1 11.1 %fusion = f32[1024,1024]{1,0:T(8,128)} fusion(f32[1024,1024]{1,0:T(8,128)} %slice.242, f32[1024,2048]{1,0:T(8,128)} %all-gather.12.cloned.1.call-done), kind=kOutput, calls=%fused_computation | convolution fusion | flops 6442450944 | bytes 12582912 | tf_op jit(solution)/shard_map/dot_general | solution.py:28
  662.2 3.5 copy.108
  665.8 3.8 copy.111
  (521 shorter events, 227.8 us)
Async XLA Ops:
  7.3 59.3 %all-gather.10.cloned.1.call-start = ((), (), s32[]{:S(2)}) async-start(), calls=%async_computation.1 | async-start | bytes 4718592 | tf_op jit(solution)/shard_map/all_gather | solution.py:708
  11.9 128.2 %all-gather.20.cloned.1.call-start = ((), (), s32[]{:S(2)}) async-start(), calls=%async_computation.6 | async-start | bytes 2293760 | tf_op jit(solution)/shard_map/all_gather | solution.py:793
  15.3 14.1 %collective-permute-start = (f32[264,512]{1,0:T(8,128)}, f32[264,512]{1,0:T(8,128)}, u32[]{:S(2)}, u32[]{:S(2)}) collective-permute-start(f32[264,512]{1,0:T(8,128)} %pad_maximum_fusion.8), channel_id=1, source_target_pairs={{0,1},{1,2},{2,3},{3,0},{4,5},{5,6},{6,7},{7,4},{8,9},{9,10},{10,1... | collective-permute-start | bytes 1622024 | tf_op jit(solution)/shard_map/ppermute | solution.py:662
  16.6 46.0 %collective-permute-start.1 = (f32[264,512]{1,0:T(8,128)}, f32[264,512]{1,0:T(8,128)}, u32[]{:S(2)}, u32[]{:S(2)}) collective-permute-start(f32[264,512]{1,0:T(8,128)} %pad_maximum_fusion.8), channel_id=1, source_target_pairs={{0,2},{1,3},{2,0},{3,1},{4,6},{5,7},{6,4},{7,5},{8,10},{9,11},{10,... | collective-permute-start | bytes 1622024 | tf_op jit(solution)/shard_map/ppermute | solution.py:662
  17.6 47.8 %collective-permute-start.2 = (f32[264,512]{1,0:T(8,128)}, f32[264,512]{1,0:T(8,128)}, u32[]{:S(2)}, u32[]{:S(2)}) collective-permute-start(f32[264,512]{1,0:T(8,128)} %pad_maximum_fusion.8), channel_id=1, source_target_pairs={{0,3},{1,0},{2,1},{3,2},{4,7},{5,4},{6,5},{7,6},{8,11},{9,8},{10,9... | collective-permute-start | bytes 1622024 | tf_op jit(solution)/shard_map/ppermute | solution.py:662
  67.8 321.7 %all-gather.12.cloned.1.call-start = ((), (), s32[]{:S(2)}) async-start(), calls=%async_computation.2 | async-start | bytes 9437184 | tf_op jit(solution)/shard_map/all_gather | solution.py:708
  80.4 14.6 %collective-permute-start.5 = (f32[32,1024]{1,0:T(8,128)S(1)}, f32[32,1024]{1,0:T(8,128)S(1)}, u32[]{:S(2)}, u32[]{:S(2)}) collective-permute-start(f32[32,1024]{1,0:T(8,128)S(1)} %get-tuple-element.510), channel_id=1, source_target_pairs={{0,3},{1,0},{2,1},{3,2},{4,7},{5,4},{6,5},{7,6},{8,11},{9,8},{10,9... | collective-permute-start | bytes 393224 | tf_op jit(solution)/shard_map/ppermute | solution.py:662
  80.4 17.1 %collective-permute-start.4 = (f32[32,1024]{1,0:T(8,128)S(1)}, f32[32,1024]{1,0:T(8,128)S(1)}, u32[]{:S(2)}, u32[]{:S(2)}) collective-permute-start(f32[32,1024]{1,0:T(8,128)S(1)} %get-tuple-element.511), channel_id=1, source_target_pairs={{0,2},{1,3},{2,0},{3,1},{4,6},{5,7},{6,4},{7,5},{8,10},{9,11},{10,... | collective-permute-start | bytes 393224 | tf_op jit(solution)/shard_map/ppermute | solution.py:662
  81.8 24.2 %collective-permute-start.3 = (f32[32,1024]{1,0:T(8,128)S(1)}, f32[32,1024]{1,0:T(8,128)S(1)}, u32[]{:S(2)}, u32[]{:S(2)}) collective-permute-start(f32[32,1024]{1,0:T(8,128)S(1)} %get-tuple-element.509), channel_id=1, source_target_pairs={{0,1},{1,2},{2,3},{3,0},{4,5},{5,6},{6,7},{7,4},{8,9},{9,10},{10,1... | collective-permute-start | bytes 393224 | tf_op jit(solution)/shard_map/ppermute | solution.py:662
  107.0 13.2 %collective-permute-start.6 = (f32[32,1024]{1,0:T(8,128)S(1)}, f32[32,1024]{1,0:T(8,128)S(1)}, u32[]{:S(2)}, u32[]{:S(2)}) collective-permute-start(f32[32,1024]{1,0:T(8,128)S(1)} %bitcast_add_fusion.15), channel_id=1, source_target_pairs={{0,1},{1,2},{2,3},{3,0},{4,5},{5,6},{6,7},{7,4},{8,9},{9,10},{10,1... | collective-permute-start | bytes 393224 | tf_op jit(solution)/shard_map/ppermute | solution.py:662
  110.9 18.3 %collective-permute-start.7 = (f32[32,1024]{1,0:T(8,128)S(1)}, f32[32,1024]{1,0:T(8,128)S(1)}, u32[]{:S(2)}, u32[]{:S(2)}) collective-permute-start(f32[32,1024]{1,0:T(8,128)S(1)} %bitcast_add_fusion.15), channel_id=1, source_target_pairs={{0,2},{1,3},{2,0},{3,1},{4,6},{5,7},{6,4},{7,5},{8,10},{9,11},{10,... | collective-permute-start | bytes 393224 | tf_op jit(solution)/shard_map/ppermute | solution.py:662
  112.7 18.9 %collective-permute-start.8 = (f32[32,1024]{1,0:T(8,128)S(1)}, f32[32,1024]{1,0:T(8,128)S(1)}, u32[]{:S(2)}, u32[]{:S(2)}) collective-permute-start(f32[32,1024]{1,0:T(8,128)S(1)} %bitcast_add_fusion.15), channel_id=1, source_target_pairs={{0,3},{1,0},{2,1},{3,2},{4,7},{5,4},{6,5},{7,6},{8,11},{9,8},{10,9... | collective-permute-start | bytes 393224 | tf_op jit(solution)/shard_map/ppermute | solution.py:662
  140.1 42.0 %collective-permute-start.15 = (f32[4,448,256]{2,1,0:T(8,128)}, f32[4,448,256]{2,1,0:T(8,128)S(1)}, u32[]{:S(2)}, u32[]{:S(2)}) collective-permute-start(f32[4,448,256]{2,1,0:T(8,128)} %bitcast.504), channel_id=1, source_target_pairs={{0,8},{4,12},{8,0},{12,4},{16,24},{20,28},{24,16},{28,20},{1,9},{5... | collective-permute-start | bytes 5505032 | tf_op jit(solution)/shard_map/ppermute | solution.py:714
  141.4 41.0 %collective-permute-start.16 = (f32[4,448,256]{2,1,0:T(8,128)}, f32[4,448,256]{2,1,0:T(8,128)}, u32[]{:S(2)}, u32[]{:S(2)}) collective-permute-start(f32[4,448,256]{2,1,0:T(8,128)} %bitcast.505), channel_id=1, source_target_pairs={{0,16},{4,20},{8,24},{12,28},{16,0},{20,4},{24,8},{28,12},{1,17},{... | collective-permute-start | bytes 5505032 | tf_op jit(solution)/shard_map/ppermute | solution.py:714
  143.5 10.8 %collective-permute-start.9 = (f32[32,1024]{1,0:T(8,128)S(1)}, f32[32,1024]{1,0:T(8,128)S(1)}, u32[]{:S(2)}, u32[]{:S(2)}) collective-permute-start(f32[32,1024]{1,0:T(8,128)S(1)} %get-tuple-element.506), channel_id=1, source_target_pairs={{0,1},{1,2},{2,3},{3,0},{4,5},{5,6},{6,7},{7,4},{8,9},{9,10},{10,1... | collective-permute-start | bytes 393224 | tf_op jit(solution)/shard_map/ppermute | solution.py:662
  155.3 16.5 %collective-permute-start.12 = (f32[32,1024]{1,0:T(8,128)S(1)}, f32[32,1024]{1,0:T(8,128)S(1)}, u32[]{:S(2)}, u32[]{:S(2)}) collective-permute-start(f32[32,1024]{1,0:T(8,128)S(1)} %fusion.43), channel_id=1, source_target_pairs={{0,1},{1,2},{2,3},{3,0},{4,5},{5,6},{6,7},{7,4},{8,9},{9,10},{10,1... | collective-permute-start | bytes 393224 | tf_op jit(solution)/shard_map/ppermute | solution.py:662
  157.7 14.2 %collective-permute-start.13 = (f32[32,1024]{1,0:T(8,128)S(1)}, f32[32,1024]{1,0:T(8,128)S(1)}, u32[]{:S(2)}, u32[]{:S(2)}) collective-permute-start(f32[32,1024]{1,0:T(8,128)S(1)} %fusion.43), channel_id=1, source_target_pairs={{0,2},{1,3},{2,0},{3,1},{4,6},{5,7},{6,4},{7,5},{8,10},{9,11},{10,... | collective-permute-start | bytes 393224 | tf_op jit(solution)/shard_map/ppermute | solution.py:662
  159.6 16.3 %collective-permute-start.14 = (f32[32,1024]{1,0:T(8,128)S(1)}, f32[32,1024]{1,0:T(8,128)S(1)}, u32[]{:S(2)}, u32[]{:S(2)}) collective-permute-start(f32[32,1024]{1,0:T(8,128)S(1)} %fusion.43), channel_id=1, source_target_pairs={{0,3},{1,0},{2,1},{3,2},{4,7},{5,4},{6,5},{7,6},{8,11},{9,8},{10,9... | collective-permute-start | bytes 393224 | tf_op jit(solution)/shard_map/ppermute | solution.py:662
  185.6 10.8 %collective-permute-start.17 = (f32[32,1024]{1,0:T(8,128)S(1)}, f32[32,1024]{1,0:T(8,128)S(1)}, u32[]{:S(2)}, u32[]{:S(2)}) collective-permute-start(f32[32,1024]{1,0:T(8,128)S(1)} %get-tuple-element.503), channel_id=1, source_target_pairs={{0,1},{1,2},{2,3},{3,0},{4,5},{5,6},{6,7},{7,4},{8,9},{9,10},{10,1... | collective-permute-start | bytes 393224 | tf_op jit(solution)/shard_map/ppermute | solution.py:662
  189.0 31.5 %collective-permute-start.23 = (f32[4,256,256]{2,1,0:T(8,128)S(1)}, f32[4,256,256]{2,1,0:T(8,128)S(1)}, u32[]{:S(2)}, u32[]{:S(2)}) collective-permute-start(f32[4,256,256]{2,1,0:T(8,128)S(1)} %slice.219), channel_id=1, source_target_pairs={{0,16},{4,20},{8,24},{12,28},{16,0},{20,4},{24,8},{28,12},{1,17},{... | collective-permute-start | bytes 3145736 | tf_op jit(solution)/shard_map/ppermute | solution.py:714
  191.5 29.1 %collective-permute-start.24 = (f32[4,192,256]{2,1,0:T(8,128)S(1)}, f32[4,192,256]{2,1,0:T(8,128)S(1)}, u32[]{:S(2)}, u32[]{:S(2)}) collective-permute-start(f32[4,192,256]{2,1,0:T(8,128)S(1)} %slice.220), channel_id=1, source_target_pairs={{0,8},{4,12},{8,0},{12,4},{16,24},{20,28},{24,16},{28,20},{1,9},{5... | collective-permute-start | bytes 2359304 | tf_op jit(solution)/shard_map/ppermute | solution.py:714
  200.2 11.7 %collective-permute-start.22 = (f32[32,1024]{1,0:T(8,128)S(1)}, f32[32,1024]{1,0:T(8,128)S(1)}, u32[]{:S(2)}, u32[]{:S(2)}) collective-permute-start(f32[32,1024]{1,0:T(8,128)S(1)} %fusion.40), channel_id=1, source_target_pairs={{0,3},{1,0},{2,1},{3,2},{4,7},{5,4},{6,5},{7,6},{8,11},{9,8},{10,9... | collective-permute-start | bytes 393224 | tf_op jit(solution)/shard_map/ppermute | solution.py:662
  222.4 204.6 %all-gather.14.cloned.1.call-start = ((), (), s32[]{:S(2)}) async-start(), calls=%async_computation.3 | async-start | bytes 14155776 | tf_op jit(solution)/shard_map/all_gather | solution.py:708
  224.4 10.8 %collective-permute-start.25 = (f32[32,1024]{1,0:T(8,128)S(1)}, f32[32,1024]{1,0:T(8,128)S(1)}, u32[]{:S(2)}, u32[]{:S(2)}) collective-permute-start(f32[32,1024]{1,0:T(8,128)S(1)} %get-tuple-element.500), channel_id=1, source_target_pairs={{0,1},{1,2},{2,3},{3,0},{4,5},{5,6},{6,7},{7,4},{8,9},{9,10},{10,1... | collective-permute-start | bytes 393224 | tf_op jit(solution)/shard_map/ppermute | solution.py:662
  238.7 235.2 %reduce-scatter.4.cloned.1.call-start = ((), (), s32[]{:S(2)}) async-start(), calls=%async_computation.8 | async-start | bytes 6553600
  238.8 22.1 %collective-permute-start.31 = (f32[4,448,256]{2,1,0:T(8,128)}, f32[4,448,256]{2,1,0:T(8,128)}, u32[]{:S(2)}, u32[]{:S(2)}) collective-permute-start(f32[4,448,256]{2,1,0:T(8,128)} %bitcast.506), channel_id=1, source_target_pairs={{0,4},{4,0},{8,12},{12,8},{16,20},{20,16},{24,28},{28,24},{1,5},{5... | collective-permute-start | bytes 5505032 | tf_op jit(solution)/shard_map/ppermute | solution.py:714
  240.2 20.7 %collective-permute-start.32 = (f32[4,448,256]{2,1,0:T(8,128)S(1)}, f32[4,448,256]{2,1,0:T(8,128)}, u32[]{:S(2)}, u32[]{:S(2)}) collective-permute-start(f32[4,448,256]{2,1,0:T(8,128)S(1)} %collective-permute-done.15.refs_9_), channel_id=1, source_target_pairs={{0,4},{4,0},{8,12},{12,8},{16,20},{20,16},{24,28},{28,24},{1,5},{5... | collective-permute-start | bytes 5505032 | tf_op jit(solution)/shard_map/ppermute | solution.py:714
  240.3 20.6 %collective-permute-start.33 = (f32[4,448,256]{2,1,0:T(8,128)}, f32[4,448,256]{2,1,0:T(8,128)}, u32[]{:S(2)}, u32[]{:S(2)}) collective-permute-start(f32[4,448,256]{2,1,0:T(8,128)} %collective-permute-done.16.refs_10_), channel_id=1, source_target_pairs={{0,4},{4,0},{8,12},{12,8},{16,20},{20,16},{24,28},{28,24},{1,5},{5... | collective-permute-start | bytes 5505032 | tf_op jit(solution)/shard_map/ppermute | solution.py:714
  247.1 13.8 %collective-permute-start.34 = (f32[4,256,256]{2,1,0:T(8,128)}, f32[4,256,256]{2,1,0:T(8,128)}, u32[]{:S(2)}, u32[]{:S(2)}) collective-permute-start(f32[4,256,256]{2,1,0:T(8,128)} %copy-done.64), channel_id=1, source_target_pairs={{0,4},{4,0},{8,12},{12,8},{16,20},{20,16},{24,28},{28,24},{1,5},{5... | collective-permute-start | bytes 3145736 | tf_op jit(solution)/shard_map/ppermute | solution.py:714
  305.4 11.0 %collective-permute-start.36 = (f32[32,1024]{1,0:T(8,128)S(1)}, f32[32,1024]{1,0:T(8,128)S(1)}, u32[]{:S(2)}, u32[]{:S(2)}) collective-permute-start(f32[32,1024]{1,0:T(8,128)S(1)} %get-tuple-element.497), channel_id=1, source_target_pairs={{0,1},{1,2},{2,3},{3,0},{4,5},{5,6},{6,7},{7,4},{8,9},{9,10},{10,1... | collective-permute-start | bytes 393224 | tf_op jit(solution)/shard_map/ppermute | solution.py:662
  317.3 16.4 %collective-permute-start.39 = (f32[32,1024]{1,0:T(8,128)S(1)}, f32[32,1024]{1,0:T(8,128)S(1)}, u32[]{:S(2)}, u32[]{:S(2)}) collective-permute-start(f32[32,1024]{1,0:T(8,128)S(1)} %fusion.34), channel_id=1, source_target_pairs={{0,1},{1,2},{2,3},{3,0},{4,5},{5,6},{6,7},{7,4},{8,9},{9,10},{10,1... | collective-permute-start | bytes 393224 | tf_op jit(solution)/shard_map/ppermute | solution.py:662
  319.7 14.1 %collective-permute-start.40 = (f32[32,1024]{1,0:T(8,128)S(1)}, f32[32,1024]{1,0:T(8,128)S(1)}, u32[]{:S(2)}, u32[]{:S(2)}) collective-permute-start(f32[32,1024]{1,0:T(8,128)S(1)} %fusion.34), channel_id=1, source_target_pairs={{0,2},{1,3},{2,0},{3,1},{4,6},{5,7},{6,4},{7,5},{8,10},{9,11},{10,... | collective-permute-start | bytes 393224 | tf_op jit(solution)/shard_map/ppermute | solution.py:662
  321.0 12.7 %collective-permute-start.41 = (f32[32,1024]{1,0:T(8,128)S(1)}, f32[32,1024]{1,0:T(8,128)S(1)}, u32[]{:S(2)}, u32[]{:S(2)}) collective-permute-start(f32[32,1024]{1,0:T(8,128)S(1)} %fusion.34), channel_id=1, source_target_pairs={{0,3},{1,0},{2,1},{3,2},{4,7},{5,4},{6,5},{7,6},{8,11},{9,8},{10,9... | collective-permute-start | bytes 393224 | tf_op jit(solution)/shard_map/ppermute | solution.py:662
  333.8 18.4 %collective-permute-start.42 = (f32[4,1280,256]{2,1,0:T(8,128)}, f32[4,1280,256]{2,1,0:T(8,128)}, u32[]{:S(2)}, u32[]{:S(2)}) collective-permute-start(f32[4,1280,256]{2,1,0:T(8,128)} %bitcast.503), channel_id=1, source_target_pairs={{0,4},{4,0},{8,12},{12,8},{16,20},{20,16},{24,28},{28,24},{1,5},{5... | collective-permute-start | bytes 15728648 | tf_op jit(solution)/shard_map/ppermute | solution.py:714
  336.6 15.5 %collective-permute-start.45 = (f32[128,256]{1,0:T(8,128)S(1)}, f32[128,256]{1,0:T(8,128)S(1)}, u32[]{:S(2)}, u32[]{:S(2)}) collective-permute-start(f32[128,256]{1,0:T(8,128)S(1)} %get-tuple-element.495), channel_id=1, source_target_pairs={{0,3},{1,0},{2,1},{3,2},{4,7},{5,4},{6,5},{7,6},{8,11},{9,8},{10,9... | collective-permute-start | bytes 393224 | tf_op jit(solution)/shard_map/ppermute | solution.py:662
  339.4 12.7 %collective-permute-start.44 = (f32[128,256]{1,0:T(8,128)S(1)}, f32[128,256]{1,0:T(8,128)S(1)}, u32[]{:S(2)}, u32[]{:S(2)}) collective-permute-start(f32[128,256]{1,0:T(8,128)S(1)} %get-tuple-element.496), channel_id=1, source_target_pairs={{0,2},{1,3},{2,0},{3,1},{4,6},{5,7},{6,4},{7,5},{8,10},{9,11},{10,... | collective-permute-start | bytes 393224 | tf_op jit(solution)/shard_map/ppermute | solution.py:662
  340.0 12.1 %collective-permute-start.43 = (f32[128,256]{1,0:T(8,128)S(1)}, f32[128,256]{1,0:T(8,128)S(1)}, u32[]{:S(2)}, u32[]{:S(2)}) collective-permute-start(f32[128,256]{1,0:T(8,128)S(1)} %get-tuple-element.494), channel_id=1, source_target_pairs={{0,1},{1,2},{2,3},{3,0},{4,5},{5,6},{6,7},{7,4},{8,9},{9,10},{10,1... | collective-permute-start | bytes 393224 | tf_op jit(solution)/shard_map/ppermute | solution.py:662
  357.8 170.1 %all-gather.16.cloned.1.call-start = ((), (), s32[]{:S(2)}) async-start(), calls=%async_computation.4 | async-start | bytes 15335424 | tf_op jit(solution)/shard_map/all_gather | solution.py:708
  361.4 11.5 %collective-permute-start.46 = (f32[32,1024]{1,0:T(8,128)S(1)}, f32[32,1024]{1,0:T(8,128)S(1)}, u32[]{:S(2)}, u32[]{:S(2)}) collective-permute-start(f32[32,1024]{1,0:T(8,128)S(1)} %get-tuple-element.491), channel_id=1, source_target_pairs={{0,1},{1,2},{2,3},{3,0},{4,5},{5,6},{6,7},{7,4},{8,9},{9,10},{10,1... | collective-permute-start | bytes 393224 | tf_op jit(solution)/shard_map/ppermute | solution.py:662
  374.3 203.7 %all-gather.18.cloned.1.call-start = ((), (), s32[]{:S(2)}) async-start(), calls=%async_computation.5 | async-start | bytes 12976128 | tf_op jit(solution)/shard_map/all_gather | solution.py:708
  376.7 10.9 %collective-permute-start.50 = (f32[32,1024]{1,0:T(8,128)S(1)}, f32[32,1024]{1,0:T(8,128)S(1)}, u32[]{:S(2)}, u32[]{:S(2)}) collective-permute-start(f32[32,1024]{1,0:T(8,128)S(1)} %fusion.30), channel_id=1, source_target_pairs={{0,2},{1,3},{2,0},{3,1},{4,6},{5,7},{6,4},{7,5},{8,10},{9,11},{10,... | collective-permute-start | bytes 393224 | tf_op jit(solution)/shard_map/ppermute | solution.py:662
  377.2 12.2 %collective-permute-start.51 = (f32[32,1024]{1,0:T(8,128)S(1)}, f32[32,1024]{1,0:T(8,128)S(1)}, u32[]{:S(2)}, u32[]{:S(2)}) collective-permute-start(f32[32,1024]{1,0:T(8,128)S(1)} %fusion.30), channel_id=1, source_target_pairs={{0,3},{1,0},{2,1},{3,2},{4,7},{5,4},{6,5},{7,6},{8,11},{9,8},{10,9... | collective-permute-start | bytes 393224 | tf_op jit(solution)/shard_map/ppermute | solution.py:662
  400.5 10.8 %collective-permute-start.52 = (f32[32,1024]{1,0:T(8,128)S(1)}, f32[32,1024]{1,0:T(8,128)S(1)}, u32[]{:S(2)}, u32[]{:S(2)}) collective-permute-start(f32[32,1024]{1,0:T(8,128)S(1)} %get-tuple-element.488), channel_id=1, source_target_pairs={{0,1},{1,2},{2,3},{3,0},{4,5},{5,6},{6,7},{7,4},{8,9},{9,10},{10,1... | collective-permute-start | bytes 393224 | tf_op jit(solution)/shard_map/ppermute | solution.py:662
  416.3 10.7 %collective-permute-start.57 = (f32[32,1024]{1,0:T(8,128)S(1)}, f32[32,1024]{1,0:T(8,128)S(1)}, u32[]{:S(2)}, u32[]{:S(2)}) collective-permute-start(f32[32,1024]{1,0:T(8,128)S(1)} %fusion.28), channel_id=1, source_target_pairs={{0,3},{1,0},{2,1},{3,2},{4,7},{5,4},{6,5},{7,6},{8,11},{9,8},{10,9... | collective-permute-start | bytes 393224 | tf_op jit(solution)/shard_map/ppermute | solution.py:662
  441.8 10.8 %collective-permute-start.58 = (f32[32,1024]{1,0:T(8,128)S(1)}, f32[32,1024]{1,0:T(8,128)S(1)}, u32[]{:S(2)}, u32[]{:S(2)}) collective-permute-start(f32[32,1024]{1,0:T(8,128)S(1)} %get-tuple-element.485), channel_id=1, source_target_pairs={{0,1},{1,2},{2,3},{3,0},{4,5},{5,6},{6,7},{7,4},{8,9},{9,10},{10,1... | collective-permute-start | bytes 393224 | tf_op jit(solution)/shard_map/ppermute | solution.py:662
  455.9 220.5 %all-gather.22.cloned.1.call-start = ((), (), s32[]{:S(2)}) async-start(), calls=%async_computation.7 | async-start | bytes 6488064 | tf_op jit(solution)/shard_map/all_gather | solution.py:1011
  460.6 10.6 %collective-permute-start.62 = (f32[32,1024]{1,0:T(8,128)S(1)}, f32[32,1024]{1,0:T(8,128)S(1)}, u32[]{:S(2)}, u32[]{:S(2)}) collective-permute-start(f32[32,1024]{1,0:T(8,128)S(1)} %fusion.26), channel_id=1, source_target_pairs={{0,2},{1,3},{2,0},{3,1},{4,6},{5,7},{6,4},{7,5},{8,10},{9,11},{10,... | collective-permute-start | bytes 393224 | tf_op jit(solution)/shard_map/ppermute | solution.py:662
  463.1 10.8 %collective-permute-start.63 = (f32[32,1024]{1,0:T(8,128)S(1)}, f32[32,1024]{1,0:T(8,128)S(1)}, u32[]{:S(2)}, u32[]{:S(2)}) collective-permute-start(f32[32,1024]{1,0:T(8,128)S(1)} %fusion.26), channel_id=1, source_target_pairs={{0,3},{1,0},{2,1},{3,2},{4,7},{5,4},{6,5},{7,6},{8,11},{9,8},{10,9... | collective-permute-start | bytes 393224 | tf_op jit(solution)/shard_map/ppermute | solution.py:662
  475.3 24.1 %collective-permute-start.66 = (f32[320,256]{1,0:T(8,128)S(1)}, f32[320,256]{1,0:T(8,128)S(1)}, u32[]{:S(2)}, u32[]{:S(2)}) collective-permute-start(f32[320,256]{1,0:T(8,128)S(1)} %get-tuple-element.476), channel_id=1, source_target_pairs={{0,3},{1,0},{2,1},{3,2},{4,7},{5,4},{6,5},{7,6},{8,11},{9,8},{10,9... | collective-permute-start | bytes 983048 | tf_op jit(solution)/shard_map/ppermute | solution.py:662
  475.4 24.1 %collective-permute-start.65 = (f32[320,256]{1,0:T(8,128)S(1)}, f32[320,256]{1,0:T(8,128)S(1)}, u32[]{:S(2)}, u32[]{:S(2)}) collective-permute-start(f32[320,256]{1,0:T(8,128)S(1)} %get-tuple-element.477), channel_id=1, source_target_pairs={{0,2},{1,3},{2,0},{3,1},{4,6},{5,7},{6,4},{7,5},{8,10},{9,11},{10,... | collective-permute-start | bytes 983048 | tf_op jit(solution)/shard_map/ppermute | solution.py:662
  475.9 27.7 %collective-permute-start.64 = (f32[320,256]{1,0:T(8,128)S(1)}, f32[320,256]{1,0:T(8,128)S(1)}, u32[]{:S(2)}, u32[]{:S(2)}) collective-permute-start(f32[320,256]{1,0:T(8,128)S(1)} %get-tuple-element.475), channel_id=1, source_target_pairs={{0,1},{1,2},{2,3},{3,0},{4,5},{5,6},{6,7},{7,4},{8,9},{9,10},{10,1... | collective-permute-start | bytes 983048 | tf_op jit(solution)/shard_map/ppermute | solution.py:662
  496.8 45.0 %collective-permute-start.75 = (f32[4,192,512]{2,1,0:T(8,128)}, f32[4,192,512]{2,1,0:T(8,128)}, u32[]{:S(2)}, u32[]{:S(2)}) collective-permute-start(f32[4,192,512]{2,1,0:T(8,128)} %get-tuple-element.462), channel_id=1, source_target_pairs={{0,4},{4,0},{8,12},{12,8},{16,20},{20,16},{24,28},{28,24},{1,5},{5... | collective-permute-start | bytes 4718600 | tf_op jit(solution)/shard_map/ppermute | solution.py:714
  520.9 20.9 %collective-permute-start.73 = (f32[128,384]{1,0:T(8,128)S(1)}, f32[128,384]{1,0:T(8,128)}, u32[]{:S(2)}, u32[]{:S(2)}) collective-permute-start(f32[128,384]{1,0:T(8,128)S(1)} %select_maximum_fusion.refs_0_), channel_id=1, source_target_pairs={{0,8},{4,12},{8,0},{12,4},{16,24},{20,28},{24,16},{28,20},{1,9},{5... | collective-permute-start | bytes 589832 | tf_op jit(solution)/shard_map/ppermute | solution.py:714
  521.0 20.8 %collective-permute-start.74 = (f32[128,384]{1,0:T(8,128)S(1)}, f32[128,384]{1,0:T(8,128)}, u32[]{:S(2)}, u32[]{:S(2)}) collective-permute-start(f32[128,384]{1,0:T(8,128)S(1)} %select_maximum_fusion.refs_0_), channel_id=1, source_target_pairs={{0,16},{4,20},{8,24},{12,28},{16,0},{20,4},{24,8},{28,12},{1,17},{... | collective-permute-start | bytes 589832 | tf_op jit(solution)/shard_map/ppermute | solution.py:714
  542.9 28.2 %collective-permute-start.76 = (f32[256,512]{1,0:T(8,128)S(1)}, f32[256,512]{1,0:T(8,128)}, u32[]{:S(2)}, u32[]{:S(2)}) collective-permute-start(f32[256,512]{1,0:T(8,128)S(1)} %get-tuple-element.466), channel_id=1, source_target_pairs={{0,1},{1,2},{2,3},{3,0},{4,5},{5,6},{6,7},{7,4},{8,9},{9,10},{10,1... | collective-permute-start | bytes 1572872 | tf_op jit(solution)/shard_map/ppermute | solution.py:662
  546.0 14.6 %collective-permute-start.77 = (f32[64,384]{1,0:T(8,128)S(1)}, f32[64,384]{1,0:T(8,128)S(1)}, u32[]{:S(2)}, u32[]{:S(2)}) collective-permute-start(f32[64,384]{1,0:T(8,128)S(1)} %slice.234), channel_id=1, source_target_pairs={{0,16},{4,20},{8,24},{12,28},{16,0},{20,4},{24,8},{28,12},{1,17},{... | collective-permute-start | bytes 294920 | tf_op jit(solution)/shard_map/ppermute | solution.py:714
  548.1 12.9 %collective-permute-start.78 = (f32[64,384]{1,0:T(8,128)S(1)}, f32[64,384]{1,0:T(8,128)S(1)}, u32[]{:S(2)}, u32[]{:S(2)}) collective-permute-start(f32[64,384]{1,0:T(8,128)S(1)} %slice.235), channel_id=1, source_target_pairs={{0,8},{4,12},{8,0},{12,4},{16,24},{20,28},{24,16},{28,20},{1,9},{5... | collective-permute-start | bytes 294920 | tf_op jit(solution)/shard_map/ppermute | solution.py:714
  550.1 20.9 %collective-permute-start.79 = (f32[2,96,512]{2,1,0:T(8,128)S(1)}, f32[2,96,512]{2,1,0:T(8,128)S(1)}, u32[]{:S(2)}, u32[]{:S(2)}) collective-permute-start(f32[2,96,512]{2,1,0:T(8,128)S(1)} %get-tuple-element.469), channel_id=1, source_target_pairs={{0,8},{4,12},{8,0},{12,4},{16,24},{20,28},{24,16},{28,20},{1,9},{5... | collective-permute-start | bytes 1179656 | tf_op jit(solution)/shard_map/ppermute | solution.py:714
  551.6 19.4 %collective-permute-start.80 = (f32[2,96,512]{2,1,0:T(8,128)S(1)}, f32[2,96,512]{2,1,0:T(8,128)}, u32[]{:S(2)}, u32[]{:S(2)}) collective-permute-start(f32[2,96,512]{2,1,0:T(8,128)S(1)} %get-tuple-element.467), channel_id=1, source_target_pairs={{0,16},{4,20},{8,24},{12,28},{16,0},{20,4},{24,8},{28,12},{1,17},{... | collective-permute-start | bytes 1179656 | tf_op jit(solution)/shard_map/ppermute | solution.py:714
  560.6 41.0 %collective-permute-start.83 = (f32[256,512]{1,0:T(8,128)}, f32[256,512]{1,0:T(8,128)S(1)}, u32[]{:S(2)}, u32[]{:S(2)}) collective-permute-start(f32[256,512]{1,0:T(8,128)} %get-tuple-element.465), channel_id=1, source_target_pairs={{0,3},{1,0},{2,1},{3,2},{4,7},{5,4},{6,5},{7,6},{8,11},{9,8},{10,9... | collective-permute-start | bytes 1572872 | tf_op jit(solution)/shard_map/ppermute | solution.py:662
  579.0 17.3 %collective-permute-start.82 = (f32[96,512]{1,0:T(8,128)S(1)}, f32[96,512]{1,0:T(8,128)S(1)}, u32[]{:S(2)}, u32[]{:S(2)}) collective-permute-start(f32[96,512]{1,0:T(8,128)S(1)} %add_bitcast_fusion.4), channel_id=1, source_target_pairs={{0,8},{4,12},{8,0},{12,4},{16,24},{20,28},{24,16},{28,20},{1,9},{5... | collective-permute-start | bytes 589832 | tf_op jit(solution)/shard_map/ppermute | solution.py:714
  606.1 22.4 %collective-permute-start.90 = (f32[32,1024]{1,0:T(8,128)S(1)}, f32[32,1024]{1,0:T(8,128)S(1)}, u32[]{:S(2)}, u32[]{:S(2)}) collective-permute-start(f32[32,1024]{1,0:T(8,128)S(1)} %fusion.24), channel_id=1, source_target_pairs={{0,2},{1,3},{2,0},{3,1},{4,6},{5,7},{6,4},{7,5},{8,10},{9,11},{10,... | collective-permute-start | bytes 393224 | tf_op jit(solution)/shard_map/ppermute | solution.py:662
  607.3 23.7 %collective-permute-start.91 = (f32[32,1024]{1,0:T(8,128)S(1)}, f32[32,1024]{1,0:T(8,128)S(1)}, u32[]{:S(2)}, u32[]{:S(2)}) collective-permute-start(f32[32,1024]{1,0:T(8,128)S(1)} %fusion.24), channel_id=1, source_target_pairs={{0,3},{1,0},{2,1},{3,2},{4,7},{5,4},{6,5},{7,6},{8,11},{9,8},{10,9... | collective-permute-start | bytes 393224 | tf_op jit(solution)/shard_map/ppermute | solution.py:662
  608.5 53.7 %collective-permute-start.92 = (f32[256,512]{1,0:T(8,128)}, f32[256,512]{1,0:T(8,128)}, u32[]{:S(2)}, u32[]{:S(2)}) collective-permute-start(f32[256,512]{1,0:T(8,128)} %get-tuple-element.464), channel_id=1, source_target_pairs={{0,2},{1,3},{2,0},{3,1},{4,6},{5,7},{6,4},{7,5},{8,10},{9,11},{10,... | collective-permute-start | bytes 1572872 | tf_op jit(solution)/shard_map/ppermute | solution.py:662
  (117 other events, 1105.1 us)
Sparse Core Ops, SparseCore 0:
  12.0 38.0 all-gather.9
  67.9 60.9 all-gather.19
  222.5 54.5 all-gather.11
  278.9 71.9 all-gather.13
  357.9 60.8 reduce-scatter.3
  420.5 76.4 all-gather.15
  498.9 79.0 all-gather.17
  604.9 43.4 all-gather.21

commit v4 on v3

--- a/solution.py
+++ b/solution.py
@@ -986,9 +986,11 @@
         dkeyval = jnp.concatenate([grad.reshape(ds, -1, 2 * part) for grad in dkeyval], axis=1)
         dkeyval = dkeyval.reshape(4, 2, -1, 2 * part)
         pair = [pick(dkeyval, core, 1), swap(pick(dkeyval, 1 - core, 1), 1)]
-        half, dint_part, grad_layer_up, act3_all, normed4_all, *held = tie(
-            half, dint_part, grad_layer_up, act3_all, normed4_all, *late, *pair
+        half, dint_part, grad_layer_up, layer_all, write_all, *held = tie(
+            half, dint_part, grad_layer_up, layer_all, write_all, *late, *pair
         )
+        _, _, act3_all = cut_up(layer_all, [normed2, normed3, act3])
+        normed4_all, dkv_all, dstate4_all, _ = cut_up(write_all, [normed4, dkv_mine, dstate4, dpre3])
         late, pair = to_across(*held[:3]), scatter_one(*held[3:])
     dint_own, *dint_got = z_pieces(dint_part.reshape(zs, patches, wide))
     near, middle_got, far = dint_got[0], dint_got[1:-1], dint_got[-1]
@@ -1001,7 +1003,8 @@
     normed1_all, act1_all = cut_up(read_all, [normed1, act1])
     grad_layer_qkv, grad_read_up = tmm(normed2_all, dpacked_all), tmm(normed1_all, dpre1_all)
     if direct:
-        dkeyval, grad_layer_qkv, dstate2_all, far, *late = tie(dkeyval, grad_layer_qkv, dstate2_all, far, *late)
+        dkeyval, grad_layer_qkv, both_all, far, *late = tie(dkeyval, grad_layer_qkv, both_all, far, *late)
+        _, dstate2_all, _ = cut_up(both_all, [dpacked, dstate2, dpre1])
     grad_read_down = tmm(act1_all, dstate2_all)
     if direct:
         dlat, grad_write_keyval, grad_read_up, grad_read_down, *middle_got = tie(

time: 712 us -> 704 us (0.989)
  local copies, waits for them, and re-layouts: 88.4 us -> 80.2 us
    slice x4 -> x0, local copies, waits for them, and re-layouts: 7.69 us -> none  [cut_up(): out.append(full[:, at:at + part.shape[1]])]
    unnamed x177 -> x183, local copies, waits for them, and re-layouts: 25.7 us -> 25 us
  transfers between devices with their start and end apart: 101 -> 101, of which waited for: 52 -> 50; matrix products, arithmetic and copies ran while one was open for 22% -> 22% of each run, Pallas kernels for 19% -> 19%
where the time goes in v4:
time: 704 us; the launch traced here: 694 us
  waiting for transfers between devices  230 us (33%)
  Pallas kernels  134 us (19%)
  starting transfers between devices  125 us (18%)
  local copies, waits for them, and re-layouts  80.2 us (11%)
  matrix products  60.7 us (9%)
  other arithmetic  47.7 us (7%)
  between operations  16.6 us (2%)
    ppermute x69, waiting for transfers between devices, shift(): lax.ppermute(values, 'head', [(i, (i + step) % zs) for i in range(zs)])  207 us
    ppermute x69, starting transfers between devices, shift(): lax.ppermute(values, 'head', [(i, (i + step) % zs) for i in range(zs)])  104 us
    dot_general x7, matrix products, tmm(): lax.dot_general(left, right, (((0,), (0,)), ((), ())), precision=PRECISE)  59.7 us
    pallas_call x1, Pallas kernels, write_stage(): pl.pallas_call(call, out_shape=outs, in_specs=[vmem] * 7 + [pl.BlockSpec(...  38.8 us
    pallas_call x4, Pallas kernels, run_whole(): pl.pallas_call(kernel, out_shape=outs, in_specs=[pl.BlockSpec(memory_spac...  36.9 us
    unnamed x183, local copies, waits for them, and re-layouts  25 us
    pallas_call x2, Pallas kernels, ffn_backward(): pl.pallas_call(ffn_back_kernel, grid=(inner // tile,), out_shape=[shape_o...  23.5 us
    ppermute x24, starting transfers between devices, swap(): return lax.ppermute(values, 'dp', [(i, i ^ bits) for i in range(ds)])  20.7 us
  transfers between devices with their start and end apart: 101, of which 50 were waited for; matrix products, arithmetic and copies ran while one was open for 22% of the time, Pallas kernels for 19%

profile of v4, /device:TPU:13, one launch (start us, length us, event | category | flops | bytes accessed | tf_op | source)
XLA Modules:
  0.0 694.5 jit_solution(14539060970552574997)
XLA Ops:
  19.0 2.5 copy.95
  30.4 32.1 %collective-permute-done.1 = f32[264,512]{1,0:T(8,128)} collective-permute-done((f32[264,512]{1,0:T(8,128)}, f32[264,512]{1,0:T(8,128)}, u32[]{:S(2)}, u32[]{:S(2)}) %collective-permute-start.1) | collective-permute-done | bytes 540704 | tf_op jit(solution)/shard_map/ppermute | solution.py:662
  70.7 8.6 %shard_map.458 = (f32[1024,512]{1,0:T(8,128)}, f32[128,256]{1,0:T(8,128)}, f32[512,1024]{1,0:T(8,128)}, f32[128,1024]{1,0:T(8,128)}) custom-call(f32[128,256]{1,0:T(8,128)} %fusion.69.q_ref, f32[4,264,512]{2,1,0:T(8,128)} %copy-done.5, f32[1,512]{1,0:T(1,128)} %get-tuple-element.526.gain_ref.int_gain_ref, s32[1,1024]{1,0:T(1,128)} %seg_ref.1, ...), custom_call_target="tpu_custom_call" | custom-call | flops 3221225472 | bytes 9246720 | tf_op jit(solution)/shard_map/pallas_call | solution.py:61
  84.1 10.9 %collective-permute-done.5 = f32[32,1024]{1,0:T(8,128)S(1)} collective-permute-done((f32[32,1024]{1,0:T(8,128)S(1)}, f32[32,1024]{1,0:T(8,128)S(1)}, u32[]{:S(2)}, u32[]{:S(2)}) %collective-permute-start.5) | collective-permute-done | bytes 131104 | tf_op jit(solution)/shard_map/ppermute | solution.py:662
  95.0 2.5 collective-permute-done.4
  97.5 8.5 %collective-permute-done.3 = f32[32,1024]{1,0:T(8,128)S(1)} collective-permute-done((f32[32,1024]{1,0:T(8,128)S(1)}, f32[32,1024]{1,0:T(8,128)S(1)}, u32[]{:S(2)}, u32[]{:S(2)}) %collective-permute-start.3) | collective-permute-done | bytes 131104 | tf_op jit(solution)/shard_map/ppermute | solution.py:662
  107.0 3.8 collective-permute-start.6
  112.8 7.4 %collective-permute-done.6 = f32[32,1024]{1,0:T(8,128)S(1)} collective-permute-done((f32[32,1024]{1,0:T(8,128)S(1)}, f32[32,1024]{1,0:T(8,128)S(1)}, u32[]{:S(2)}, u32[]{:S(2)}) %collective-permute-start.6) | collective-permute-done | bytes 131104 | tf_op jit(solution)/shard_map/ppermute | solution.py:662
  120.2 9.0 %collective-permute-done.7 = f32[32,1024]{1,0:T(8,128)S(1)} collective-permute-done((f32[32,1024]{1,0:T(8,128)S(1)}, f32[32,1024]{1,0:T(8,128)S(1)}, u32[]{:S(2)}, u32[]{:S(2)}) %collective-permute-start.7) | collective-permute-done | bytes 131104 | tf_op jit(solution)/shard_map/ppermute | solution.py:662
  129.2 2.4 collective-permute-done.8
  132.5 7.6 %shard_map.459 = (f32[128,1024]{1,0:T(8,128)}, f32[128,1024]{1,0:T(8,128)}, f32[128,1024]{1,0:T(8,128)}, f32[128,1024]{1,0:T(8,128)}) custom-call(f32[128,1024]{1,0:T(8,128)} %bitcast.411, f32[1,1024]{1,0:T(1,128)} %bitcast.483, f32[1024,1024]{1,0:T(8,128)} %up_ref.3, f32[1024,1024]{1,0:T(8,128)} %down_ref.3), custom_call_target="tpu_custom_call" | custom-call | flops 1610612736 | bytes 8388608 | tf_op jit(solution)/shard_map/pallas_call | solution.py:142
  145.8 3.5 copy.101
  149.4 3.5 copy.102.qkv_ref
  159.6 12.1 %collective-permute-start.14 = (f32[32,1024]{1,0:T(8,128)S(1)}, f32[32,1024]{1,0:T(8,128)S(1)}, u32[]{:S(2)}, u32[]{:S(2)}) collective-permute-start(f32[32,1024]{1,0:T(8,128)S(1)} %fusion.46), channel_id=1, source_target_pairs={{0,3},{1,0},{2,1},{3,2},{4,7},{5,4},{6,5},{7,6},{8,11},{9,8},{10,9... | collective-permute-start | bytes 393224 | tf_op jit(solution)/shard_map/ppermute | solution.py:662
  171.9 4.0 collective-permute-done.14
  176.7 5.4 shard_map.460
  191.8 4.5 collective-permute-done.17
  201.8 8.1 %collective-permute-done.21 = f32[32,1024]{1,0:T(8,128)S(1)} collective-permute-done((f32[32,1024]{1,0:T(8,128)S(1)}, f32[32,1024]{1,0:T(8,128)S(1)}, u32[]{:S(2)}, u32[]{:S(2)}) %collective-permute-start.21) | collective-permute-done | bytes 131104 | tf_op jit(solution)/shard_map/ppermute | solution.py:662
  212.9 7.7 %shard_map.461 = (f32[128,1024]{1,0:T(8,128)}, f32[128,1024]{1,0:T(8,128)}, f32[128,1024]{1,0:T(8,128)}, f32[128,1024]{1,0:T(8,128)}) custom-call(f32[128,1024]{1,0:T(8,128)} %bitcast.417, f32[1,1024]{1,0:T(1,128)} %gain_ref.6, f32[1024,1024]{1,0:T(8,128)} %bitcast.400, f32[1024,1024]{1,0:T(8,128)} %bitcast.402), custom_call_target="tpu_custom_call" | custom-call | flops 1610612736 | bytes 8388608 | tf_op jit(solution)/shard_map/pallas_call | solution.py:142
  226.7 2.5 collective-permute-done.27
  230.2 5.0 collective-permute-done.25
  236.2 2.5 pad_maximum_fusion.1
  242.9 2.4 collective-permute-start.29
  248.0 3.8 collective-permute-done.29
  251.8 3.0 collective-permute-start.30
  261.8 38.8 %shard_map.462 = (f32[128,1024]{1,0:T(8,128)}, f32[256,512]{1,0:T(8,128)}, f32[256,512]{1,0:T(8,128)}, f32[256,512]{1,0:T(8,128)}, f32[256,512]{1,0:T(8,128)}, /...) custom-call(f32[128,1024]{1,0:T(8,128)} %bitcast.432, ...), custom_call_target="tpu_custom_call" | custom-call | flops 20000000000 | bytes 40000000 | tf_op jit(solution)/shard_map/pallas_call | solution.py:503
  307.6 5.7 collective-permute-done.37
  313.3 3.0 collective-permute-done.36
  321.0 12.6 %shard_map.463 = (f32[4,4,320,256]{3,2,1,0:T(8,128)}, f32[4,4,320,256]{3,2,1,0:T(8,128)}) custom-call(f32[256,512]{1,0:T(8,128)} %get-tuple-element.221.y_ref, f32[256,2048]{1,0:T(8,128)} %get-tuple-element.222.dpre_ref, f32[256,2048]{1,0:T(8,128)} %get-tuple-element.223.act_ref, f32[256,512]{1,0:T(8,128)} %bitcast.508, f32[256,512]{1,0:T(8,128)} %copy-done.10, ...), custom_call_target="tpu_custom_call" | custom-call | flops 10000000000 | bytes 20000000 | tf_op jit(solution)/shard_map/pallas_call | solution.py:558
  336.5 2.8 collective-permute-start.45
  340.6 11.4 %shard_map.464 = (f32[128,1024]{1,0:T(8,128)}, f32[1,1024]{1,0:T(1,128)}, f32[128,1024]{1,0:T(8,128)}, f32[128,1024]{1,0:T(8,128)}) custom-call(f32[128,1024]{1,0:T(8,128)} %bitcast.456, f32[128,1024]{1,0:T(8,128)} %bitcast.435, f32[128,1024]{1,0:T(8,128)} %bitcast.433, f32[1,1024]{1,0:T(1,128)} %bitcast.491, f32[128,1024]{1,0:T(8,128)} %get-tuple-element.231.pre_ref, ...), custom_call_target="tpu_custom_call" | custom-call | flops 1610612736 | bytes 8388608 | tf_op jit(solution)/shard_map/pallas_call | solution.py:185
  352.2 5.5 add.581
  363.3 6.8 collective-permute-done.47
  370.0 2.8 collective-permute-done.46
  379.7 7.9 %collective-permute-done.50 = f32[32,1024]{1,0:T(8,128)S(1)} collective-permute-done((f32[32,1024]{1,0:T(8,128)S(1)}, f32[32,1024]{1,0:T(8,128)S(1)}, u32[]{:S(2)}, u32[]{:S(2)}) %collective-permute-start.50) | collective-permute-done | bytes 131104 | tf_op jit(solution)/shard_map/ppermute | solution.py:662
  390.2 7.8 %shard_map.465 = (f32[128,1024]{1,0:T(8,128)}, f32[1,1024]{1,0:T(1,128)}, f32[128,768]{1,0:T(8,128)}, f32[128,1024]{1,0:T(8,128)}) custom-call(f32[128,1024]{1,0:T(8,128)} %get-tuple-element.280.base_ref, f32[128,1024]{1,0:T(8,128)} %bitcast.445, f32[128,1024]{1,0:T(8,128)} %bitcast.419, f32[1,1024]{1,0:T(1,128)} %gain_ref.6, ...), custom_call_target="tpu_custom_call" | custom-call | flops 805306368 | bytes 7872512 | tf_op jit(solution)/shard_map/pallas_call | solution.py:61
  404.4 2.7 collective-permute-done.53
  407.1 4.1 collective-permute-done.52
  417.0 7.8 %collective-permute-done.56 = f32[32,1024]{1,0:T(8,128)S(1)} collective-permute-done((f32[32,1024]{1,0:T(8,128)S(1)}, f32[32,1024]{1,0:T(8,128)S(1)}, u32[]{:S(2)}, u32[]{:S(2)}) %collective-permute-start.56) | collective-permute-done | bytes 131104 | tf_op jit(solution)/shard_map/ppermute | solution.py:662
  427.8 12.1 %shard_map.466 = (f32[128,1024]{1,0:T(8,128)}, f32[1,1024]{1,0:T(1,128)}, f32[128,1024]{1,0:T(8,128)}, f32[128,1024]{1,0:T(8,128)}) custom-call(f32[128,1024]{1,0:T(8,128)} %get-tuple-element.246.base_ref, f32[128,1024]{1,0:T(8,128)} %bitcast.436, f32[128,1024]{1,0:T(8,128)} %bitcast.416, f32[1,1024]{1,0:T(1,128)} %gain_ref.7, ...), custom_call_target="tpu_custom_call" | custom-call | flops 1610612736 | bytes 8388608 | tf_op jit(solution)/shard_map/pallas_call | solution.py:185
  444.0 2.7 collective-permute-done.60
  447.4 5.1 collective-permute-done.58
  459.9 2.5 collective-permute-start.62
  463.1 7.4 %collective-permute-done.62 = f32[32,1024]{1,0:T(8,128)S(1)} collective-permute-done((f32[32,1024]{1,0:T(8,128)S(1)}, f32[32,1024]{1,0:T(8,128)S(1)}, u32[]{:S(2)}, u32[]{:S(2)}) %collective-permute-start.62) | collective-permute-done | bytes 131104 | tf_op jit(solution)/shard_map/ppermute | solution.py:662
  470.5 2.7 collective-permute-done.63
  475.3 2.4 collective-permute-start.64
  477.7 15.2 %shard_map.467 = (f32[128,1024]{1,0:T(8,128)}, f32[1,1024]{1,0:T(1,128)}, f32[128,256]{1,0:T(8,128)}, f32[1024,512]{1,0:T(8,128)}, f32[128,1024]{1,0:T(8,128)}, ...) custom-call(f32[128,1024]{1,0:T(8,128)} %get-tuple-element.292.base_, ...), custom_call_target="tpu_custom_call" | custom-call | flops 3000000 | bytes 1000000 | tf_op jit(solution)/shard_map/pallas_call | solution.py:61
  496.1 2.6 collective-permute-start.75
  498.8 4.1 collective-permute-done.64
  514.0 5.0 collective-permute-done.71
  521.8 4.2 collective-permute-done.67
  527.8 11.3 %fusion.13 = f32[1024,1024]{1,0:T(8,128)} fusion(f32[1024,3328]{1,0:T(8,128)} %all-gather.16.cloned.1.call-done, f32[1024,3072]{1,0:T(8,128)} %all-gather.14.cloned.1.call-done), kind=kOutput, calls=%fused_computation.13 | convolution fusion | flops 6442450944 | bytes 12582912 | tf_op jit(solution)/shard_map/dot_general | solution.py:28
  548.5 9.8 %fusion.10 = f32[1024,1024]{1,0:T(8,128)} fusion(f32[1024,3328]{1,0:T(8,128)} %all-gather.16.cloned.1.call-done, f32[1024,3072]{1,0:T(8,128)S(1)} %bitcast.501), kind=kOutput, calls=%fused_computation.10 | convolution fusion | flops 6442450944 | bytes 12582912 | tf_op jit(solution)/shard_map/dot_general | solution.py:28
  558.8 8.9 %collective-permute-done.79 = f32[2,96,512]{2,1,0:T(8,128)S(1)} collective-permute-done((f32[2,96,512]{2,1,0:T(8,128)S(1)}, f32[2,96,512]{2,1,0:T(8,128)S(1)}, u32[]{:S(2)}, u32[]{:S(2)}) %collective-permute-start.79) | collective-permute-done | bytes 393248 | tf_op jit(solution)/shard_map/ppermute | solution.py:714
  567.7 10.4 %all-gather.18.cloned.1.call-done = f32[1024,2816]{1,0:T(8,128)} async-done(((f32[128,2816]{1,0:T(8,128)}), f32[1024,2816]{1,0:T(8,128)}) %all-gather.18.cloned.1.call-update) | async-done | bytes 11534352 | tf_op jit(solution)/shard_map/all_gather | solution.py:708
  581.2 9.6 %fusion.8 = f32[1024,768]{1,0:T(8,128)} fusion(f32[1024,3072]{1,0:T(8,128)} %all-gather.14.cloned.1.call-done, f32[1024,2816]{1,0:T(8,128)} %all-gather.18.cloned.1.call-done), kind=kOutput, calls=%fused_computation.8 | convolution fusion | flops 4831838208 | bytes 10485760 | tf_op jit(solution)/shard_map/dot_general | solution.py:28
  601.5 5.9 fusion.6
  608.5 12.9 %collective-permute-done.90 = f32[32,1024]{1,0:T(8,128)S(1)} collective-permute-done((f32[32,1024]{1,0:T(8,128)}, f32[32,1024]{1,0:T(8,128)S(1)}, u32[]{:S(2)}, u32[]{:S(2)}) %collective-permute-start.90) | collective-permute-done | bytes 131104 | tf_op jit(solution)/shard_map/ppermute | solution.py:662
  621.4 2.5 collective-permute-done.91
  624.0 11.3 %fusion.3 = f32[1024,1024]{1,0:T(8,128)} fusion(f32[1024,2816]{1,0:T(8,128)} %all-gather.18.cloned.1.call-done, f32[1024,2048]{1,0:T(8,128)} %all-gather.12.cloned.1.call-done), kind=kOutput, calls=%fused_computation.3 | convolution fusion | flops 6442450944 | bytes 12582912 | tf_op jit(solution)/shard_map/dot_general | solution.py:28
  635.3 6.9 shard_map.468
  644.1 11.1 %fusion = f32[1024,1024]{1,0:T(8,128)} fusion(f32[1024,2816]{1,0:T(8,128)} %all-gather.18.cloned.1.call-done, f32[1024,2048]{1,0:T(8,128)} %all-gather.12.cloned.1.call-done), kind=kOutput, calls=%fused_computation | convolution fusion | flops 6442450944 | bytes 12582912 | tf_op jit(solution)/shard_map/dot_general | solution.py:28
  655.2 3.8 copy.108
  659.0 3.8 copy.111
  (524 shorter events, 220.4 us)
Async XLA Ops:
  7.3 59.3 %all-gather.10.cloned.1.call-start = ((), (), s32[]{:S(2)}) async-start(), calls=%async_computation.1 | async-start | bytes 4718592 | tf_op jit(solution)/shard_map/all_gather | solution.py:708
  11.9 128.2 %all-gather.20.cloned.1.call-start = ((), (), s32[]{:S(2)}) async-start(), calls=%async_computation.6 | async-start | bytes 2293760 | tf_op jit(solution)/shard_map/all_gather | solution.py:793
  15.3 14.1 %collective-permute-start = (f32[264,512]{1,0:T(8,128)}, f32[264,512]{1,0:T(8,128)}, u32[]{:S(2)}, u32[]{:S(2)}) collective-permute-start(f32[264,512]{1,0:T(8,128)} %pad_maximum_fusion.8), channel_id=1, source_target_pairs={{0,1},{1,2},{2,3},{3,0},{4,5},{5,6},{6,7},{7,4},{8,9},{9,10},{10,1... | collective-permute-start | bytes 1622024 | tf_op jit(solution)/shard_map/ppermute | solution.py:662
  16.6 46.0 %collective-permute-start.1 = (f32[264,512]{1,0:T(8,128)}, f32[264,512]{1,0:T(8,128)}, u32[]{:S(2)}, u32[]{:S(2)}) collective-permute-start(f32[264,512]{1,0:T(8,128)} %pad_maximum_fusion.8), channel_id=1, source_target_pairs={{0,2},{1,3},{2,0},{3,1},{4,6},{5,7},{6,4},{7,5},{8,10},{9,11},{10,... | collective-permute-start | bytes 1622024 | tf_op jit(solution)/shard_map/ppermute | solution.py:662
  17.6 47.8 %collective-permute-start.2 = (f32[264,512]{1,0:T(8,128)}, f32[264,512]{1,0:T(8,128)}, u32[]{:S(2)}, u32[]{:S(2)}) collective-permute-start(f32[264,512]{1,0:T(8,128)} %pad_maximum_fusion.8), channel_id=1, source_target_pairs={{0,3},{1,0},{2,1},{3,2},{4,7},{5,4},{6,5},{7,6},{8,11},{9,8},{10,9... | collective-permute-start | bytes 1622024 | tf_op jit(solution)/shard_map/ppermute | solution.py:662
  67.8 321.6 %all-gather.12.cloned.1.call-start = ((), (), s32[]{:S(2)}) async-start(), calls=%async_computation.2 | async-start | bytes 9437184 | tf_op jit(solution)/shard_map/all_gather | solution.py:708
  80.4 14.6 %collective-permute-start.5 = (f32[32,1024]{1,0:T(8,128)S(1)}, f32[32,1024]{1,0:T(8,128)S(1)}, u32[]{:S(2)}, u32[]{:S(2)}) collective-permute-start(f32[32,1024]{1,0:T(8,128)S(1)} %get-tuple-element.510), channel_id=1, source_target_pairs={{0,3},{1,0},{2,1},{3,2},{4,7},{5,4},{6,5},{7,6},{8,11},{9,8},{10,9... | collective-permute-start | bytes 393224 | tf_op jit(solution)/shard_map/ppermute | solution.py:662
  80.4 17.1 %collective-permute-start.4 = (f32[32,1024]{1,0:T(8,128)S(1)}, f32[32,1024]{1,0:T(8,128)S(1)}, u32[]{:S(2)}, u32[]{:S(2)}) collective-permute-start(f32[32,1024]{1,0:T(8,128)S(1)} %get-tuple-element.511), channel_id=1, source_target_pairs={{0,2},{1,3},{2,0},{3,1},{4,6},{5,7},{6,4},{7,5},{8,10},{9,11},{10,... | collective-permute-start | bytes 393224 | tf_op jit(solution)/shard_map/ppermute | solution.py:662
  81.8 24.2 %collective-permute-start.3 = (f32[32,1024]{1,0:T(8,128)S(1)}, f32[32,1024]{1,0:T(8,128)S(1)}, u32[]{:S(2)}, u32[]{:S(2)}) collective-permute-start(f32[32,1024]{1,0:T(8,128)S(1)} %get-tuple-element.509), channel_id=1, source_target_pairs={{0,1},{1,2},{2,3},{3,0},{4,5},{5,6},{6,7},{7,4},{8,9},{9,10},{10,1... | collective-permute-start | bytes 393224 | tf_op jit(solution)/shard_map/ppermute | solution.py:662
  107.0 13.2 %collective-permute-start.6 = (f32[32,1024]{1,0:T(8,128)S(1)}, f32[32,1024]{1,0:T(8,128)S(1)}, u32[]{:S(2)}, u32[]{:S(2)}) collective-permute-start(f32[32,1024]{1,0:T(8,128)S(1)} %bitcast_add_fusion.15), channel_id=1, source_target_pairs={{0,1},{1,2},{2,3},{3,0},{4,5},{5,6},{6,7},{7,4},{8,9},{9,10},{10,1... | collective-permute-start | bytes 393224 | tf_op jit(solution)/shard_map/ppermute | solution.py:662
  110.9 18.3 %collective-permute-start.7 = (f32[32,1024]{1,0:T(8,128)S(1)}, f32[32,1024]{1,0:T(8,128)S(1)}, u32[]{:S(2)}, u32[]{:S(2)}) collective-permute-start(f32[32,1024]{1,0:T(8,128)S(1)} %bitcast_add_fusion.15), channel_id=1, source_target_pairs={{0,2},{1,3},{2,0},{3,1},{4,6},{5,7},{6,4},{7,5},{8,10},{9,11},{10,... | collective-permute-start | bytes 393224 | tf_op jit(solution)/shard_map/ppermute | solution.py:662
  112.7 18.9 %collective-permute-start.8 = (f32[32,1024]{1,0:T(8,128)S(1)}, f32[32,1024]{1,0:T(8,128)S(1)}, u32[]{:S(2)}, u32[]{:S(2)}) collective-permute-start(f32[32,1024]{1,0:T(8,128)S(1)} %bitcast_add_fusion.15), channel_id=1, source_target_pairs={{0,3},{1,0},{2,1},{3,2},{4,7},{5,4},{6,5},{7,6},{8,11},{9,8},{10,9... | collective-permute-start | bytes 393224 | tf_op jit(solution)/shard_map/ppermute | solution.py:662
  140.1 42.0 %collective-permute-start.15 = (f32[4,448,256]{2,1,0:T(8,128)}, f32[4,448,256]{2,1,0:T(8,128)S(1)}, u32[]{:S(2)}, u32[]{:S(2)}) collective-permute-start(f32[4,448,256]{2,1,0:T(8,128)} %bitcast.503), channel_id=1, source_target_pairs={{0,8},{4,12},{8,0},{12,4},{16,24},{20,28},{24,16},{28,20},{1,9},{5... | collective-permute-start | bytes 5505032 | tf_op jit(solution)/shard_map/ppermute | solution.py:714
  141.4 41.0 %collective-permute-start.16 = (f32[4,448,256]{2,1,0:T(8,128)}, f32[4,448,256]{2,1,0:T(8,128)}, u32[]{:S(2)}, u32[]{:S(2)}) collective-permute-start(f32[4,448,256]{2,1,0:T(8,128)} %bitcast.504), channel_id=1, source_target_pairs={{0,16},{4,20},{8,24},{12,28},{16,0},{20,4},{24,8},{28,12},{1,17},{... | collective-permute-start | bytes 5505032 | tf_op jit(solution)/shard_map/ppermute | solution.py:714
  143.5 10.8 %collective-permute-start.9 = (f32[32,1024]{1,0:T(8,128)S(1)}, f32[32,1024]{1,0:T(8,128)S(1)}, u32[]{:S(2)}, u32[]{:S(2)}) collective-permute-start(f32[32,1024]{1,0:T(8,128)S(1)} %get-tuple-element.506), channel_id=1, source_target_pairs={{0,1},{1,2},{2,3},{3,0},{4,5},{5,6},{6,7},{7,4},{8,9},{9,10},{10,1... | collective-permute-start | bytes 393224 | tf_op jit(solution)/shard_map/ppermute | solution.py:662
  155.3 16.5 %collective-permute-start.12 = (f32[32,1024]{1,0:T(8,128)S(1)}, f32[32,1024]{1,0:T(8,128)S(1)}, u32[]{:S(2)}, u32[]{:S(2)}) collective-permute-start(f32[32,1024]{1,0:T(8,128)S(1)} %fusion.46), channel_id=1, source_target_pairs={{0,1},{1,2},{2,3},{3,0},{4,5},{5,6},{6,7},{7,4},{8,9},{9,10},{10,1... | collective-permute-start | bytes 393224 | tf_op jit(solution)/shard_map/ppermute | solution.py:662
  157.7 14.2 %collective-permute-start.13 = (f32[32,1024]{1,0:T(8,128)S(1)}, f32[32,1024]{1,0:T(8,128)S(1)}, u32[]{:S(2)}, u32[]{:S(2)}) collective-permute-start(f32[32,1024]{1,0:T(8,128)S(1)} %fusion.46), channel_id=1, source_target_pairs={{0,2},{1,3},{2,0},{3,1},{4,6},{5,7},{6,4},{7,5},{8,10},{9,11},{10,... | collective-permute-start | bytes 393224 | tf_op jit(solution)/shard_map/ppermute | solution.py:662
  159.6 16.3 %collective-permute-start.14 = (f32[32,1024]{1,0:T(8,128)S(1)}, f32[32,1024]{1,0:T(8,128)S(1)}, u32[]{:S(2)}, u32[]{:S(2)}) collective-permute-start(f32[32,1024]{1,0:T(8,128)S(1)} %fusion.46), channel_id=1, source_target_pairs={{0,3},{1,0},{2,1},{3,2},{4,7},{5,4},{6,5},{7,6},{8,11},{9,8},{10,9... | collective-permute-start | bytes 393224 | tf_op jit(solution)/shard_map/ppermute | solution.py:662
  185.6 10.8 %collective-permute-start.17 = (f32[32,1024]{1,0:T(8,128)S(1)}, f32[32,1024]{1,0:T(8,128)S(1)}, u32[]{:S(2)}, u32[]{:S(2)}) collective-permute-start(f32[32,1024]{1,0:T(8,128)S(1)} %get-tuple-element.503), channel_id=1, source_target_pairs={{0,1},{1,2},{2,3},{3,0},{4,5},{5,6},{6,7},{7,4},{8,9},{9,10},{10,1... | collective-permute-start | bytes 393224 | tf_op jit(solution)/shard_map/ppermute | solution.py:662
  189.0 31.5 %collective-permute-start.23 = (f32[4,256,256]{2,1,0:T(8,128)S(1)}, f32[4,256,256]{2,1,0:T(8,128)S(1)}, u32[]{:S(2)}, u32[]{:S(2)}) collective-permute-start(f32[4,256,256]{2,1,0:T(8,128)S(1)} %slice.219), channel_id=1, source_target_pairs={{0,16},{4,20},{8,24},{12,28},{16,0},{20,4},{24,8},{28,12},{1,17},{... | collective-permute-start | bytes 3145736 | tf_op jit(solution)/shard_map/ppermute | solution.py:714
  191.5 29.1 %collective-permute-start.24 = (f32[4,192,256]{2,1,0:T(8,128)S(1)}, f32[4,192,256]{2,1,0:T(8,128)S(1)}, u32[]{:S(2)}, u32[]{:S(2)}) collective-permute-start(f32[4,192,256]{2,1,0:T(8,128)S(1)} %slice.220), channel_id=1, source_target_pairs={{0,8},{4,12},{8,0},{12,4},{16,24},{20,28},{24,16},{28,20},{1,9},{5... | collective-permute-start | bytes 2359304 | tf_op jit(solution)/shard_map/ppermute | solution.py:714
  200.2 11.7 %collective-permute-start.22 = (f32[32,1024]{1,0:T(8,128)S(1)}, f32[32,1024]{1,0:T(8,128)S(1)}, u32[]{:S(2)}, u32[]{:S(2)}) collective-permute-start(f32[32,1024]{1,0:T(8,128)S(1)} %fusion.43), channel_id=1, source_target_pairs={{0,3},{1,0},{2,1},{3,2},{4,7},{5,4},{6,5},{7,6},{8,11},{9,8},{10,9... | collective-permute-start | bytes 393224 | tf_op jit(solution)/shard_map/ppermute | solution.py:662
  222.4 204.6 %all-gather.14.cloned.1.call-start = ((), (), s32[]{:S(2)}) async-start(), calls=%async_computation.3 | async-start | bytes 14155776 | tf_op jit(solution)/shard_map/all_gather | solution.py:708
  224.4 10.8 %collective-permute-start.25 = (f32[32,1024]{1,0:T(8,128)S(1)}, f32[32,1024]{1,0:T(8,128)S(1)}, u32[]{:S(2)}, u32[]{:S(2)}) collective-permute-start(f32[32,1024]{1,0:T(8,128)S(1)} %get-tuple-element.500), channel_id=1, source_target_pairs={{0,1},{1,2},{2,3},{3,0},{4,5},{5,6},{6,7},{7,4},{8,9},{9,10},{10,1... | collective-permute-start | bytes 393224 | tf_op jit(solution)/shard_map/ppermute | solution.py:662
  238.7 234.6 %reduce-scatter.4.cloned.1.call-start = ((), (), s32[]{:S(2)}) async-start(), calls=%async_computation.8 | async-start | bytes 6553600
  238.7 22.2 %collective-permute-start.31 = (f32[4,448,256]{2,1,0:T(8,128)}, f32[4,448,256]{2,1,0:T(8,128)}, u32[]{:S(2)}, u32[]{:S(2)}) collective-permute-start(f32[4,448,256]{2,1,0:T(8,128)} %bitcast.505), channel_id=1, source_target_pairs={{0,4},{4,0},{8,12},{12,8},{16,20},{20,16},{24,28},{28,24},{1,5},{5... | collective-permute-start | bytes 5505032 | tf_op jit(solution)/shard_map/ppermute | solution.py:714
  240.2 20.7 %collective-permute-start.32 = (f32[4,448,256]{2,1,0:T(8,128)S(1)}, f32[4,448,256]{2,1,0:T(8,128)}, u32[]{:S(2)}, u32[]{:S(2)}) collective-permute-start(f32[4,448,256]{2,1,0:T(8,128)S(1)} %collective-permute-done.15.refs_9_), channel_id=1, source_target_pairs={{0,4},{4,0},{8,12},{12,8},{16,20},{20,16},{24,28},{28,24},{1,5},{5... | collective-permute-start | bytes 5505032 | tf_op jit(solution)/shard_map/ppermute | solution.py:714
  240.3 20.7 %collective-permute-start.33 = (f32[4,448,256]{2,1,0:T(8,128)}, f32[4,448,256]{2,1,0:T(8,128)}, u32[]{:S(2)}, u32[]{:S(2)}) collective-permute-start(f32[4,448,256]{2,1,0:T(8,128)} %collective-permute-done.16.refs_10_), channel_id=1, source_target_pairs={{0,4},{4,0},{8,12},{12,8},{16,20},{20,16},{24,28},{28,24},{1,5},{5... | collective-permute-start | bytes 5505032 | tf_op jit(solution)/shard_map/ppermute | solution.py:714
  247.0 13.9 %collective-permute-start.34 = (f32[4,256,256]{2,1,0:T(8,128)}, f32[4,256,256]{2,1,0:T(8,128)}, u32[]{:S(2)}, u32[]{:S(2)}) collective-permute-start(f32[4,256,256]{2,1,0:T(8,128)} %copy-done.64), channel_id=1, source_target_pairs={{0,4},{4,0},{8,12},{12,8},{16,20},{20,16},{24,28},{28,24},{1,5},{5... | collective-permute-start | bytes 3145736 | tf_op jit(solution)/shard_map/ppermute | solution.py:714
  305.3 11.0 %collective-permute-start.36 = (f32[32,1024]{1,0:T(8,128)S(1)}, f32[32,1024]{1,0:T(8,128)S(1)}, u32[]{:S(2)}, u32[]{:S(2)}) collective-permute-start(f32[32,1024]{1,0:T(8,128)S(1)} %get-tuple-element.497), channel_id=1, source_target_pairs={{0,1},{1,2},{2,3},{3,0},{4,5},{5,6},{6,7},{7,4},{8,9},{9,10},{10,1... | collective-permute-start | bytes 393224 | tf_op jit(solution)/shard_map/ppermute | solution.py:662
  317.3 16.4 %collective-permute-start.39 = (f32[32,1024]{1,0:T(8,128)S(1)}, f32[32,1024]{1,0:T(8,128)S(1)}, u32[]{:S(2)}, u32[]{:S(2)}) collective-permute-start(f32[32,1024]{1,0:T(8,128)S(1)} %fusion.37), channel_id=1, source_target_pairs={{0,1},{1,2},{2,3},{3,0},{4,5},{5,6},{6,7},{7,4},{8,9},{9,10},{10,1... | collective-permute-start | bytes 393224 | tf_op jit(solution)/shard_map/ppermute | solution.py:662
  319.6 14.0 %collective-permute-start.40 = (f32[32,1024]{1,0:T(8,128)S(1)}, f32[32,1024]{1,0:T(8,128)S(1)}, u32[]{:S(2)}, u32[]{:S(2)}) collective-permute-start(f32[32,1024]{1,0:T(8,128)S(1)} %fusion.37), channel_id=1, source_target_pairs={{0,2},{1,3},{2,0},{3,1},{4,6},{5,7},{6,4},{7,5},{8,10},{9,11},{10,... | collective-permute-start | bytes 393224 | tf_op jit(solution)/shard_map/ppermute | solution.py:662
  321.0 12.7 %collective-permute-start.41 = (f32[32,1024]{1,0:T(8,128)S(1)}, f32[32,1024]{1,0:T(8,128)S(1)}, u32[]{:S(2)}, u32[]{:S(2)}) collective-permute-start(f32[32,1024]{1,0:T(8,128)S(1)} %fusion.37), channel_id=1, source_target_pairs={{0,3},{1,0},{2,1},{3,2},{4,7},{5,4},{6,5},{7,6},{8,11},{9,8},{10,9... | collective-permute-start | bytes 393224 | tf_op jit(solution)/shard_map/ppermute | solution.py:662
  333.7 18.4 %collective-permute-start.42 = (f32[4,1280,256]{2,1,0:T(8,128)}, f32[4,1280,256]{2,1,0:T(8,128)}, u32[]{:S(2)}, u32[]{:S(2)}) collective-permute-start(f32[4,1280,256]{2,1,0:T(8,128)} %bitcast.502), channel_id=1, source_target_pairs={{0,4},{4,0},{8,12},{12,8},{16,20},{20,16},{24,28},{28,24},{1,5},{5... | collective-permute-start | bytes 15728648 | tf_op jit(solution)/shard_map/ppermute | solution.py:714
  336.5 15.5 %collective-permute-start.45 = (f32[128,256]{1,0:T(8,128)S(1)}, f32[128,256]{1,0:T(8,128)S(1)}, u32[]{:S(2)}, u32[]{:S(2)}) collective-permute-start(f32[128,256]{1,0:T(8,128)S(1)} %get-tuple-element.495), channel_id=1, source_target_pairs={{0,3},{1,0},{2,1},{3,2},{4,7},{5,4},{6,5},{7,6},{8,11},{9,8},{10,9... | collective-permute-start | bytes 393224 | tf_op jit(solution)/shard_map/ppermute | solution.py:662
  339.4 12.7 %collective-permute-start.44 = (f32[128,256]{1,0:T(8,128)S(1)}, f32[128,256]{1,0:T(8,128)S(1)}, u32[]{:S(2)}, u32[]{:S(2)}) collective-permute-start(f32[128,256]{1,0:T(8,128)S(1)} %get-tuple-element.496), channel_id=1, source_target_pairs={{0,2},{1,3},{2,0},{3,1},{4,6},{5,7},{6,4},{7,5},{8,10},{9,11},{10,... | collective-permute-start | bytes 393224 | tf_op jit(solution)/shard_map/ppermute | solution.py:662
  339.9 12.2 %collective-permute-start.43 = (f32[128,256]{1,0:T(8,128)S(1)}, f32[128,256]{1,0:T(8,128)S(1)}, u32[]{:S(2)}, u32[]{:S(2)}) collective-permute-start(f32[128,256]{1,0:T(8,128)S(1)} %get-tuple-element.494), channel_id=1, source_target_pairs={{0,1},{1,2},{2,3},{3,0},{4,5},{5,6},{6,7},{7,4},{8,9},{9,10},{10,1... | collective-permute-start | bytes 393224 | tf_op jit(solution)/shard_map/ppermute | solution.py:662
  357.7 170.1 %all-gather.16.cloned.1.call-start = ((), (), s32[]{:S(2)}) async-start(), calls=%async_computation.4 | async-start | bytes 15335424 | tf_op jit(solution)/shard_map/all_gather | solution.py:708
  361.4 11.5 %collective-permute-start.46 = (f32[32,1024]{1,0:T(8,128)S(1)}, f32[32,1024]{1,0:T(8,128)S(1)}, u32[]{:S(2)}, u32[]{:S(2)}) collective-permute-start(f32[32,1024]{1,0:T(8,128)S(1)} %get-tuple-element.491), channel_id=1, source_target_pairs={{0,1},{1,2},{2,3},{3,0},{4,5},{5,6},{6,7},{7,4},{8,9},{9,10},{10,1... | collective-permute-start | bytes 393224 | tf_op jit(solution)/shard_map/ppermute | solution.py:662
  374.3 203.9 %all-gather.18.cloned.1.call-start = ((), (), s32[]{:S(2)}) async-start(), calls=%async_computation.5 | async-start | bytes 12976128 | tf_op jit(solution)/shard_map/all_gather | solution.py:708
  376.7 10.9 %collective-permute-start.50 = (f32[32,1024]{1,0:T(8,128)S(1)}, f32[32,1024]{1,0:T(8,128)S(1)}, u32[]{:S(2)}, u32[]{:S(2)}) collective-permute-start(f32[32,1024]{1,0:T(8,128)S(1)} %fusion.33), channel_id=1, source_target_pairs={{0,2},{1,3},{2,0},{3,1},{4,6},{5,7},{6,4},{7,5},{8,10},{9,11},{10,... | collective-permute-start | bytes 393224 | tf_op jit(solution)/shard_map/ppermute | solution.py:662
  377.2 12.2 %collective-permute-start.51 = (f32[32,1024]{1,0:T(8,128)S(1)}, f32[32,1024]{1,0:T(8,128)S(1)}, u32[]{:S(2)}, u32[]{:S(2)}) collective-permute-start(f32[32,1024]{1,0:T(8,128)S(1)} %fusion.33), channel_id=1, source_target_pairs={{0,3},{1,0},{2,1},{3,2},{4,7},{5,4},{6,5},{7,6},{8,11},{9,8},{10,9... | collective-permute-start | bytes 393224 | tf_op jit(solution)/shard_map/ppermute | solution.py:662
  400.5 10.8 %collective-permute-start.52 = (f32[32,1024]{1,0:T(8,128)S(1)}, f32[32,1024]{1,0:T(8,128)S(1)}, u32[]{:S(2)}, u32[]{:S(2)}) collective-permute-start(f32[32,1024]{1,0:T(8,128)S(1)} %get-tuple-element.488), channel_id=1, source_target_pairs={{0,1},{1,2},{2,3},{3,0},{4,5},{5,6},{6,7},{7,4},{8,9},{9,10},{10,1... | collective-permute-start | bytes 393224 | tf_op jit(solution)/shard_map/ppermute | solution.py:662
  441.7 10.8 %collective-permute-start.58 = (f32[32,1024]{1,0:T(8,128)S(1)}, f32[32,1024]{1,0:T(8,128)S(1)}, u32[]{:S(2)}, u32[]{:S(2)}) collective-permute-start(f32[32,1024]{1,0:T(8,128)S(1)} %get-tuple-element.485), channel_id=1, source_target_pairs={{0,1},{1,2},{2,3},{3,0},{4,5},{5,6},{6,7},{7,4},{8,9},{9,10},{10,1... | collective-permute-start | bytes 393224 | tf_op jit(solution)/shard_map/ppermute | solution.py:662
  455.9 213.8 %all-gather.22.cloned.1.call-start = ((), (), s32[]{:S(2)}) async-start(), calls=%async_computation.7 | async-start | bytes 6488064 | tf_op jit(solution)/shard_map/all_gather | solution.py:1014
  462.4 10.8 %collective-permute-start.63 = (f32[32,1024]{1,0:T(8,128)S(1)}, f32[32,1024]{1,0:T(8,128)S(1)}, u32[]{:S(2)}, u32[]{:S(2)}) collective-permute-start(f32[32,1024]{1,0:T(8,128)S(1)} %fusion.29), channel_id=1, source_target_pairs={{0,3},{1,0},{2,1},{3,2},{4,7},{5,4},{6,5},{7,6},{8,11},{9,8},{10,9... | collective-permute-start | bytes 393224 | tf_op jit(solution)/shard_map/ppermute | solution.py:662
  474.7 24.1 %collective-permute-start.66 = (f32[320,256]{1,0:T(8,128)S(1)}, f32[320,256]{1,0:T(8,128)S(1)}, u32[]{:S(2)}, u32[]{:S(2)}) collective-permute-start(f32[320,256]{1,0:T(8,128)S(1)} %get-tuple-element.476), channel_id=1, source_target_pairs={{0,3},{1,0},{2,1},{3,2},{4,7},{5,4},{6,5},{7,6},{8,11},{9,8},{10,9... | collective-permute-start | bytes 983048 | tf_op jit(solution)/shard_map/ppermute | solution.py:662
  474.8 24.0 %collective-permute-start.65 = (f32[320,256]{1,0:T(8,128)S(1)}, f32[320,256]{1,0:T(8,128)S(1)}, u32[]{:S(2)}, u32[]{:S(2)}) collective-permute-start(f32[320,256]{1,0:T(8,128)S(1)} %get-tuple-element.477), channel_id=1, source_target_pairs={{0,2},{1,3},{2,0},{3,1},{4,6},{5,7},{6,4},{7,5},{8,10},{9,11},{10,... | collective-permute-start | bytes 983048 | tf_op jit(solution)/shard_map/ppermute | solution.py:662
  475.3 27.7 %collective-permute-start.64 = (f32[320,256]{1,0:T(8,128)S(1)}, f32[320,256]{1,0:T(8,128)S(1)}, u32[]{:S(2)}, u32[]{:S(2)}) collective-permute-start(f32[320,256]{1,0:T(8,128)S(1)} %get-tuple-element.475), channel_id=1, source_target_pairs={{0,1},{1,2},{2,3},{3,0},{4,5},{5,6},{6,7},{7,4},{8,9},{9,10},{10,1... | collective-permute-start | bytes 983048 | tf_op jit(solution)/shard_map/ppermute | solution.py:662
  496.1 43.0 %collective-permute-start.75 = (f32[4,192,512]{2,1,0:T(8,128)}, f32[4,192,512]{2,1,0:T(8,128)}, u32[]{:S(2)}, u32[]{:S(2)}) collective-permute-start(f32[4,192,512]{2,1,0:T(8,128)} %get-tuple-element.462), channel_id=1, source_target_pairs={{0,4},{4,0},{8,12},{12,8},{16,20},{20,16},{24,28},{28,24},{1,5},{5... | collective-permute-start | bytes 4718600 | tf_op jit(solution)/shard_map/ppermute | solution.py:714
  520.2 18.9 %collective-permute-start.73 = (f32[128,384]{1,0:T(8,128)S(1)}, f32[128,384]{1,0:T(8,128)S(1)}, u32[]{:S(2)}, u32[]{:S(2)}) collective-permute-start(f32[128,384]{1,0:T(8,128)S(1)} %select_maximum_fusion.refs_0_), channel_id=1, source_target_pairs={{0,8},{4,12},{8,0},{12,4},{16,24},{20,28},{24,16},{28,20},{1,9},{5... | collective-permute-start | bytes 589832 | tf_op jit(solution)/shard_map/ppermute | solution.py:714
  520.3 18.8 %collective-permute-start.74 = (f32[128,384]{1,0:T(8,128)S(1)}, f32[128,384]{1,0:T(8,128)}, u32[]{:S(2)}, u32[]{:S(2)}) collective-permute-start(f32[128,384]{1,0:T(8,128)S(1)} %select_maximum_fusion.refs_0_), channel_id=1, source_target_pairs={{0,16},{4,20},{8,24},{12,28},{16,0},{20,4},{24,8},{28,12},{1,17},{... | collective-permute-start | bytes 589832 | tf_op jit(solution)/shard_map/ppermute | solution.py:714
  540.2 27.5 %collective-permute-start.76 = (f32[256,512]{1,0:T(8,128)S(1)}, f32[256,512]{1,0:T(8,128)}, u32[]{:S(2)}, u32[]{:S(2)}) collective-permute-start(f32[256,512]{1,0:T(8,128)S(1)} %get-tuple-element.466), channel_id=1, source_target_pairs={{0,1},{1,2},{2,3},{3,0},{4,5},{5,6},{6,7},{7,4},{8,9},{9,10},{10,1... | collective-permute-start | bytes 1572872 | tf_op jit(solution)/shard_map/ppermute | solution.py:662
  542.4 15.9 %collective-permute-start.77 = (f32[64,384]{1,0:T(8,128)S(1)}, f32[64,384]{1,0:T(8,128)S(1)}, u32[]{:S(2)}, u32[]{:S(2)}) collective-permute-start(f32[64,384]{1,0:T(8,128)S(1)} %slice.233), channel_id=1, source_target_pairs={{0,16},{4,20},{8,24},{12,28},{16,0},{20,4},{24,8},{28,12},{1,17},{... | collective-permute-start | bytes 294920 | tf_op jit(solution)/shard_map/ppermute | solution.py:714
  544.7 14.1 %collective-permute-start.78 = (f32[64,384]{1,0:T(8,128)S(1)}, f32[64,384]{1,0:T(8,128)S(1)}, u32[]{:S(2)}, u32[]{:S(2)}) collective-permute-start(f32[64,384]{1,0:T(8,128)S(1)} %slice.234), channel_id=1, source_target_pairs={{0,8},{4,12},{8,0},{12,4},{16,24},{20,28},{24,16},{28,20},{1,9},{5... | collective-permute-start | bytes 294920 | tf_op jit(solution)/shard_map/ppermute | solution.py:714
  546.8 20.9 %collective-permute-start.79 = (f32[2,96,512]{2,1,0:T(8,128)S(1)}, f32[2,96,512]{2,1,0:T(8,128)S(1)}, u32[]{:S(2)}, u32[]{:S(2)}) collective-permute-start(f32[2,96,512]{2,1,0:T(8,128)S(1)} %get-tuple-element.469), channel_id=1, source_target_pairs={{0,8},{4,12},{8,0},{12,4},{16,24},{20,28},{24,16},{28,20},{1,9},{5... | collective-permute-start | bytes 1179656 | tf_op jit(solution)/shard_map/ppermute | solution.py:714
  548.2 19.5 %collective-permute-start.80 = (f32[2,96,512]{2,1,0:T(8,128)S(1)}, f32[2,96,512]{2,1,0:T(8,128)}, u32[]{:S(2)}, u32[]{:S(2)}) collective-permute-start(f32[2,96,512]{2,1,0:T(8,128)S(1)} %get-tuple-element.467), channel_id=1, source_target_pairs={{0,16},{4,20},{8,24},{12,28},{16,0},{20,4},{24,8},{28,12},{1,17},{... | collective-permute-start | bytes 1179656 | tf_op jit(solution)/shard_map/ppermute | solution.py:714
  558.4 36.0 %collective-permute-start.83 = (f32[256,512]{1,0:T(8,128)}, f32[256,512]{1,0:T(8,128)S(1)}, u32[]{:S(2)}, u32[]{:S(2)}) collective-permute-start(f32[256,512]{1,0:T(8,128)} %get-tuple-element.465), channel_id=1, source_target_pairs={{0,3},{1,0},{2,1},{3,2},{4,7},{5,4},{6,5},{7,6},{8,11},{9,8},{10,9... | collective-permute-start | bytes 1572872 | tf_op jit(solution)/shard_map/ppermute | solution.py:662
  579.1 12.7 %collective-permute-start.82 = (f32[96,512]{1,0:T(8,128)S(1)}, f32[96,512]{1,0:T(8,128)S(1)}, u32[]{:S(2)}, u32[]{:S(2)}) collective-permute-start(f32[96,512]{1,0:T(8,128)S(1)} %add_bitcast_fusion.4), channel_id=1, source_target_pairs={{0,8},{4,12},{8,0},{12,4},{16,24},{20,28},{24,16},{28,20},{1,9},{5... | collective-permute-start | bytes 589832 | tf_op jit(solution)/shard_map/ppermute | solution.py:714
  580.0 13.2 %collective-permute-start.81 = (f32[96,512]{1,0:T(8,128)S(1)}, f32[96,512]{1,0:T(8,128)S(1)}, u32[]{:S(2)}, u32[]{:S(2)}) collective-permute-start(f32[96,512]{1,0:T(8,128)S(1)} %add_bitcast_fusion.5), channel_id=1, source_target_pairs={{0,16},{4,20},{8,24},{12,28},{16,0},{20,4},{24,8},{28,12},{1,17},{... | collective-permute-start | bytes 589832 | tf_op jit(solution)/shard_map/ppermute | solution.py:714
  597.6 10.8 %collective-permute-start.89 = (f32[32,1024]{1,0:T(8,128)}, f32[32,1024]{1,0:T(8,128)S(1)}, u32[]{:S(2)}, u32[]{:S(2)}) collective-permute-start(f32[32,1024]{1,0:T(8,128)} %fusion.27), channel_id=1, source_target_pairs={{0,1},{1,2},{2,3},{3,0},{4,5},{5,6},{6,7},{7,4},{8,9},{9,10},{10,1... | collective-permute-start | bytes 393224 | tf_op jit(solution)/shard_map/ppermute | solution.py:662
  598.9 22.5 %collective-permute-start.90 = (f32[32,1024]{1,0:T(8,128)}, f32[32,1024]{1,0:T(8,128)S(1)}, u32[]{:S(2)}, u32[]{:S(2)}) collective-permute-start(f32[32,1024]{1,0:T(8,128)} %fusion.27), channel_id=1, source_target_pairs={{0,2},{1,3},{2,0},{3,1},{4,6},{5,7},{6,4},{7,5},{8,10},{9,11},{10,... | collective-permute-start | bytes 393224 | tf_op jit(solution)/shard_map/ppermute | solution.py:662
  600.0 23.9 %collective-permute-start.91 = (f32[32,1024]{1,0:T(8,128)}, f32[32,1024]{1,0:T(8,128)S(1)}, u32[]{:S(2)}, u32[]{:S(2)}) collective-permute-start(f32[32,1024]{1,0:T(8,128)} %fusion.27), channel_id=1, source_target_pairs={{0,3},{1,0},{2,1},{3,2},{4,7},{5,4},{6,5},{7,6},{8,11},{9,8},{10,9... | collective-permute-start | bytes 393224 | tf_op jit(solution)/shard_map/ppermute | solution.py:662
  601.3 53.9 %collective-permute-start.92 = (f32[256,512]{1,0:T(8,128)}, f32[256,512]{1,0:T(8,128)S(1)}, u32[]{:S(2)}, u32[]{:S(2)}) collective-permute-start(f32[256,512]{1,0:T(8,128)} %get-tuple-element.464), channel_id=1, source_target_pairs={{0,2},{1,3},{2,0},{3,1},{4,6},{5,7},{6,4},{7,5},{8,10},{9,11},{10,... | collective-permute-start | bytes 1572872 | tf_op jit(solution)/shard_map/ppermute | solution.py:662
  (119 other events, 1163.4 us)
Sparse Core Ops, SparseCore 0:
  12.0 38.0 all-gather.9
  67.9 60.9 all-gather.19
  222.6 54.5 all-gather.11
  278.9 71.9 all-gather.13
  357.9 60.7 reduce-scatter.3
  420.4 76.4 all-gather.15
  498.9 79.2 all-gather.17
  597.7 43.1 all-gather.21

commit v5 on v4

--- a/solution.py
+++ b/solution.py
@@ -849,7 +849,7 @@
         full_out = jnp.transpose(widen(everything, at, wq_rows, wide), (1, 0, 2, 3)).reshape(zs, -1, wide)
         pieces = [full_kv, full_query, full_out, full_up, full_down]
     read_all = d_gather([read_joined])
-    state4, normed2, normed3, act3 = sum_over_head(part3, state3, (normed2, normed3, act3))
+    state4, normed2, normed3, act3, *pieces = sum_over_head(part3, state3, (normed2, normed3, act3, *pieces))
     layer_all = d_gather([normed2, normed3, act3])
 
     (

time: 704 us -> 714 us (1.014)
  waiting for transfers between devices: 230 us -> 242 us
    unnamed x183 -> x191, local copies, waits for them, and re-layouts: 25 us -> 28.6 us
  transfers between devices with their start and end apart: 101 -> 101, of which waited for: 50 -> 52; matrix products, arithmetic and copies ran while one was open for 22% -> 22% of each run, Pallas kernels for 19% -> 19%
where the time goes in v5:
time: 714 us; the launch traced here: 704 us
  waiting for transfers between devices  242 us (34%)
  Pallas kernels  133 us (19%)
  starting transfers between devices  120 us (17%)
  local copies, waits for them, and re-layouts  83.9 us (12%)
  matrix products  60.7 us (9%)
  other arithmetic  47.7 us (7%)
  between operations  16.6 us (2%)
    ppermute x69, waiting for transfers between devices, shift(): lax.ppermute(values, 'head', [(i, (i + step) % zs) for i in range(zs)])  213 us
    ppermute x69, starting transfers between devices, shift(): lax.ppermute(values, 'head', [(i, (i + step) % zs) for i in range(zs)])  99.7 us
    dot_general x7, matrix products, tmm(): lax.dot_general(left, right, (((0,), (0,)), ((), ())), precision=PRECISE)  59.7 us
    pallas_call x1, Pallas kernels, write_stage(): pl.pallas_call(call, out_shape=outs, in_specs=[vmem] * 7 + [pl.BlockSpec(...  38.8 us
    pallas_call x4, Pallas kernels, run_whole(): pl.pallas_call(kernel, out_shape=outs, in_specs=[pl.BlockSpec(memory_spac...  37 us
    unnamed x191, local copies, waits for them, and re-layouts  28.6 us
    pallas_call x2, Pallas kernels, ffn_backward(): pl.pallas_call(ffn_back_kernel, grid=(inner // tile,), out_shape=[shape_o...  22.7 us
    ppermute x24, starting transfers between devices, swap(): return lax.ppermute(values, 'dp', [(i, i ^ bits) for i in range(ds)])  20.2 us
  transfers between devices with their start and end apart: 101, of which 52 were waited for; matrix products, arithmetic and copies ran while one was open for 22% of the time, Pallas kernels for 19%

profile of v5, /device:TPU:13, one launch (start us, length us, event | category | flops | bytes accessed | tf_op | source)
XLA Modules:
  0.0 704.3 jit_solution(2141464258335294843)
XLA Ops:
  19.0 2.5 copy.95
  30.4 32.1 %collective-permute-done.1 = f32[264,512]{1,0:T(8,128)} collective-permute-done((f32[264,512]{1,0:T(8,128)}, f32[264,512]{1,0:T(8,128)}, u32[]{:S(2)}, u32[]{:S(2)}) %collective-permute-start.1) | collective-permute-done | bytes 540704 | tf_op jit(solution)/shard_map/ppermute | solution.py:662
  70.7 8.6 %shard_map.458 = (f32[1024,512]{1,0:T(8,128)}, f32[128,256]{1,0:T(8,128)}, f32[512,1024]{1,0:T(8,128)}, f32[128,1024]{1,0:T(8,128)}) custom-call(f32[128,256]{1,0:T(8,128)} %fusion.69.q_ref, f32[4,264,512]{2,1,0:T(8,128)} %copy-done.5, f32[1,512]{1,0:T(1,128)} %get-tuple-element.546.gain_ref.int_gain_ref, s32[1,1024]{1,0:T(1,128)} %seg_ref.1, ...), custom_call_target="tpu_custom_call" | custom-call | flops 3221225472 | bytes 9246720 | tf_op jit(solution)/shard_map/pallas_call | solution.py:61
  84.1 10.9 %collective-permute-done.5 = f32[32,1024]{1,0:T(8,128)S(1)} collective-permute-done((f32[32,1024]{1,0:T(8,128)S(1)}, f32[32,1024]{1,0:T(8,128)S(1)}, u32[]{:S(2)}, u32[]{:S(2)}) %collective-permute-start.5) | collective-permute-done | bytes 131104 | tf_op jit(solution)/shard_map/ppermute | solution.py:662
  95.0 2.5 collective-permute-done.4
  97.5 8.5 %collective-permute-done.3 = f32[32,1024]{1,0:T(8,128)S(1)} collective-permute-done((f32[32,1024]{1,0:T(8,128)S(1)}, f32[32,1024]{1,0:T(8,128)S(1)}, u32[]{:S(2)}, u32[]{:S(2)}) %collective-permute-start.3) | collective-permute-done | bytes 131104 | tf_op jit(solution)/shard_map/ppermute | solution.py:662
  107.0 3.8 collective-permute-start.6
  112.8 7.4 %collective-permute-done.6 = f32[32,1024]{1,0:T(8,128)S(1)} collective-permute-done((f32[32,1024]{1,0:T(8,128)S(1)}, f32[32,1024]{1,0:T(8,128)S(1)}, u32[]{:S(2)}, u32[]{:S(2)}) %collective-permute-start.6) | collective-permute-done | bytes 131104 | tf_op jit(solution)/shard_map/ppermute | solution.py:662
  120.2 9.0 %collective-permute-done.7 = f32[32,1024]{1,0:T(8,128)S(1)} collective-permute-done((f32[32,1024]{1,0:T(8,128)S(1)}, f32[32,1024]{1,0:T(8,128)S(1)}, u32[]{:S(2)}, u32[]{:S(2)}) %collective-permute-start.7) | collective-permute-done | bytes 131104 | tf_op jit(solution)/shard_map/ppermute | solution.py:662
  129.2 2.4 collective-permute-done.8
  132.5 7.6 %shard_map.459 = (f32[128,1024]{1,0:T(8,128)}, f32[128,1024]{1,0:T(8,128)}, f32[128,1024]{1,0:T(8,128)}, f32[128,1024]{1,0:T(8,128)}) custom-call(f32[128,1024]{1,0:T(8,128)} %bitcast.411, f32[1,1024]{1,0:T(1,128)} %bitcast.483, f32[1024,1024]{1,0:T(8,128)} %up_ref.3, f32[1024,1024]{1,0:T(8,128)} %down_ref.3), custom_call_target="tpu_custom_call" | custom-call | flops 1610612736 | bytes 8388608 | tf_op jit(solution)/shard_map/pallas_call | solution.py:142
  145.8 3.5 copy.101
  149.4 3.5 copy.102.qkv_ref
  155.3 2.4 collective-permute-start.12
  159.6 12.2 %collective-permute-start.14 = (f32[32,1024]{1,0:T(8,128)S(1)}, f32[32,1024]{1,0:T(8,128)S(1)}, u32[]{:S(2)}, u32[]{:S(2)}) collective-permute-start(f32[32,1024]{1,0:T(8,128)S(1)} %fusion.46), channel_id=1, source_target_pairs={{0,3},{1,0},{2,1},{3,2},{4,7},{5,4},{6,5},{7,6},{8,11},{9,8},{10,9... | collective-permute-start | bytes 393224 | tf_op jit(solution)/shard_map/ppermute | solution.py:662
  172.0 4.0 collective-permute-done.14
  176.9 5.4 shard_map.460
  192.0 4.5 collective-permute-done.17
  202.0 8.1 %collective-permute-done.21 = f32[32,1024]{1,0:T(8,128)S(1)} collective-permute-done((f32[32,1024]{1,0:T(8,128)S(1)}, f32[32,1024]{1,0:T(8,128)S(1)}, u32[]{:S(2)}, u32[]{:S(2)}) %collective-permute-start.21) | collective-permute-done | bytes 131104 | tf_op jit(solution)/shard_map/ppermute | solution.py:662
  212.9 7.7 %shard_map.461 = (f32[128,1024]{1,0:T(8,128)}, f32[128,1024]{1,0:T(8,128)}, f32[128,1024]{1,0:T(8,128)}, f32[128,1024]{1,0:T(8,128)}) custom-call(f32[128,1024]{1,0:T(8,128)} %bitcast.417, f32[1,1024]{1,0:T(1,128)} %gain_ref.6, f32[1024,1024]{1,0:T(8,128)} %bitcast.400, f32[1024,1024]{1,0:T(8,128)} %bitcast.402), custom_call_target="tpu_custom_call" | custom-call | flops 1610612736 | bytes 8388608 | tf_op jit(solution)/shard_map/pallas_call | solution.py:142
  227.2 3.1 collective-permute-done.27
  231.2 4.5 collective-permute-done.26
  236.0 4.0 collective-permute-done.25
  247.5 2.5 pad_maximum_fusion.1
  253.3 4.2 collective-permute-start.34
  259.0 6.7 collective-permute-done.34
  265.8 2.6 collective-permute-done.35
  269.2 38.8 %shard_map.462 = (f32[128,1024]{1,0:T(8,128)}, f32[256,512]{1,0:T(8,128)}, f32[256,512]{1,0:T(8,128)}, f32[256,512]{1,0:T(8,128)}, f32[256,512]{1,0:T(8,128)}, /...) custom-call(f32[128,1024]{1,0:T(8,128)} %bitcast.432, ...), custom_call_target="tpu_custom_call" | custom-call | flops 20000000000 | bytes 40000000 | tf_op jit(solution)/shard_map/pallas_call | solution.py:503
  313.8 2.8 collective-permute-done.37
  316.6 3.8 collective-permute-done.36
  326.0 12.5 %shard_map.463 = (f32[4,4,320,256]{3,2,1,0:T(8,128)}, f32[4,4,320,256]{3,2,1,0:T(8,128)}) custom-call(f32[256,512]{1,0:T(8,128)} %get-tuple-element.241.y_ref, f32[256,2048]{1,0:T(8,128)} %get-tuple-element.242.dpre_ref, f32[256,2048]{1,0:T(8,128)} %get-tuple-element.243.act_ref, f32[256,512]{1,0:T(8,128)} %bitcast.508, f32[256,512]{1,0:T(8,128)} %copy-done.10, ...), custom_call_target="tpu_custom_call" | custom-call | flops 10000000000 | bytes 20000000 | tf_op jit(solution)/shard_map/pallas_call | solution.py:558
  338.6 2.4 collective-permute-start.42
  345.4 11.4 %shard_map.464 = (f32[128,1024]{1,0:T(8,128)}, f32[1,1024]{1,0:T(1,128)}, f32[128,1024]{1,0:T(8,128)}, f32[128,1024]{1,0:T(8,128)}) custom-call(f32[128,1024]{1,0:T(8,128)} %bitcast.456, f32[128,1024]{1,0:T(8,128)} %bitcast.435, f32[128,1024]{1,0:T(8,128)} %bitcast.433, f32[1,1024]{1,0:T(1,128)} %bitcast.491, f32[128,1024]{1,0:T(8,128)} %get-tuple-element.251.pre_ref, ...), custom_call_target="tpu_custom_call" | custom-call | flops 1610612736 | bytes 8388608 | tf_op jit(solution)/shard_map/pallas_call | solution.py:185
  356.9 5.5 add.581
  368.0 5.1 collective-permute-done.47
  373.2 3.4 collective-permute-done.46
  382.6 8.1 %collective-permute-done.50 = f32[32,1024]{1,0:T(8,128)S(1)} collective-permute-done((f32[32,1024]{1,0:T(8,128)S(1)}, f32[32,1024]{1,0:T(8,128)S(1)}, u32[]{:S(2)}, u32[]{:S(2)}) %collective-permute-start.50) | collective-permute-done | bytes 131104 | tf_op jit(solution)/shard_map/ppermute | solution.py:662
  393.3 7.7 %shard_map.465 = (f32[128,1024]{1,0:T(8,128)}, f32[1,1024]{1,0:T(1,128)}, f32[128,768]{1,0:T(8,128)}, f32[128,1024]{1,0:T(8,128)}) custom-call(f32[128,1024]{1,0:T(8,128)} %get-tuple-element.300.base_ref, f32[128,1024]{1,0:T(8,128)} %bitcast.445, f32[128,1024]{1,0:T(8,128)} %bitcast.419, f32[1,1024]{1,0:T(1,128)} %gain_ref.6, ...), custom_call_target="tpu_custom_call" | custom-call | flops 805306368 | bytes 7872512 | tf_op jit(solution)/shard_map/pallas_call | solution.py:61
  409.4 4.8 collective-permute-done.52
  419.8 8.0 %collective-permute-done.56 = f32[32,1024]{1,0:T(8,128)S(1)} collective-permute-done((f32[32,1024]{1,0:T(8,128)S(1)}, f32[32,1024]{1,0:T(8,128)S(1)}, u32[]{:S(2)}, u32[]{:S(2)}) %collective-permute-start.56) | collective-permute-done | bytes 131104 | tf_op jit(solution)/shard_map/ppermute | solution.py:662
  430.6 11.3 %shard_map.466 = (f32[128,1024]{1,0:T(8,128)}, f32[1,1024]{1,0:T(1,128)}, f32[128,1024]{1,0:T(8,128)}, f32[128,1024]{1,0:T(8,128)}) custom-call(f32[128,1024]{1,0:T(8,128)} %get-tuple-element.266.base_ref, f32[128,1024]{1,0:T(8,128)} %bitcast.436, f32[128,1024]{1,0:T(8,128)} %bitcast.416, f32[1,1024]{1,0:T(1,128)} %gain_ref.7, ...), custom_call_target="tpu_custom_call" | custom-call | flops 1610612736 | bytes 8388608 | tf_op jit(solution)/shard_map/pallas_call | solution.py:185
  450.4 4.9 collective-permute-done.58
  456.3 2.4 pad_maximum_fusion.2
  465.1 8.0 %collective-permute-done.62 = f32[32,1024]{1,0:T(8,128)S(1)} collective-permute-done((f32[32,1024]{1,0:T(8,128)S(1)}, f32[32,1024]{1,0:T(8,128)S(1)}, u32[]{:S(2)}, u32[]{:S(2)}) %collective-permute-start.62) | collective-permute-done | bytes 131104 | tf_op jit(solution)/shard_map/ppermute | solution.py:662
  477.8 2.4 collective-permute-start.64
  480.3 15.3 %shard_map.467 = (f32[128,1024]{1,0:T(8,128)}, f32[1,1024]{1,0:T(1,128)}, f32[128,256]{1,0:T(8,128)}, f32[1024,512]{1,0:T(8,128)}, f32[128,1024]{1,0:T(8,128)}, ...) custom-call(f32[128,1024]{1,0:T(8,128)} %get-tuple-element.312.base_, ...), custom_call_target="tpu_custom_call" | custom-call | flops 3000000 | bytes 1000000 | tf_op jit(solution)/shard_map/pallas_call | solution.py:61
  498.8 2.5 collective-permute-start.75
  501.4 4.0 collective-permute-done.64
  519.6 3.5 collective-permute-done.69
  524.0 4.2 collective-permute-done.67
  530.0 11.3 %fusion.13 = f32[1024,1024]{1,0:T(8,128)} fusion(f32[1024,3328]{1,0:T(8,128)} %all-gather.16.cloned.1.call-done, f32[1024,3072]{1,0:T(8,128)} %all-gather.14.cloned.1.call-done), kind=kOutput, calls=%fused_computation.13 | convolution fusion | flops 6442450944 | bytes 12582912 | tf_op jit(solution)/shard_map/dot_general | solution.py:28
  551.1 9.8 %fusion.10 = f32[1024,1024]{1,0:T(8,128)} fusion(f32[1024,3328]{1,0:T(8,128)} %all-gather.16.cloned.1.call-done, f32[1024,3072]{1,0:T(8,128)S(1)} %bitcast.501), kind=kOutput, calls=%fused_computation.10 | convolution fusion | flops 6442450944 | bytes 12582912 | tf_op jit(solution)/shard_map/dot_general | solution.py:28
  561.4 9.2 %collective-permute-done.79 = f32[2,96,512]{2,1,0:T(8,128)S(1)} collective-permute-done((f32[2,96,512]{2,1,0:T(8,128)S(1)}, f32[2,96,512]{2,1,0:T(8,128)S(1)}, u32[]{:S(2)}, u32[]{:S(2)}) %collective-permute-start.79) | collective-permute-done | bytes 393248 | tf_op jit(solution)/shard_map/ppermute | solution.py:714
  570.6 17.4 %all-gather.18.cloned.1.call-done = f32[1024,2816]{1,0:T(8,128)} async-done(((f32[128,2816]{1,0:T(8,128)}), f32[1024,2816]{1,0:T(8,128)}) %all-gather.18.cloned.1.call-update) | async-done | bytes 11534352 | tf_op jit(solution)/shard_map/all_gather | solution.py:708
  591.1 9.6 %fusion.8 = f32[1024,768]{1,0:T(8,128)} fusion(f32[1024,3072]{1,0:T(8,128)} %all-gather.14.cloned.1.call-done, f32[1024,2816]{1,0:T(8,128)} %all-gather.18.cloned.1.call-done), kind=kOutput, calls=%fused_computation.8 | convolution fusion | flops 4831838208 | bytes 10485760 | tf_op jit(solution)/shard_map/dot_general | solution.py:28
  611.3 5.9 fusion.6
  618.3 12.9 %collective-permute-done.90 = f32[32,1024]{1,0:T(8,128)S(1)} collective-permute-done((f32[32,1024]{1,0:T(8,128)}, f32[32,1024]{1,0:T(8,128)S(1)}, u32[]{:S(2)}, u32[]{:S(2)}) %collective-permute-start.90) | collective-permute-done | bytes 131104 | tf_op jit(solution)/shard_map/ppermute | solution.py:662
  631.2 2.5 collective-permute-done.91
  633.8 11.3 %fusion.3 = f32[1024,1024]{1,0:T(8,128)} fusion(f32[1024,2816]{1,0:T(8,128)} %all-gather.18.cloned.1.call-done, f32[1024,2048]{1,0:T(8,128)} %all-gather.12.cloned.1.call-done), kind=kOutput, calls=%fused_computation.3 | convolution fusion | flops 6442450944 | bytes 12582912 | tf_op jit(solution)/shard_map/dot_general | solution.py:28
  645.1 6.9 shard_map.468
  653.9 11.1 %fusion = f32[1024,1024]{1,0:T(8,128)} fusion(f32[1024,2816]{1,0:T(8,128)} %all-gather.18.cloned.1.call-done, f32[1024,2048]{1,0:T(8,128)} %all-gather.12.cloned.1.call-done), kind=kOutput, calls=%fused_computation | convolution fusion | flops 6442450944 | bytes 12582912 | tf_op jit(solution)/shard_map/dot_general | solution.py:28
  665.1 3.8 copy.108
  668.8 3.8 copy.111
  691.2 2.4 pad_maximum_fusion.4
  (532 shorter events, 222.6 us)
Async XLA Ops:
  7.3 59.3 %all-gather.10.cloned.1.call-start = ((), (), s32[]{:S(2)}) async-start(), calls=%async_computation.1 | async-start | bytes 4718592 | tf_op jit(solution)/shard_map/all_gather | solution.py:708
  11.9 128.2 %all-gather.20.cloned.1.call-start = ((), (), s32[]{:S(2)}) async-start(), calls=%async_computation.6 | async-start | bytes 2293760 | tf_op jit(solution)/shard_map/all_gather | solution.py:793
  15.3 14.1 %collective-permute-start = (f32[264,512]{1,0:T(8,128)}, f32[264,512]{1,0:T(8,128)}, u32[]{:S(2)}, u32[]{:S(2)}) collective-permute-start(f32[264,512]{1,0:T(8,128)} %pad_maximum_fusion.8), channel_id=1, source_target_pairs={{0,1},{1,2},{2,3},{3,0},{4,5},{5,6},{6,7},{7,4},{8,9},{9,10},{10,1... | collective-permute-start | bytes 1622024 | tf_op jit(solution)/shard_map/ppermute | solution.py:662
  16.6 46.0 %collective-permute-start.1 = (f32[264,512]{1,0:T(8,128)}, f32[264,512]{1,0:T(8,128)}, u32[]{:S(2)}, u32[]{:S(2)}) collective-permute-start(f32[264,512]{1,0:T(8,128)} %pad_maximum_fusion.8), channel_id=1, source_target_pairs={{0,2},{1,3},{2,0},{3,1},{4,6},{5,7},{6,4},{7,5},{8,10},{9,11},{10,... | collective-permute-start | bytes 1622024 | tf_op jit(solution)/shard_map/ppermute | solution.py:662
  17.6 47.8 %collective-permute-start.2 = (f32[264,512]{1,0:T(8,128)}, f32[264,512]{1,0:T(8,128)}, u32[]{:S(2)}, u32[]{:S(2)}) collective-permute-start(f32[264,512]{1,0:T(8,128)} %pad_maximum_fusion.8), channel_id=1, source_target_pairs={{0,3},{1,0},{2,1},{3,2},{4,7},{5,4},{6,5},{7,6},{8,11},{9,8},{10,9... | collective-permute-start | bytes 1622024 | tf_op jit(solution)/shard_map/ppermute | solution.py:662
  67.8 324.8 %all-gather.12.cloned.1.call-start = ((), (), s32[]{:S(2)}) async-start(), calls=%async_computation.2 | async-start | bytes 9437184 | tf_op jit(solution)/shard_map/all_gather | solution.py:708
  80.4 14.6 %collective-permute-start.5 = (f32[32,1024]{1,0:T(8,128)S(1)}, f32[32,1024]{1,0:T(8,128)S(1)}, u32[]{:S(2)}, u32[]{:S(2)}) collective-permute-start(f32[32,1024]{1,0:T(8,128)S(1)} %get-tuple-element.530), channel_id=1, source_target_pairs={{0,3},{1,0},{2,1},{3,2},{4,7},{5,4},{6,5},{7,6},{8,11},{9,8},{10,9... | collective-permute-start | bytes 393224 | tf_op jit(solution)/shard_map/ppermute | solution.py:662
  80.4 17.1 %collective-permute-start.4 = (f32[32,1024]{1,0:T(8,128)S(1)}, f32[32,1024]{1,0:T(8,128)S(1)}, u32[]{:S(2)}, u32[]{:S(2)}) collective-permute-start(f32[32,1024]{1,0:T(8,128)S(1)} %get-tuple-element.531), channel_id=1, source_target_pairs={{0,2},{1,3},{2,0},{3,1},{4,6},{5,7},{6,4},{7,5},{8,10},{9,11},{10,... | collective-permute-start | bytes 393224 | tf_op jit(solution)/shard_map/ppermute | solution.py:662
  81.8 24.2 %collective-permute-start.3 = (f32[32,1024]{1,0:T(8,128)S(1)}, f32[32,1024]{1,0:T(8,128)S(1)}, u32[]{:S(2)}, u32[]{:S(2)}) collective-permute-start(f32[32,1024]{1,0:T(8,128)S(1)} %get-tuple-element.529), channel_id=1, source_target_pairs={{0,1},{1,2},{2,3},{3,0},{4,5},{5,6},{6,7},{7,4},{8,9},{9,10},{10,1... | collective-permute-start | bytes 393224 | tf_op jit(solution)/shard_map/ppermute | solution.py:662
  107.0 13.2 %collective-permute-start.6 = (f32[32,1024]{1,0:T(8,128)S(1)}, f32[32,1024]{1,0:T(8,128)S(1)}, u32[]{:S(2)}, u32[]{:S(2)}) collective-permute-start(f32[32,1024]{1,0:T(8,128)S(1)} %bitcast_add_fusion.15), channel_id=1, source_target_pairs={{0,1},{1,2},{2,3},{3,0},{4,5},{5,6},{6,7},{7,4},{8,9},{9,10},{10,1... | collective-permute-start | bytes 393224 | tf_op jit(solution)/shard_map/ppermute | solution.py:662
  110.9 18.3 %collective-permute-start.7 = (f32[32,1024]{1,0:T(8,128)S(1)}, f32[32,1024]{1,0:T(8,128)S(1)}, u32[]{:S(2)}, u32[]{:S(2)}) collective-permute-start(f32[32,1024]{1,0:T(8,128)S(1)} %bitcast_add_fusion.15), channel_id=1, source_target_pairs={{0,2},{1,3},{2,0},{3,1},{4,6},{5,7},{6,4},{7,5},{8,10},{9,11},{10,... | collective-permute-start | bytes 393224 | tf_op jit(solution)/shard_map/ppermute | solution.py:662
  112.7 18.9 %collective-permute-start.8 = (f32[32,1024]{1,0:T(8,128)S(1)}, f32[32,1024]{1,0:T(8,128)S(1)}, u32[]{:S(2)}, u32[]{:S(2)}) collective-permute-start(f32[32,1024]{1,0:T(8,128)S(1)} %bitcast_add_fusion.15), channel_id=1, source_target_pairs={{0,3},{1,0},{2,1},{3,2},{4,7},{5,4},{6,5},{7,6},{8,11},{9,8},{10,9... | collective-permute-start | bytes 393224 | tf_op jit(solution)/shard_map/ppermute | solution.py:662
  140.1 42.2 %collective-permute-start.15 = (f32[4,448,256]{2,1,0:T(8,128)}, f32[4,448,256]{2,1,0:T(8,128)S(1)}, u32[]{:S(2)}, u32[]{:S(2)}) collective-permute-start(f32[4,448,256]{2,1,0:T(8,128)} %bitcast.503), channel_id=1, source_target_pairs={{0,8},{4,12},{8,0},{12,4},{16,24},{20,28},{24,16},{28,20},{1,9},{5... | collective-permute-start | bytes 5505032 | tf_op jit(solution)/shard_map/ppermute | solution.py:714
  141.4 41.0 %collective-permute-start.16 = (f32[4,448,256]{2,1,0:T(8,128)}, f32[4,448,256]{2,1,0:T(8,128)}, u32[]{:S(2)}, u32[]{:S(2)}) collective-permute-start(f32[4,448,256]{2,1,0:T(8,128)} %bitcast.504), channel_id=1, source_target_pairs={{0,16},{4,20},{8,24},{12,28},{16,0},{20,4},{24,8},{28,12},{1,17},{... | collective-permute-start | bytes 5505032 | tf_op jit(solution)/shard_map/ppermute | solution.py:714
  143.5 10.8 %collective-permute-start.9 = (f32[32,1024]{1,0:T(8,128)S(1)}, f32[32,1024]{1,0:T(8,128)S(1)}, u32[]{:S(2)}, u32[]{:S(2)}) collective-permute-start(f32[32,1024]{1,0:T(8,128)S(1)} %get-tuple-element.526), channel_id=1, source_target_pairs={{0,1},{1,2},{2,3},{3,0},{4,5},{5,6},{6,7},{7,4},{8,9},{9,10},{10,1... | collective-permute-start | bytes 393224 | tf_op jit(solution)/shard_map/ppermute | solution.py:662
  155.3 16.6 %collective-permute-start.12 = (f32[32,1024]{1,0:T(8,128)S(1)}, f32[32,1024]{1,0:T(8,128)S(1)}, u32[]{:S(2)}, u32[]{:S(2)}) collective-permute-start(f32[32,1024]{1,0:T(8,128)S(1)} %fusion.46), channel_id=1, source_target_pairs={{0,1},{1,2},{2,3},{3,0},{4,5},{5,6},{6,7},{7,4},{8,9},{9,10},{10,1... | collective-permute-start | bytes 393224 | tf_op jit(solution)/shard_map/ppermute | solution.py:662
  157.7 14.3 %collective-permute-start.13 = (f32[32,1024]{1,0:T(8,128)S(1)}, f32[32,1024]{1,0:T(8,128)S(1)}, u32[]{:S(2)}, u32[]{:S(2)}) collective-permute-start(f32[32,1024]{1,0:T(8,128)S(1)} %fusion.46), channel_id=1, source_target_pairs={{0,2},{1,3},{2,0},{3,1},{4,6},{5,7},{6,4},{7,5},{8,10},{9,11},{10,... | collective-permute-start | bytes 393224 | tf_op jit(solution)/shard_map/ppermute | solution.py:662
  159.6 16.4 %collective-permute-start.14 = (f32[32,1024]{1,0:T(8,128)S(1)}, f32[32,1024]{1,0:T(8,128)S(1)}, u32[]{:S(2)}, u32[]{:S(2)}) collective-permute-start(f32[32,1024]{1,0:T(8,128)S(1)} %fusion.46), channel_id=1, source_target_pairs={{0,3},{1,0},{2,1},{3,2},{4,7},{5,4},{6,5},{7,6},{8,11},{9,8},{10,9... | collective-permute-start | bytes 393224 | tf_op jit(solution)/shard_map/ppermute | solution.py:662
  185.7 10.8 %collective-permute-start.17 = (f32[32,1024]{1,0:T(8,128)S(1)}, f32[32,1024]{1,0:T(8,128)S(1)}, u32[]{:S(2)}, u32[]{:S(2)}) collective-permute-start(f32[32,1024]{1,0:T(8,128)S(1)} %get-tuple-element.523), channel_id=1, source_target_pairs={{0,1},{1,2},{2,3},{3,0},{4,5},{5,6},{6,7},{7,4},{8,9},{9,10},{10,1... | collective-permute-start | bytes 393224 | tf_op jit(solution)/shard_map/ppermute | solution.py:662
  189.2 31.5 %collective-permute-start.23 = (f32[4,256,256]{2,1,0:T(8,128)S(1)}, f32[4,256,256]{2,1,0:T(8,128)S(1)}, u32[]{:S(2)}, u32[]{:S(2)}) collective-permute-start(f32[4,256,256]{2,1,0:T(8,128)S(1)} %slice.219), channel_id=1, source_target_pairs={{0,16},{4,20},{8,24},{12,28},{16,0},{20,4},{24,8},{28,12},{1,17},{... | collective-permute-start | bytes 3145736 | tf_op jit(solution)/shard_map/ppermute | solution.py:714
  191.6 29.0 %collective-permute-start.24 = (f32[4,192,256]{2,1,0:T(8,128)S(1)}, f32[4,192,256]{2,1,0:T(8,128)S(1)}, u32[]{:S(2)}, u32[]{:S(2)}) collective-permute-start(f32[4,192,256]{2,1,0:T(8,128)S(1)} %slice.220), channel_id=1, source_target_pairs={{0,8},{4,12},{8,0},{12,4},{16,24},{20,28},{24,16},{28,20},{1,9},{5... | collective-permute-start | bytes 2359304 | tf_op jit(solution)/shard_map/ppermute | solution.py:714
  200.4 11.8 %collective-permute-start.22 = (f32[32,1024]{1,0:T(8,128)S(1)}, f32[32,1024]{1,0:T(8,128)S(1)}, u32[]{:S(2)}, u32[]{:S(2)}) collective-permute-start(f32[32,1024]{1,0:T(8,128)S(1)} %fusion.43), channel_id=1, source_target_pairs={{0,3},{1,0},{2,1},{3,2},{4,7},{5,4},{6,5},{7,6},{8,11},{9,8},{10,9... | collective-permute-start | bytes 393224 | tf_op jit(solution)/shard_map/ppermute | solution.py:662
  222.5 207.4 %all-gather.14.cloned.1.call-start = ((), (), s32[]{:S(2)}) async-start(), calls=%async_computation.3 | async-start | bytes 14155776 | tf_op jit(solution)/shard_map/all_gather | solution.py:708
  222.6 21.2 %collective-permute-start.28 = (f32[4,448,256]{2,1,0:T(8,128)}, f32[4,448,256]{2,1,0:T(8,128)S(1)}, u32[]{:S(2)}, u32[]{:S(2)}) collective-permute-start(f32[4,448,256]{2,1,0:T(8,128)} %bitcast.505), channel_id=1, source_target_pairs={{0,4},{4,0},{8,12},{12,8},{16,20},{20,16},{24,28},{28,24},{1,5},{5... | collective-permute-start | bytes 5505032 | tf_op jit(solution)/shard_map/ppermute | solution.py:714
  223.6 20.2 %collective-permute-start.29 = (f32[4,448,256]{2,1,0:T(8,128)S(1)}, f32[4,448,256]{2,1,0:T(8,128)S(1)}, u32[]{:S(2)}, u32[]{:S(2)}) collective-permute-start(f32[4,448,256]{2,1,0:T(8,128)S(1)} %collective-permute-done.15.refs_9_), channel_id=1, source_target_pairs={{0,4},{4,0},{8,12},{12,8},{16,20},{20,16},{24,28},{28,24},{1,5},{5... | collective-permute-start | bytes 5505032 | tf_op jit(solution)/shard_map/ppermute | solution.py:714
  223.7 21.3 %collective-permute-start.30 = (f32[4,448,256]{2,1,0:T(8,128)}, f32[4,448,256]{2,1,0:T(8,128)S(1)}, u32[]{:S(2)}, u32[]{:S(2)}) collective-permute-start(f32[4,448,256]{2,1,0:T(8,128)} %collective-permute-done.16.refs_10_), channel_id=1, source_target_pairs={{0,4},{4,0},{8,12},{12,8},{16,20},{20,16},{24,28},{28,24},{1,5},{5... | collective-permute-start | bytes 5505032 | tf_op jit(solution)/shard_map/ppermute | solution.py:714
  230.3 13.4 %collective-permute-start.31 = (f32[4,256,256]{2,1,0:T(8,128)}, f32[4,256,256]{2,1,0:T(8,128)S(1)}, u32[]{:S(2)}, u32[]{:S(2)}) collective-permute-start(f32[4,256,256]{2,1,0:T(8,128)} %copy-done.67), channel_id=1, source_target_pairs={{0,4},{4,0},{8,12},{12,8},{16,20},{20,16},{24,28},{28,24},{1,5},{5... | collective-permute-start | bytes 3145736 | tf_op jit(solution)/shard_map/ppermute | solution.py:714
  250.0 225.2 %reduce-scatter.4.cloned.1.call-start = ((), (), s32[]{:S(2)}) async-start(), calls=%async_computation.8 | async-start | bytes 6553600
  253.3 12.5 %collective-permute-start.34 = (f32[32,1024]{1,0:T(8,128)S(1)}, f32[32,1024]{1,0:T(8,128)S(1)}, u32[]{:S(2)}, u32[]{:S(2)}) collective-permute-start(f32[32,1024]{1,0:T(8,128)S(1)} %fusion.40), channel_id=1, source_target_pairs={{0,2},{1,3},{2,0},{3,1},{4,6},{5,7},{6,4},{7,5},{8,10},{9,11},{10,... | collective-permute-start | bytes 393224 | tf_op jit(solution)/shard_map/ppermute | solution.py:662
  257.5 10.8 %collective-permute-start.35 = (f32[32,1024]{1,0:T(8,128)S(1)}, f32[32,1024]{1,0:T(8,128)S(1)}, u32[]{:S(2)}, u32[]{:S(2)}) collective-permute-start(f32[32,1024]{1,0:T(8,128)S(1)} %fusion.40), channel_id=1, source_target_pairs={{0,3},{1,0},{2,1},{3,2},{4,7},{5,4},{6,5},{7,6},{8,11},{9,8},{10,9... | collective-permute-start | bytes 393224 | tf_op jit(solution)/shard_map/ppermute | solution.py:662
  321.4 17.2 %collective-permute-start.39 = (f32[32,1024]{1,0:T(8,128)S(1)}, f32[32,1024]{1,0:T(8,128)S(1)}, u32[]{:S(2)}, u32[]{:S(2)}) collective-permute-start(f32[32,1024]{1,0:T(8,128)S(1)} %fusion.37), channel_id=1, source_target_pairs={{0,1},{1,2},{2,3},{3,0},{4,5},{5,6},{6,7},{7,4},{8,9},{9,10},{10,1... | collective-permute-start | bytes 393224 | tf_op jit(solution)/shard_map/ppermute | solution.py:662
  323.7 14.8 %collective-permute-start.40 = (f32[32,1024]{1,0:T(8,128)S(1)}, f32[32,1024]{1,0:T(8,128)S(1)}, u32[]{:S(2)}, u32[]{:S(2)}) collective-permute-start(f32[32,1024]{1,0:T(8,128)S(1)} %fusion.37), channel_id=1, source_target_pairs={{0,2},{1,3},{2,0},{3,1},{4,6},{5,7},{6,4},{7,5},{8,10},{9,11},{10,... | collective-permute-start | bytes 393224 | tf_op jit(solution)/shard_map/ppermute | solution.py:662
  326.0 12.6 %collective-permute-start.41 = (f32[32,1024]{1,0:T(8,128)S(1)}, f32[32,1024]{1,0:T(8,128)S(1)}, u32[]{:S(2)}, u32[]{:S(2)}) collective-permute-start(f32[32,1024]{1,0:T(8,128)S(1)} %fusion.37), channel_id=1, source_target_pairs={{0,3},{1,0},{2,1},{3,2},{4,7},{5,4},{6,5},{7,6},{8,11},{9,8},{10,9... | collective-permute-start | bytes 393224 | tf_op jit(solution)/shard_map/ppermute | solution.py:662
  338.6 18.2 %collective-permute-start.42 = (f32[4,1280,256]{2,1,0:T(8,128)}, f32[4,1280,256]{2,1,0:T(8,128)}, u32[]{:S(2)}, u32[]{:S(2)}) collective-permute-start(f32[4,1280,256]{2,1,0:T(8,128)} %bitcast.502), channel_id=1, source_target_pairs={{0,4},{4,0},{8,12},{12,8},{16,20},{20,16},{24,28},{28,24},{1,5},{5... | collective-permute-start | bytes 15728648 | tf_op jit(solution)/shard_map/ppermute | solution.py:714
  342.0 14.8 %collective-permute-start.45 = (f32[128,256]{1,0:T(8,128)S(1)}, f32[128,256]{1,0:T(8,128)S(1)}, u32[]{:S(2)}, u32[]{:S(2)}) collective-permute-start(f32[128,256]{1,0:T(8,128)S(1)} %get-tuple-element.515), channel_id=1, source_target_pairs={{0,3},{1,0},{2,1},{3,2},{4,7},{5,4},{6,5},{7,6},{8,11},{9,8},{10,9... | collective-permute-start | bytes 393224 | tf_op jit(solution)/shard_map/ppermute | solution.py:662
  343.3 13.5 %collective-permute-start.44 = (f32[128,256]{1,0:T(8,128)S(1)}, f32[128,256]{1,0:T(8,128)S(1)}, u32[]{:S(2)}, u32[]{:S(2)}) collective-permute-start(f32[128,256]{1,0:T(8,128)S(1)} %get-tuple-element.516), channel_id=1, source_target_pairs={{0,2},{1,3},{2,0},{3,1},{4,6},{5,7},{6,4},{7,5},{8,10},{9,11},{10,... | collective-permute-start | bytes 393224 | tf_op jit(solution)/shard_map/ppermute | solution.py:662
  344.9 11.9 %collective-permute-start.43 = (f32[128,256]{1,0:T(8,128)S(1)}, f32[128,256]{1,0:T(8,128)S(1)}, u32[]{:S(2)}, u32[]{:S(2)}) collective-permute-start(f32[128,256]{1,0:T(8,128)S(1)} %get-tuple-element.514), channel_id=1, source_target_pairs={{0,1},{1,2},{2,3},{3,0},{4,5},{5,6},{6,7},{7,4},{8,9},{9,10},{10,1... | collective-permute-start | bytes 393224 | tf_op jit(solution)/shard_map/ppermute | solution.py:662
  362.5 167.5 %all-gather.16.cloned.1.call-start = ((), (), s32[]{:S(2)}) async-start(), calls=%async_computation.4 | async-start | bytes 15335424 | tf_op jit(solution)/shard_map/all_gather | solution.py:708
  365.7 10.8 %collective-permute-start.46 = (f32[32,1024]{1,0:T(8,128)S(1)}, f32[32,1024]{1,0:T(8,128)S(1)}, u32[]{:S(2)}, u32[]{:S(2)}) collective-permute-start(f32[32,1024]{1,0:T(8,128)S(1)} %get-tuple-element.511), channel_id=1, source_target_pairs={{0,1},{1,2},{2,3},{3,0},{4,5},{5,6},{6,7},{7,4},{8,9},{9,10},{10,1... | collective-permute-start | bytes 393224 | tf_op jit(solution)/shard_map/ppermute | solution.py:662
  377.9 210.0 %all-gather.18.cloned.1.call-start = ((), (), s32[]{:S(2)}) async-start(), calls=%async_computation.5 | async-start | bytes 12976128 | tf_op jit(solution)/shard_map/all_gather | solution.py:708
  381.7 10.8 %collective-permute-start.51 = (f32[32,1024]{1,0:T(8,128)S(1)}, f32[32,1024]{1,0:T(8,128)S(1)}, u32[]{:S(2)}, u32[]{:S(2)}) collective-permute-start(f32[32,1024]{1,0:T(8,128)S(1)} %fusion.33), channel_id=1, source_target_pairs={{0,3},{1,0},{2,1},{3,2},{4,7},{5,4},{6,5},{7,6},{8,11},{9,8},{10,9... | collective-permute-start | bytes 393224 | tf_op jit(solution)/shard_map/ppermute | solution.py:662
  403.4 10.8 %collective-permute-start.52 = (f32[32,1024]{1,0:T(8,128)S(1)}, f32[32,1024]{1,0:T(8,128)S(1)}, u32[]{:S(2)}, u32[]{:S(2)}) collective-permute-start(f32[32,1024]{1,0:T(8,128)S(1)} %get-tuple-element.508), channel_id=1, source_target_pairs={{0,1},{1,2},{2,3},{3,0},{4,5},{5,6},{6,7},{7,4},{8,9},{9,10},{10,1... | collective-permute-start | bytes 393224 | tf_op jit(solution)/shard_map/ppermute | solution.py:662
  444.5 10.8 %collective-permute-start.58 = (f32[32,1024]{1,0:T(8,128)S(1)}, f32[32,1024]{1,0:T(8,128)S(1)}, u32[]{:S(2)}, u32[]{:S(2)}) collective-permute-start(f32[32,1024]{1,0:T(8,128)S(1)} %get-tuple-element.505), channel_id=1, source_target_pairs={{0,1},{1,2},{2,3},{3,0},{4,5},{5,6},{6,7},{7,4},{8,9},{9,10},{10,1... | collective-permute-start | bytes 393224 | tf_op jit(solution)/shard_map/ppermute | solution.py:662
  458.7 220.8 %all-gather.22.cloned.1.call-start = ((), (), s32[]{:S(2)}) async-start(), calls=%async_computation.7 | async-start | bytes 6488064 | tf_op jit(solution)/shard_map/all_gather | solution.py:1014
  464.3 10.8 %collective-permute-start.63 = (f32[32,1024]{1,0:T(8,128)S(1)}, f32[32,1024]{1,0:T(8,128)S(1)}, u32[]{:S(2)}, u32[]{:S(2)}) collective-permute-start(f32[32,1024]{1,0:T(8,128)S(1)} %fusion.29), channel_id=1, source_target_pairs={{0,3},{1,0},{2,1},{3,2},{4,7},{5,4},{6,5},{7,6},{8,11},{9,8},{10,9... | collective-permute-start | bytes 393224 | tf_op jit(solution)/shard_map/ppermute | solution.py:662
  476.6 24.8 %collective-permute-start.66 = (f32[320,256]{1,0:T(8,128)S(1)}, f32[320,256]{1,0:T(8,128)S(1)}, u32[]{:S(2)}, u32[]{:S(2)}) collective-permute-start(f32[320,256]{1,0:T(8,128)S(1)} %get-tuple-element.496), channel_id=1, source_target_pairs={{0,3},{1,0},{2,1},{3,2},{4,7},{5,4},{6,5},{7,6},{8,11},{9,8},{10,9... | collective-permute-start | bytes 983048 | tf_op jit(solution)/shard_map/ppermute | solution.py:662
  476.7 24.8 %collective-permute-start.65 = (f32[320,256]{1,0:T(8,128)S(1)}, f32[320,256]{1,0:T(8,128)S(1)}, u32[]{:S(2)}, u32[]{:S(2)}) collective-permute-start(f32[320,256]{1,0:T(8,128)S(1)} %get-tuple-element.497), channel_id=1, source_target_pairs={{0,2},{1,3},{2,0},{3,1},{4,6},{5,7},{6,4},{7,5},{8,10},{9,11},{10,... | collective-permute-start | bytes 983048 | tf_op jit(solution)/shard_map/ppermute | solution.py:662
  477.8 27.7 %collective-permute-start.64 = (f32[320,256]{1,0:T(8,128)S(1)}, f32[320,256]{1,0:T(8,128)S(1)}, u32[]{:S(2)}, u32[]{:S(2)}) collective-permute-start(f32[320,256]{1,0:T(8,128)S(1)} %get-tuple-element.495), channel_id=1, source_target_pairs={{0,1},{1,2},{2,3},{3,0},{4,5},{5,6},{6,7},{7,4},{8,9},{9,10},{10,1... | collective-permute-start | bytes 983048 | tf_op jit(solution)/shard_map/ppermute | solution.py:662
  498.8 42.4 %collective-permute-start.75 = (f32[4,192,512]{2,1,0:T(8,128)}, f32[4,192,512]{2,1,0:T(8,128)}, u32[]{:S(2)}, u32[]{:S(2)}) collective-permute-start(f32[4,192,512]{2,1,0:T(8,128)} %get-tuple-element.482), channel_id=1, source_target_pairs={{0,4},{4,0},{8,12},{12,8},{16,20},{20,16},{24,28},{28,24},{1,5},{5... | collective-permute-start | bytes 4718600 | tf_op jit(solution)/shard_map/ppermute | solution.py:714
  515.9 12.3 %collective-permute-start.67 = (f32[32,1024]{1,0:T(8,128)}, f32[32,1024]{1,0:T(8,128)}, u32[]{:S(2)}, u32[]{:S(2)}) collective-permute-start(f32[32,1024]{1,0:T(8,128)} %get-tuple-element.502), channel_id=1, source_target_pairs={{0,1},{1,2},{2,3},{3,0},{4,5},{5,6},{6,7},{7,4},{8,9},{9,10},{10,1... | collective-permute-start | bytes 393224 | tf_op jit(solution)/shard_map/ppermute | solution.py:662
  519.3 21.9 %collective-permute-start.73 = (f32[128,384]{1,0:T(8,128)S(1)}, f32[128,384]{1,0:T(8,128)S(1)}, u32[]{:S(2)}, u32[]{:S(2)}) collective-permute-start(f32[128,384]{1,0:T(8,128)S(1)} %select_maximum_fusion.refs_0_), channel_id=1, source_target_pairs={{0,8},{4,12},{8,0},{12,4},{16,24},{20,28},{24,16},{28,20},{1,9},{5... | collective-permute-start | bytes 589832 | tf_op jit(solution)/shard_map/ppermute | solution.py:714
  523.1 18.1 %collective-permute-start.74 = (f32[128,384]{1,0:T(8,128)S(1)}, f32[128,384]{1,0:T(8,128)}, u32[]{:S(2)}, u32[]{:S(2)}) collective-permute-start(f32[128,384]{1,0:T(8,128)S(1)} %select_maximum_fusion.refs_0_), channel_id=1, source_target_pairs={{0,16},{4,20},{8,24},{12,28},{16,0},{20,4},{24,8},{28,12},{1,17},{... | collective-permute-start | bytes 589832 | tf_op jit(solution)/shard_map/ppermute | solution.py:714
  542.4 28.2 %collective-permute-start.76 = (f32[256,512]{1,0:T(8,128)S(1)}, f32[256,512]{1,0:T(8,128)}, u32[]{:S(2)}, u32[]{:S(2)}) collective-permute-start(f32[256,512]{1,0:T(8,128)S(1)} %get-tuple-element.486), channel_id=1, source_target_pairs={{0,1},{1,2},{2,3},{3,0},{4,5},{5,6},{6,7},{7,4},{8,9},{9,10},{10,1... | collective-permute-start | bytes 1572872 | tf_op jit(solution)/shard_map/ppermute | solution.py:662
  544.6 16.4 %collective-permute-start.77 = (f32[64,384]{1,0:T(8,128)S(1)}, f32[64,384]{1,0:T(8,128)S(1)}, u32[]{:S(2)}, u32[]{:S(2)}) collective-permute-start(f32[64,384]{1,0:T(8,128)S(1)} %slice.233), channel_id=1, source_target_pairs={{0,16},{4,20},{8,24},{12,28},{16,0},{20,4},{24,8},{28,12},{1,17},{... | collective-permute-start | bytes 294920 | tf_op jit(solution)/shard_map/ppermute | solution.py:714
  547.4 13.9 %collective-permute-start.78 = (f32[64,384]{1,0:T(8,128)S(1)}, f32[64,384]{1,0:T(8,128)S(1)}, u32[]{:S(2)}, u32[]{:S(2)}) collective-permute-start(f32[64,384]{1,0:T(8,128)S(1)} %slice.234), channel_id=1, source_target_pairs={{0,8},{4,12},{8,0},{12,4},{16,24},{20,28},{24,16},{28,20},{1,9},{5... | collective-permute-start | bytes 294920 | tf_op jit(solution)/shard_map/ppermute | solution.py:714
  549.4 21.2 %collective-permute-start.79 = (f32[2,96,512]{2,1,0:T(8,128)S(1)}, f32[2,96,512]{2,1,0:T(8,128)S(1)}, u32[]{:S(2)}, u32[]{:S(2)}) collective-permute-start(f32[2,96,512]{2,1,0:T(8,128)S(1)} %get-tuple-element.489), channel_id=1, source_target_pairs={{0,8},{4,12},{8,0},{12,4},{16,24},{20,28},{24,16},{28,20},{1,9},{5... | collective-permute-start | bytes 1179656 | tf_op jit(solution)/shard_map/ppermute | solution.py:714
  551.0 19.6 %collective-permute-start.80 = (f32[2,96,512]{2,1,0:T(8,128)S(1)}, f32[2,96,512]{2,1,0:T(8,128)}, u32[]{:S(2)}, u32[]{:S(2)}) collective-permute-start(f32[2,96,512]{2,1,0:T(8,128)S(1)} %get-tuple-element.487), channel_id=1, source_target_pairs={{0,16},{4,20},{8,24},{12,28},{16,0},{20,4},{24,8},{28,12},{1,17},{... | collective-permute-start | bytes 1179656 | tf_op jit(solution)/shard_map/ppermute | solution.py:714
  561.0 43.2 %collective-permute-start.83 = (f32[256,512]{1,0:T(8,128)}, f32[256,512]{1,0:T(8,128)S(1)}, u32[]{:S(2)}, u32[]{:S(2)}) collective-permute-start(f32[256,512]{1,0:T(8,128)} %get-tuple-element.485), channel_id=1, source_target_pairs={{0,3},{1,0},{2,1},{3,2},{4,7},{5,4},{6,5},{7,6},{8,11},{9,8},{10,9... | collective-permute-start | bytes 1572872 | tf_op jit(solution)/shard_map/ppermute | solution.py:662
  588.9 12.7 %collective-permute-start.82 = (f32[96,512]{1,0:T(8,128)S(1)}, f32[96,512]{1,0:T(8,128)S(1)}, u32[]{:S(2)}, u32[]{:S(2)}) collective-permute-start(f32[96,512]{1,0:T(8,128)S(1)} %add_bitcast_fusion.4), channel_id=1, source_target_pairs={{0,8},{4,12},{8,0},{12,4},{16,24},{20,28},{24,16},{28,20},{1,9},{5... | collective-permute-start | bytes 589832 | tf_op jit(solution)/shard_map/ppermute | solution.py:714
  589.8 13.2 %collective-permute-start.81 = (f32[96,512]{1,0:T(8,128)S(1)}, f32[96,512]{1,0:T(8,128)S(1)}, u32[]{:S(2)}, u32[]{:S(2)}) collective-permute-start(f32[96,512]{1,0:T(8,128)S(1)} %add_bitcast_fusion.5), channel_id=1, source_target_pairs={{0,16},{4,20},{8,24},{12,28},{16,0},{20,4},{24,8},{28,12},{1,17},{... | collective-permute-start | bytes 589832 | tf_op jit(solution)/shard_map/ppermute | solution.py:714
  607.5 10.8 %collective-permute-start.89 = (f32[32,1024]{1,0:T(8,128)}, f32[32,1024]{1,0:T(8,128)S(1)}, u32[]{:S(2)}, u32[]{:S(2)}) collective-permute-start(f32[32,1024]{1,0:T(8,128)} %fusion.27), channel_id=1, source_target_pairs={{0,1},{1,2},{2,3},{3,0},{4,5},{5,6},{6,7},{7,4},{8,9},{9,10},{10,1... | collective-permute-start | bytes 393224 | tf_op jit(solution)/shard_map/ppermute | solution.py:662
  608.7 22.5 %collective-permute-start.90 = (f32[32,1024]{1,0:T(8,128)}, f32[32,1024]{1,0:T(8,128)S(1)}, u32[]{:S(2)}, u32[]{:S(2)}) collective-permute-start(f32[32,1024]{1,0:T(8,128)} %fusion.27), channel_id=1, source_target_pairs={{0,2},{1,3},{2,0},{3,1},{4,6},{5,7},{6,4},{7,5},{8,10},{9,11},{10,... | collective-permute-start | bytes 393224 | tf_op jit(solution)/shard_map/ppermute | solution.py:662
  609.9 23.9 %collective-permute-start.91 = (f32[32,1024]{1,0:T(8,128)}, f32[32,1024]{1,0:T(8,128)S(1)}, u32[]{:S(2)}, u32[]{:S(2)}) collective-permute-start(f32[32,1024]{1,0:T(8,128)} %fusion.27), channel_id=1, source_target_pairs={{0,3},{1,0},{2,1},{3,2},{4,7},{5,4},{6,5},{7,6},{8,11},{9,8},{10,9... | collective-permute-start | bytes 393224 | tf_op jit(solution)/shard_map/ppermute | solution.py:662
  611.1 53.9 %collective-permute-start.92 = (f32[256,512]{1,0:T(8,128)}, f32[256,512]{1,0:T(8,128)S(1)}, u32[]{:S(2)}, u32[]{:S(2)}) collective-permute-start(f32[256,512]{1,0:T(8,128)} %get-tuple-element.484), channel_id=1, source_target_pairs={{0,2},{1,3},{2,0},{3,1},{4,6},{5,7},{6,4},{7,5},{8,10},{9,11},{10,... | collective-permute-start | bytes 1572872 | tf_op jit(solution)/shard_map/ppermute | solution.py:662
  (123 other events, 1168.8 us)
Sparse Core Ops, SparseCore 0:
  12.0 38.0 all-gather.9
  67.9 60.9 all-gather.19
  222.6 54.5 all-gather.11
  279.0 72.0 all-gather.13
  362.6 61.4 reduce-scatter.3
  425.8 76.7 all-gather.15
  504.6 83.3 all-gather.17
  607.5 43.1 all-gather.21
